TPU v7x, 128 devices: a whole 4x4x4 slice. The times are simulated.
128 devices in a mesh: seq: 16 (over y, x_hi, core), tp: 8 (over x_lo, z).
Axes of the slice: x: 4 (x_hi: 2, x_lo: 2; x = x_hi * 2 + x_lo), y: 4, z: 4, core: 2. Of those that a mesh axis runs over, the one named last changes fastest.
Arguments:
- hidden_in: bfloat16 [6144, 8192], P('seq', 'tp'), may hold values from -6 to 6
- w_query: bfloat16 [8192, 8192], P(None, 'tp'), may hold values from -0.0625 to 0.0625
- w_key: bfloat16 [8192, 1024], P(None, 'tp'), may hold values from -0.0625 to 0.0625
- w_value: bfloat16 [8192, 1024], P(None, 'tp'), may hold values from -0.0625 to 0.0625
- q_bias: float32 [8192], P('tp'), may hold values from -10 to 10
- k_bias: float32 [1024], P('tp'), may hold values from -10 to 10
- v_bias: float32 [1024], P('tp'), may hold values from -3 to 3
Outputs:
- attended: bfloat16 [6144, 8192], P('seq', 'tp')
All inputs are finite; a program needn't handle non-finite values.
Results may differ from a plain program's by a relative error of at most 0.0065.
The roundings to bfloat16 on the way count: a program that leaves them out, or rounds other values in their place, can miss the bound.
Values may be sent and summed in bfloat16 or wider, within the bound.
No kernel may reach another device: no remote copies, remote signals or barrier semaphores. Data moves between devices by JAX's collectives and lax.ppermute only.
A program may use at most 128 MiB of HBM per device.

v0:
```python
import jax
import jax.numpy as jnp
from jax import lax
from jax.sharding import PartitionSpec as P

HQ = 64
KVH = 8
HEAD = 128


rope_base = 1000000.0


def angles(positions, width):
    half = width // 2
    freq = rope_base ** (-2.0 * jnp.arange(half, dtype=jnp.float32) / width)
    phase = positions.astype(jnp.float32)[:, None] * freq[None, :]
    phase = jnp.concatenate([phase, phase], axis=-1)
    return (jnp.cos(phase), jnp.sin(phase))


def rotate(vectors, cosine, sine):
    half = vectors.shape[-1] // 2
    turned = jnp.concatenate([-vectors[..., half:], vectors[..., :half]], axis=-1)
    return vectors * cosine + turned * sine


def attend(running, queries, query_pos, kv_index, kv_here, key_rows, value_rows):
    key_count = key_rows.shape[0]
    key_head = lax.dynamic_index_in_dim(
        key_rows.reshape(key_count, kv_here, HEAD), kv_index, 1, keepdims=False
    )
    value_head = lax.dynamic_index_in_dim(
        value_rows.reshape(key_count, kv_here, HEAD), kv_index, 1, keepdims=False
    )
    block_size = key_count
    while block_size > 1024 and block_size % 2 == 0:
        block_size = block_size // 2
    scale = float(HEAD) ** (-0.5)
    last_query = jnp.max(query_pos)

    def one_block(block_index, carried):
        row_max, row_sum, acc_sum = carried
        block_start = block_index * block_size
        key_block = lax.dynamic_slice_in_dim(key_head, block_index * block_size, block_size, 0)
        value_block = lax.dynamic_slice_in_dim(value_head, block_index * block_size, block_size, 0)

        def compute(state):
            old_max, old_sum, old_acc = state
            scores = jnp.dot(queries, key_block.T, preferred_element_type=jnp.float32) * scale
            key_pos = block_start + jnp.arange(block_size, dtype=jnp.int32)
            scores = jnp.where(query_pos[:, None] >= key_pos[None, :], scores, -jnp.inf)
            new_max = jnp.maximum(old_max, jnp.max(scores, axis=1))
            shrink = jnp.exp(old_max - new_max)
            weights = jnp.exp(scores - new_max[:, None])
            new_sum = old_sum * shrink + jnp.sum(weights, axis=1)
            new_acc = old_acc * shrink[:, None] + jnp.dot(
                weights.astype(jnp.bfloat16), value_block, preferred_element_type=jnp.float32
            )
            return (new_max, new_sum, new_acc)

        def keep_state(state):
            return state

        return lax.cond(block_start <= last_query, compute, keep_state, (row_max, row_sum, acc_sum))

    return lax.fori_loop(0, key_count // block_size, one_block, running)


def local(hidden_in, w_query, w_key, w_value, q_bias, k_bias, v_bias):
    tok_rows = hidden_in.shape[0]
    q_width = w_query.shape[1]
    kv_width = w_key.shape[1]
    heads_here = q_width // HEAD
    kv_here = kv_width // HEAD
    seq_count = lax.axis_size("seq")
    seq_index = lax.axis_index("seq")
    feature_block = lax.all_gather(hidden_in, "tp", axis=1, tiled=True)

    def project(weight):
        return jnp.dot(feature_block, weight, preferred_element_type=jnp.float32)

    q_sum = project(w_query)
    k_sum = project(w_key)
    v_sum = project(w_value)
    positions = seq_index * tok_rows + jnp.arange(tok_rows, dtype=jnp.int32)
    cosine, sine = angles(positions, HEAD)
    query = (q_sum + q_bias).reshape(tok_rows, heads_here, HEAD).transpose(1, 0, 2)
    query = rotate(query, cosine, sine).astype(jnp.bfloat16)
    keys = (k_sum + k_bias).reshape(tok_rows, kv_here, HEAD)
    keys = (
        rotate(keys, cosine[:, None, :], sine[:, None, :])
        .astype(jnp.bfloat16)
        .reshape(tok_rows, kv_width)
    )
    values = (v_sum + v_bias).astype(jnp.bfloat16)
    piece_rows = heads_here * tok_rows // seq_count
    query_count = heads_here * tok_rows
    query_pieces = query.reshape(seq_count, piece_rows, HEAD)
    row_index = jnp.arange(query_count, dtype=jnp.int32)
    flat_index = seq_index * piece_rows + row_index % piece_rows
    query_pos = row_index // piece_rows * tok_rows + flat_index % tok_rows
    kv_index = seq_index * piece_rows // tok_rows // (HQ // KVH)
    running = (
        jnp.full((query_count,), -1e30, jnp.float32),
        jnp.zeros((query_count,), jnp.float32),
        jnp.zeros((query_count, HEAD), jnp.float32),
    )
    got_query = lax.all_to_all(query_pieces, "seq", split_axis=0, concat_axis=0, tiled=True)
    queries = got_query.reshape(query_count, HEAD)
    running = attend(
        running,
        queries,
        query_pos,
        kv_index,
        kv_here,
        lax.all_gather(keys, "seq", axis=0, tiled=True),
        lax.all_gather(values, "seq", axis=0, tiled=True),
    )
    mixed = (
        (running[2] / running[1][:, None]).astype(jnp.bfloat16).reshape(seq_count, piece_rows, HEAD)
    )
    returned = lax.all_to_all(mixed, "seq", split_axis=0, concat_axis=0, tiled=True)
    return (
        returned.reshape(heads_here, tok_rows, HEAD).transpose(1, 0, 2).reshape(tok_rows, q_width)
    )


def solution(mesh):
    return jax.shard_map(
        local,
        mesh=mesh,
        in_specs=(
            P("seq", "tp"),
            P(None, "tp"),
            P(None, "tp"),
            P(None, "tp"),
            P("tp"),
            P("tp"),
            P("tp"),
        ),
        out_specs=P("seq", "tp"),
        check_vma=False,
    )
```

profile of v0, /device:TPU:1, one launch (start us, length us, event | category | flops | bytes accessed | tf_op | source)
XLA Modules:
  0.0 305.6 jit_solution(3880953907614353224)
XLA Ops:
  7.4 77.3 %all-gather.4.cloned.1.call-done = bf16[384,8192]{1,0:T(8,128)(2,1)} async-done(((bf16[384,1024]{1,0:T(8,128)(2,1)}), bf16[384,8192]{1,0:T(8,128)(2,1)}) %all-gather.4.cloned.1.call-update) | async-done | bytes 6291472 | tf_op jit(solution)/shard_map/all_gather | solution.py:78
  84.7 4.7 %convolution_add_fusion.1 = f32[384,128]{0,1:T(8,128)S(1)} fusion(bf16[384,8192]{1,0:T(8,128)(2,1)} %all-gather.4.cloned.1.call-done, bf16[8192,128]{1,0:T(8,128)(2,1)S(1)} %copy-done, f32[128]{0:T(128)} %param.16), kind=kOutput, calls=%fused_computation.42 | convolution fusion | flops 805355520 | bytes 8585728 | tf_op jit(solution)/shard_map/dot_general | solution.py:81
  91.1 5.9 %fusion.28 = bf16[384,128]{1,0:T(8,128)(2,1)} fusion(bf16[384,8192]{1,0:T(8,128)(2,1)} %all-gather.4.cloned.1.call-done, bf16[8192,128]{1,0:T(8,128)(2,1)} %param.14, f32[128]{0:T(128)S(1)} %copy-done.3), kind=kOutput, calls=%fused_computation.43 | convolution fusion | flops 805404672 | bytes 8487424 | tf_op jit(solution)/shard_map/dot_general | solution.py:81
  97.0 12.2 %add_bitcast_fusion = f32[48,8,8,128]{3,2,1,0:T(8,128)S(1)} fusion(bf16[384,8192]{1,0:T(8,128)(2,1)} %all-gather.4.cloned.1.call-done, bf16[8192,1024]{1,0:T(8,128)(2,1)} %param.12, f32[1024]{0:T(1024)S(1)} %copy-done.4), kind=kOutput, calls=%fused_computation.40 | convolution fusion | flops 6442844160 | bytes 24645632 | tf_op jit(solution)/shard_map/dot_general | solution.py:81
  111.2 7.1 %all-to-all-start = ((bf16[16,192,128]{2,1,0:T(8,128)(2,1)}), bf16[16,192,128]{2,1,0:T(8,128)(2,1)S(1)}, u32[]{:S(2)}, u32[]{:S(2)}) async-start(bf16[16,192,128]{2,1,0:T(8,128)(2,1)} %bitcast.5), calls=%async_computation | async-start | bytes 1572864 | tf_op jit(solution)/shard_map/all_to_all | solution.py:109
  119.1 20.8 %all-gather.6.cloned.1.call-done = bf16[6144,128]{0,1:T(8,128)(2,1)} async-done(((bf16[384,128]{0,1:T(8,128)(2,1)}), bf16[6144,128]{0,1:T(8,128)(2,1)}) %all-gather.6.cloned.1.call-update) | async-done | bytes 1572880 | tf_op jit(solution)/shard_map/all_gather | solution.py:117
  139.9 2.6 copy.18
  142.5 43.5 %all-gather.8.cloned.1.call-done = bf16[6144,128]{1,0:T(8,128)(2,1)} async-done(((bf16[384,128]{1,0:T(8,128)(2,1)}), bf16[6144,128]{1,0:T(8,128)(2,1)}) %all-gather.8.cloned.1.call-update) | async-done | bytes 1572880 | tf_op jit(solution)/shard_map/all_gather | solution.py:118
  187.2 88.5 %while.18 = (s32[]{:T(128)}, f32[3072]{0:T(1024)S(1)}, f32[3072]{0:T(1024)S(1)}, f32[3072,128]{1,0:T(8,128)}, s32[]{:T(128)}, /*index=5*/bf16[6144,128]{1,0:T(8,...) while((s32[]{:T(128)}, f32[3072]{0:T(1024)S(1)}, ...), condition=%wide.region_6.7_spmd.clone, body=%wide.region_1.6_spmd.clone.sunk | while | flops 1241853696 | bytes 45656536 | solution.py:67
  187.9 10.3 %conditional.3 = ((f32[3072]{0:T(1024)S(1)}, f32[3072]{0:T(1024)S(1)}, f32[3072,128]{1,0:T(8,128)})) conditional(s32[]{:T(128)} %convert_element_type.50, (f32[3072]{0:T(1024)S(1)}, f32[3072]{0:T(1024)S(1)}, f32[3072,128]{1,0:T(8,128)}) %tuple.66, (s32[3072]{0:T(1024)S(1)}, s32[]{:T(128)}, bf16[6144,128]{1,0:T(8,128)(2,1)}, ...), branch_computations={%region_2.2_spmd, %region_3.5_spmd.clone} | conditional | flops 1241819904 | bytes 45591692 | solution.py:65
  188.0 2.6 fusion.4
  193.1 4.0 %fusion.8 = f32[3072,128]{1,0:T(8,128)S(1)} fusion(f32[768,3072]{1,0:T(8,128)S(1)} %get-tuple-element.412, f32[3072]{0:T(1024)S(1)} %max.6, s32[3072]{0:T(1024)S(1)} %fusion.15, s32[768]{0:T(1024)S(1)} %iota_add_fusion, f32[3072,128]{1,0:T(8,128)S(1)} %copy-done.1, f32[3072]{0:T(1024)S(1)} %get-tuple-element.410, bf16[6144,128]{1,0:T(8,128)(2,1)} %get-tuple-element.359, ...), kind=kOutput, calls=%fused_computation.8 | convolution fusion | flops 616562688 | bytes 12819460 | tf_op jit(solution)/shard_map/while/body/eval_jaxpr/cond/branch_1_fun/dot_general | solution.py:57
  199.0 10.3 %conditional.3 = ((f32[3072]{0:T(1024)S(1)}, f32[3072]{0:T(1024)S(1)}, f32[3072,128]{1,0:T(8,128)})) conditional(s32[]{:T(128)} %convert_element_type.50, (f32[3072]{0:T(1024)S(1)}, f32[3072]{0:T(1024)S(1)}, f32[3072,128]{1,0:T(8,128)}) %tuple.66, (s32[3072]{0:T(1024)S(1)}, s32[]{:T(128)}, bf16[6144,128]{1,0:T(8,128)(2,1)}, ...), branch_computations={%region_2.2_spmd, %region_3.5_spmd.clone} | conditional | flops 1241819904 | bytes 45591692 | solution.py:65
  199.0 2.6 fusion.4
  204.2 4.0 %fusion.8 = f32[3072,128]{1,0:T(8,128)S(1)} fusion(f32[768,3072]{1,0:T(8,128)S(1)} %get-tuple-element.412, f32[3072]{0:T(1024)S(1)} %max.6, s32[3072]{0:T(1024)S(1)} %fusion.15, s32[768]{0:T(1024)S(1)} %iota_add_fusion, f32[3072,128]{1,0:T(8,128)S(1)} %copy-done.1, f32[3072]{0:T(1024)S(1)} %get-tuple-element.410, bf16[6144,128]{1,0:T(8,128)(2,1)} %get-tuple-element.359, ...), kind=kOutput, calls=%fused_computation.8 | convolution fusion | flops 616562688 | bytes 12819460 | tf_op jit(solution)/shard_map/while/body/eval_jaxpr/cond/branch_1_fun/dot_general | solution.py:57
  210.0 10.3 %conditional.3 = ((f32[3072]{0:T(1024)S(1)}, f32[3072]{0:T(1024)S(1)}, f32[3072,128]{1,0:T(8,128)})) conditional(s32[]{:T(128)} %convert_element_type.50, (f32[3072]{0:T(1024)S(1)}, f32[3072]{0:T(1024)S(1)}, f32[3072,128]{1,0:T(8,128)}) %tuple.66, (s32[3072]{0:T(1024)S(1)}, s32[]{:T(128)}, bf16[6144,128]{1,0:T(8,128)(2,1)}, ...), branch_computations={%region_2.2_spmd, %region_3.5_spmd.clone} | conditional | flops 1241819904 | bytes 45591692 | solution.py:65
  215.3 4.0 %fusion.8 = f32[3072,128]{1,0:T(8,128)S(1)} fusion(f32[768,3072]{1,0:T(8,128)S(1)} %get-tuple-element.412, f32[3072]{0:T(1024)S(1)} %max.6, s32[3072]{0:T(1024)S(1)} %fusion.15, s32[768]{0:T(1024)S(1)} %iota_add_fusion, f32[3072,128]{1,0:T(8,128)S(1)} %copy-done.1, f32[3072]{0:T(1024)S(1)} %get-tuple-element.410, bf16[6144,128]{1,0:T(8,128)(2,1)} %get-tuple-element.359, ...), kind=kOutput, calls=%fused_computation.8 | convolution fusion | flops 616562688 | bytes 12819460 | tf_op jit(solution)/shard_map/while/body/eval_jaxpr/cond/branch_1_fun/dot_general | solution.py:57
  221.1 10.3 %conditional.3 = ((f32[3072]{0:T(1024)S(1)}, f32[3072]{0:T(1024)S(1)}, f32[3072,128]{1,0:T(8,128)})) conditional(s32[]{:T(128)} %convert_element_type.50, (f32[3072]{0:T(1024)S(1)}, f32[3072]{0:T(1024)S(1)}, f32[3072,128]{1,0:T(8,128)}) %tuple.66, (s32[3072]{0:T(1024)S(1)}, s32[]{:T(128)}, bf16[6144,128]{1,0:T(8,128)(2,1)}, ...), branch_computations={%region_2.2_spmd, %region_3.5_spmd.clone} | conditional | flops 1241819904 | bytes 45591692 | solution.py:65
  221.2 2.6 fusion.4
  226.3 4.0 %fusion.8 = f32[3072,128]{1,0:T(8,128)S(1)} fusion(f32[768,3072]{1,0:T(8,128)S(1)} %get-tuple-element.412, f32[3072]{0:T(1024)S(1)} %max.6, s32[3072]{0:T(1024)S(1)} %fusion.15, s32[768]{0:T(1024)S(1)} %iota_add_fusion, f32[3072,128]{1,0:T(8,128)S(1)} %copy-done.1, f32[3072]{0:T(1024)S(1)} %get-tuple-element.410, bf16[6144,128]{1,0:T(8,128)(2,1)} %get-tuple-element.359, ...), kind=kOutput, calls=%fused_computation.8 | convolution fusion | flops 616562688 | bytes 12819460 | tf_op jit(solution)/shard_map/while/body/eval_jaxpr/cond/branch_1_fun/dot_general | solution.py:57
  232.2 10.3 %conditional.3 = ((f32[3072]{0:T(1024)S(1)}, f32[3072]{0:T(1024)S(1)}, f32[3072,128]{1,0:T(8,128)})) conditional(s32[]{:T(128)} %convert_element_type.50, (f32[3072]{0:T(1024)S(1)}, f32[3072]{0:T(1024)S(1)}, f32[3072,128]{1,0:T(8,128)}) %tuple.66, (s32[3072]{0:T(1024)S(1)}, s32[]{:T(128)}, bf16[6144,128]{1,0:T(8,128)(2,1)}, ...), branch_computations={%region_2.2_spmd, %region_3.5_spmd.clone} | conditional | flops 1241819904 | bytes 45591692 | solution.py:65
  237.4 4.0 %fusion.8 = f32[3072,128]{1,0:T(8,128)S(1)} fusion(f32[768,3072]{1,0:T(8,128)S(1)} %get-tuple-element.412, f32[3072]{0:T(1024)S(1)} %max.6, s32[3072]{0:T(1024)S(1)} %fusion.15, s32[768]{0:T(1024)S(1)} %iota_add_fusion, f32[3072,128]{1,0:T(8,128)S(1)} %copy-done.1, f32[3072]{0:T(1024)S(1)} %get-tuple-element.410, bf16[6144,128]{1,0:T(8,128)(2,1)} %get-tuple-element.359, ...), kind=kOutput, calls=%fused_computation.8 | convolution fusion | flops 616562688 | bytes 12819460 | tf_op jit(solution)/shard_map/while/body/eval_jaxpr/cond/branch_1_fun/dot_general | solution.py:57
  243.2 10.3 %conditional.3 = ((f32[3072]{0:T(1024)S(1)}, f32[3072]{0:T(1024)S(1)}, f32[3072,128]{1,0:T(8,128)})) conditional(s32[]{:T(128)} %convert_element_type.50, (f32[3072]{0:T(1024)S(1)}, f32[3072]{0:T(1024)S(1)}, f32[3072,128]{1,0:T(8,128)}) %tuple.66, (s32[3072]{0:T(1024)S(1)}, s32[]{:T(128)}, bf16[6144,128]{1,0:T(8,128)(2,1)}, ...), branch_computations={%region_2.2_spmd, %region_3.5_spmd.clone} | conditional | flops 1241819904 | bytes 45591692 | solution.py:65
  243.3 2.6 fusion.4
  248.4 4.0 %fusion.8 = f32[3072,128]{1,0:T(8,128)S(1)} fusion(f32[768,3072]{1,0:T(8,128)S(1)} %get-tuple-element.412, f32[3072]{0:T(1024)S(1)} %max.6, s32[3072]{0:T(1024)S(1)} %fusion.15, s32[768]{0:T(1024)S(1)} %iota_add_fusion, f32[3072,128]{1,0:T(8,128)S(1)} %copy-done.1, f32[3072]{0:T(1024)S(1)} %get-tuple-element.410, bf16[6144,128]{1,0:T(8,128)(2,1)} %get-tuple-element.359, ...), kind=kOutput, calls=%fused_computation.8 | convolution fusion | flops 616562688 | bytes 12819460 | tf_op jit(solution)/shard_map/while/body/eval_jaxpr/cond/branch_1_fun/dot_general | solution.py:57
  254.3 10.3 %conditional.3 = ((f32[3072]{0:T(1024)S(1)}, f32[3072]{0:T(1024)S(1)}, f32[3072,128]{1,0:T(8,128)})) conditional(s32[]{:T(128)} %convert_element_type.50, (f32[3072]{0:T(1024)S(1)}, f32[3072]{0:T(1024)S(1)}, f32[3072,128]{1,0:T(8,128)}) %tuple.66, (s32[3072]{0:T(1024)S(1)}, s32[]{:T(128)}, bf16[6144,128]{1,0:T(8,128)(2,1)}, ...), branch_computations={%region_2.2_spmd, %region_3.5_spmd.clone} | conditional | flops 1241819904 | bytes 45591692 | solution.py:65
  254.3 2.6 fusion.4
  259.5 4.0 %fusion.8 = f32[3072,128]{1,0:T(8,128)S(1)} fusion(f32[768,3072]{1,0:T(8,128)S(1)} %get-tuple-element.412, f32[3072]{0:T(1024)S(1)} %max.6, s32[3072]{0:T(1024)S(1)} %fusion.15, s32[768]{0:T(1024)S(1)} %iota_add_fusion, f32[3072,128]{1,0:T(8,128)S(1)} %copy-done.1, f32[3072]{0:T(1024)S(1)} %get-tuple-element.410, bf16[6144,128]{1,0:T(8,128)(2,1)} %get-tuple-element.359, ...), kind=kOutput, calls=%fused_computation.8 | convolution fusion | flops 616562688 | bytes 12819460 | tf_op jit(solution)/shard_map/while/body/eval_jaxpr/cond/branch_1_fun/dot_general | solution.py:57
  265.3 10.3 %conditional.3 = ((f32[3072]{0:T(1024)S(1)}, f32[3072]{0:T(1024)S(1)}, f32[3072,128]{1,0:T(8,128)})) conditional(s32[]{:T(128)} %convert_element_type.50, (f32[3072]{0:T(1024)S(1)}, f32[3072]{0:T(1024)S(1)}, f32[3072,128]{1,0:T(8,128)}) %tuple.66, (s32[3072]{0:T(1024)S(1)}, s32[]{:T(128)}, bf16[6144,128]{1,0:T(8,128)(2,1)}, ...), branch_computations={%region_2.2_spmd, %region_3.5_spmd.clone} | conditional | flops 1241819904 | bytes 45591692 | solution.py:65
  265.4 2.6 fusion.4
  270.6 4.0 %fusion.8 = f32[3072,128]{1,0:T(8,128)S(1)} fusion(f32[768,3072]{1,0:T(8,128)S(1)} %get-tuple-element.412, f32[3072]{0:T(1024)S(1)} %max.6, s32[3072]{0:T(1024)S(1)} %fusion.15, s32[768]{0:T(1024)S(1)} %iota_add_fusion, f32[3072,128]{1,0:T(8,128)S(1)} %copy-done.1, f32[3072]{0:T(1024)S(1)} %get-tuple-element.410, bf16[6144,128]{1,0:T(8,128)(2,1)} %get-tuple-element.359, ...), kind=kOutput, calls=%fused_computation.8 | convolution fusion | flops 616562688 | bytes 12819460 | tf_op jit(solution)/shard_map/while/body/eval_jaxpr/cond/branch_1_fun/dot_general | solution.py:57
  277.6 18.0 %all_to_all.10 = bf16[16,192,128]{2,1,0:T(8,128)(2,1)S(1)} all-to-all(bf16[16,192,128]{2,1,0:T(8,128)(2,1)S(1)} %bitcast.46), channel_id=1, replica_groups=mesh['seq'=16,'tp'=8] {'seq'}, dimensions={0} | all-to-all | bytes 1572864 | tf_op jit(solution)/shard_map/all_to_all | solution.py:123
  (152 shorter events, 46.9 us)
Async XLA Ops:
  6.5 78.1 %copy-start = (bf16[8192,128]{1,0:T(8,128)(2,1)S(1)}, bf16[8192,128]{1,0:T(8,128)(2,1)}, u32[]{:S(2)}) copy-start(bf16[8192,128]{1,0:T(8,128)(2,1)} %param.13) | copy-start | bytes 6291460
  6.5 78.1 %all-gather.4.cloned.1.call-start = ((), (), s32[]{:S(2)}) async-start(), calls=%async_computation.2 | async-start | bytes 7077888 | tf_op jit(solution)/shard_map/all_gather | solution.py:78
  7.3 132.6 %all-gather.6.cloned.1.call-start = ((), (), s32[]{:S(2)}) async-start(), calls=%async_computation.3 | async-start | bytes 1671168 | tf_op jit(solution)/shard_map/all_gather | solution.py:117
  89.4 1.7 copy-start.3
  90.8 95.2 %all-gather.8.cloned.1.call-start = ((), (), s32[]{:S(2)}) async-start(), calls=%async_computation.4 | async-start | bytes 1671168 | tf_op jit(solution)/shard_map/all_gather | solution.py:118
  91.1 5.9 %copy-start.4 = (f32[1024]{0:T(1024)S(1)}, f32[1024]{0:T(1024)}, u32[]{:S(2)}) copy-start(f32[1024]{0:T(1024)} %param.15) | copy-start | bytes 12292
  111.2 31.3 %all-to-all-start = ((bf16[16,192,128]{2,1,0:T(8,128)(2,1)}), bf16[16,192,128]{2,1,0:T(8,128)(2,1)S(1)}, u32[]{:S(2)}, u32[]{:S(2)}) async-start(bf16[16,192,128]{2,1,0:T(8,128)(2,1)} %bitcast.5), calls=%async_computation | async-start | bytes 1572864 | tf_op jit(solution)/shard_map/all_to_all | solution.py:109
  190.6 2.5 copy-start.1
  197.1 1.1 copy-start.2
  201.6 2.5 copy-start.1
  208.2 1.1 copy-start.2
  212.7 2.5 copy-start.1
  219.2 1.1 copy-start.2
  223.8 2.5 copy-start.1
  230.3 1.1 copy-start.2
  234.8 2.5 copy-start.1
  241.4 1.1 copy-start.2
  245.9 2.5 copy-start.1
  252.4 1.1 copy-start.2
  257.0 2.5 copy-start.1
  263.5 1.1 copy-start.2
  268.0 2.5 copy-start.1
  274.5 1.1 copy-start.2
Sparse Core Ops, SparseCore 0:
  9.0 75.6 all-gather.3
  90.9 48.9 all-gather.5
  142.3 43.5 all-gather.7
where the time goes:
time: 306 us
  waiting for transfers between devices  142 us (46%)
  matrix products  75.1 us (25%)
  other arithmetic  26.6 us (9%)
  blocking collectives  18 us (6%)
  local copies, waits for them, and re-layouts  16.9 us (6%)
  between operations  13.2 us (4%)
  starting transfers between devices  7.22 us (2%)
  loops' own time  6.24 us (2%)
    all_gather x1, waiting for transfers between devices, local(): feature_block = lax.all_gather(hidden_in, 'tp', axis=1, tiled=True)  77.3 us
    all_gather x1, waiting for transfers between devices, local(): lax.all_gather(values, 'seq', axis=0, tiled=True)  43.5 us
    dot_general x8, matrix products, compute(): jnp.dot(weights.astype(jnp.bfloat16), value_block, preferred_element_type...  31.7 us
    dot_general x3, matrix products, project(): return jnp.dot(feature_block, weight, preferred_element_type=jnp.float32)  22.7 us
    all_gather x1, waiting for transfers between devices, local(): lax.all_gather(keys, 'seq', axis=0, tiled=True)  20.8 us
    dot_general x8, matrix products, compute(): jnp.dot(queries, key_block.T, preferred_element_type=jnp.float32) * scale  20.7 us
    reduce_sum x8, other arithmetic, compute(): new_sum = old_sum * shrink + jnp.sum(weights, axis=1)  20.1 us
    all_to_all x1, blocking collectives, local(): lax.all_to_all(mixed, 'seq', split_axis=0, concat_axis=0, tiled=True)  18 us
  transfers between devices with their start and end apart: 4, of which 3 were waited for; matrix products, arithmetic and copies ran while one was open for 8% of the time, Pallas kernels for 0%

commit v1 on v0

v1 whole, which is shorter than its diff:
```python
import functools
import math

import jax
import jax.numpy as jnp
from jax import lax
from jax.experimental import pallas as pl
from jax.experimental.pallas import tpu as pltpu
from jax.sharding import PartitionSpec as P

HEAD = 128
GROUP = 8
HALF = 192
PART = HALF // 2
DEPTH = 1024
QCOLS = GROUP * HEAD
ALLCOLS = QCOLS + 2 * HEAD
LANES = 4 * HALF
TILES = 16
SPAN = 4 * HALF
BLOCKS = 5
AXES = ("seq", "tp")
VMEM_LIMIT = 48 * 1024 * 1024
EXP2_SCALE = float(HEAD) ** (-0.5) * math.log2(math.e)
NT = (((1,), (1,)), ((), ()))
TN = (((0,), (0,)), ((), ()))
rope_base = 1000000.0


def _place(flat):
    seq, tp = divmod(flat, 8)
    x_lo, z = divmod(tp, 4)
    y, rest = divmod(seq, 4)
    x_hi, core = divmod(rest, 2)
    return x_hi * 2 + x_lo, y, z, core


def _index(x, y, z, core):
    x_hi, x_lo = divmod(x % 4, 2)
    return (((y % 4) * 2 + x_hi) * 2 + core) * 8 + x_lo * 4 + z % 4


def _send(value, move):
    pairs = [(i, _index(*move(*_place(i)))) for i in range(128)]
    return lax.ppermute(value, AXES, pairs)


def z_up(x, y, z, c):
    return x, y, z + 1, c


def z_down(x, y, z, c):
    return x, y, z - 1, c


def x_near(x, y, z, c):
    return x ^ 1, y, z, c


def x_far(x, y, z, c):
    return x ^ 2, y, z, c


def y_up(x, y, z, c):
    return x, y + 1, z, c


def y_down(x, y, z, c):
    return x, y - 1, z, c


def y_far(x, y, z, c):
    return x, y + 2, z, c


def other_core(x, y, z, c):
    return x, y, z, 1 - c


def mirror_cross(x, y, z, c):
    return 3 - x, 3 - y, z, 1 - c


def mirror(x, y, z, c):
    return x ^ 2, 3 - y, z, 1 - c


VMEM = pl.BlockSpec(memory_space=pltpu.VMEM)
HBM = pl.BlockSpec(memory_space=pl.ANY)
SMEM = pl.BlockSpec(memory_space=pltpu.SMEM)


def _block(index):
    return pl.ds(pl.multiple_of(index * DEPTH, DEPTH), DEPTH)


def _piece_loads(parts, pieces, x, sem):
    loads = []
    for i, piece in enumerate(pieces):
        at = 0
        loads.append([])
        for k, (operand, start, size) in enumerate(piece):
            loads[-1].append(
                pltpu.make_async_copy(
                    parts[operand].at[pl.ds(start, size)],
                    x.at[i, pl.ds(at, size)],
                    sem.at[i, k],
                )
            )
            at += size
    return loads


def _weight_loads(slices, n, far, near, sem):
    return [
        [
            pltpu.make_async_copy(src.at[_block(slices[i]), :], dst.at[i], sem.at[i, j])
            for j, (src, dst) in enumerate(zip(far, near))
        ]
        for i in range(n)
    ]


def _start(group):
    for copy in group:
        copy.start()


def _wait(group):
    for copy in group:
        copy.wait()


def _proj_body(arrays, pieces, started, slices, *refs):
    n = len(pieces)
    parts, far = refs[:arrays], refs[arrays : arrays + 3]
    at = arrays + 3
    acc_in = refs[at] if started else None
    at += 1 if started else 0
    acc, x, near = refs[at], refs[at + 1], refs[at + 2 : at + 5]
    x_sem, w_sem = refs[at + 5 : at + 7]
    x_loads = _piece_loads(parts, pieces, x, x_sem)
    w_loads = _weight_loads(slices, n, far, near, w_sem)
    for i in range(min(2, n)):
        _start(x_loads[i])
        _start(w_loads[i])
    spans = (slice(0, QCOLS), slice(QCOLS, QCOLS + HEAD), slice(QCOLS + HEAD, ALLCOLS))
    for i in range(n):
        _wait(x_loads[i])
        _wait(w_loads[i])
        if i + 2 < n:
            _start(x_loads[i + 2])
            _start(w_loads[i + 2])
        for w, cols in zip(near, spans):
            term = jnp.dot(x[i], w[i], preferred_element_type=jnp.float32)
            if i:
                acc[:, cols] += term
            elif started:
                acc[:, cols] = acc_in[:, cols] + term
            else:
                acc[:, cols] = term


def _project(slices, arrays, pieces, weights, acc=None):
    n = len(pieces)
    operands = [slices, *arrays, *weights]
    in_specs = [SMEM] + [HBM] * (len(arrays) + 3)
    aliases = {}
    if acc is not None:
        aliases[len(operands)] = 0
        operands.append(acc)
        in_specs.append(VMEM)
    return pl.pallas_call(
        functools.partial(_proj_body, len(arrays), pieces, acc is not None),
        out_shape=jax.ShapeDtypeStruct((HALF, ALLCOLS), jnp.float32),
        in_specs=in_specs,
        out_specs=VMEM,
        input_output_aliases=aliases,
        scratch_shapes=[
            pltpu.VMEM((n, HALF, DEPTH), jnp.bfloat16),
            pltpu.VMEM((n, DEPTH, QCOLS), jnp.bfloat16),
            pltpu.VMEM((n, DEPTH, HEAD), jnp.bfloat16),
            pltpu.VMEM((n, DEPTH, HEAD), jnp.bfloat16),
            pltpu.SemaphoreType.DMA((n, 2)),
            pltpu.SemaphoreType.DMA((n, 3)),
        ],
        compiler_params=pltpu.CompilerParams(vmem_limit_bytes=20 * 1024 * 1024),
        cost_estimate=pl.CostEstimate(
            flops=2 * n * HALF * DEPTH * ALLCOLS,
            bytes_accessed=2 * n * DEPTH * ALLCOLS,
            transcendentals=0,
        ),
        name="project",
    )(*operands)


def _rotate(u, cosine, sine):
    cosine = jnp.concatenate([cosine[...], cosine[...]], axis=1)
    sine = jnp.concatenate([-sine[...], sine[...]], axis=1)
    return u * cosine + pltpu.roll(u, HEAD // 2, 1) * sine


def _last_kv_body(arrays, pieces, slices, *refs):
    n = len(pieces)
    parts, (w_k, w_v) = refs[:arrays], refs[arrays : arrays + 2]
    acc, k_bias, v_bias, cosine, sine, out, x, near_k, near_v, x_sem, w_sem = refs[arrays + 2 :]
    x_loads = _piece_loads(parts, pieces, x, x_sem)
    w_loads = _weight_loads(slices, n, (w_k, w_v), (near_k, near_v), w_sem)
    for group in x_loads + w_loads:
        _start(group)
    k, v = acc[:, QCOLS : QCOLS + HEAD], acc[:, QCOLS + HEAD :]
    for i in range(n):
        _wait(x_loads[i])
        _wait(w_loads[i])
        k += jnp.dot(x[i], near_k[i], preferred_element_type=jnp.float32)
        v += jnp.dot(x[i], near_v[i], preferred_element_type=jnp.float32)
    out[:, :HEAD] = _rotate(k + k_bias[...], cosine, sine).astype(jnp.bfloat16)
    out[:, HEAD:] = (v + v_bias[...]).astype(jnp.bfloat16)


def _last_kv(slices, arrays, pieces, w_k, w_v, acc, k_bias, v_bias, cosine, sine):
    n = len(pieces)
    near = [acc, k_bias, v_bias, cosine, sine]
    return pl.pallas_call(
        functools.partial(_last_kv_body, len(arrays), pieces),
        out_shape=jax.ShapeDtypeStruct((HALF, 2 * HEAD), jnp.bfloat16),
        in_specs=[SMEM] + [HBM] * (len(arrays) + 2) + [VMEM] * len(near),
        out_specs=VMEM,
        scratch_shapes=[
            pltpu.VMEM((n, HALF, DEPTH), jnp.bfloat16),
            pltpu.VMEM((n, DEPTH, HEAD), jnp.bfloat16),
            pltpu.VMEM((n, DEPTH, HEAD), jnp.bfloat16),
            pltpu.SemaphoreType.DMA((n, 2)),
            pltpu.SemaphoreType.DMA((n, 2)),
        ],
        compiler_params=pltpu.CompilerParams(vmem_limit_bytes=8 * 1024 * 1024),
        cost_estimate=pl.CostEstimate(
            flops=4 * n * HALF * DEPTH * HEAD,
            bytes_accessed=4 * n * DEPTH * HEAD,
            transcendentals=0,
        ),
        name="last_kv",
    )(slices, *arrays, w_k, w_v, *near)


def _last_q_body(arrays, pieces, slices, *refs):
    n = len(pieces)
    parts, w_q = refs[:arrays], refs[arrays]
    acc, q_bias, cosine, sine, out, x, near, x_sem, w_sem = refs[arrays + 1 :]
    x_loads = _piece_loads(parts, pieces, x, x_sem)
    for group in x_loads:
        _start(group)
    w_loads = []
    for i in range(4):
        cols = slice(i * 2 * HEAD, (i + 1) * 2 * HEAD)
        w_loads.append(
            [
                pltpu.make_async_copy(
                    w_q.at[_block(slices[j]), cols], near.at[i, j], w_sem.at[i, j]
                )
                for j in range(n)
            ]
        )
    _start(w_loads[0])
    _start(w_loads[1])
    for group in x_loads:
        _wait(group)
    for i in range(4):
        both = slice(i * 2 * HEAD, (i + 1) * 2 * HEAD)
        q = acc[:, both] + q_bias[:, both]
        _wait(w_loads[i])
        if i + 2 < 4:
            _start(w_loads[i + 2])
        for j in range(n):
            q += jnp.dot(x[j], near[i, j], preferred_element_type=jnp.float32)
        for j in range(2):
            cols = slice((2 * i + j) * HEAD, (2 * i + j + 1) * HEAD)
            u = q[:, j * HEAD : (j + 1) * HEAD]
            out[:, cols] = _rotate(u, cosine, sine).astype(jnp.bfloat16)


def _last_q(slices, arrays, pieces, w_q, acc, q_bias, cosine, sine):
    n = len(pieces)
    near = [acc, q_bias, cosine, sine]
    return pl.pallas_call(
        functools.partial(_last_q_body, len(arrays), pieces),
        out_shape=jax.ShapeDtypeStruct((HALF, QCOLS), jnp.bfloat16),
        in_specs=[SMEM] + [HBM] * (len(arrays) + 1) + [VMEM] * len(near),
        out_specs=VMEM,
        scratch_shapes=[
            pltpu.VMEM((n, HALF, DEPTH), jnp.bfloat16),
            pltpu.VMEM((4, n, DEPTH, 2 * HEAD), jnp.bfloat16),
            pltpu.SemaphoreType.DMA((n, 2)),
            pltpu.SemaphoreType.DMA((4, n)),
        ],
        compiler_params=pltpu.CompilerParams(vmem_limit_bytes=12 * 1024 * 1024),
        cost_estimate=pl.CostEstimate(
            flops=2 * n * HALF * DEPTH * QCOLS,
            bytes_accessed=2 * n * DEPTH * QCOLS,
            transcendentals=0,
        ),
        name="last_q",
    )(slices, *arrays, w_q, *near)


def _stitch(shapes, moves, *operands):
    def body(*refs):
        sem = refs[-1]
        copies = []
        for i, (operand, start, size, o, at) in enumerate(moves):
            src, out = refs[operand], refs[len(operands) + o]
            if len(src.shape) < len(out.shape):
                copies.append(pltpu.make_async_copy(src, out.at[at], sem.at[i]))
            else:
                copies.append(
                    pltpu.make_async_copy(
                        src.at[pl.ds(start, size)], out.at[pl.ds(at, size)], sem.at[i]
                    )
                )
        _start(copies)
        _wait(copies)

    return pl.pallas_call(
        body,
        out_shape=[jax.ShapeDtypeStruct(shape, jnp.bfloat16) for shape in shapes],
        in_specs=[HBM] * len(operands),
        out_specs=[VMEM] * len(shapes),
        scratch_shapes=[pltpu.SemaphoreType.DMA((len(moves),))],
        compiler_params=pltpu.CompilerParams(vmem_limit_bytes=4 * 1024 * 1024),
        name="stitch",
    )(*operands)


def _stack_pair(first, second):
    return _stitch([(2, HALF, 2 * HEAD)], [(0, 0, 1, 0, 0), (1, 0, 1, 0, 1)], first, second)[0]


def _stack_pairs(pairs):
    moves = [(i, 0, 2, 0, 2 * i) for i in range(4)]
    return _stitch([(8, HALF, 2 * HEAD)], moves, *pairs)[0]


def _attend_body(given, first, final, part, meta, *refs):
    kv, refs = refs[:given], refs[given:]
    queries, refs = refs[:2], refs[2:]
    states_in, refs = ((), refs) if first else (refs[:2], refs[2:])
    outs, refs = refs[:2], refs[2:]
    keys, values = kv if given == 2 else refs[:2]
    rows, even, odd, place = refs[0 if given == 2 else 2 :][:4]
    stat, acc = refs[-2:] if final else outs
    groups = acc.shape[0] // 2
    for group in range(groups):
        for job in range(2):
            for h in range(4):
                col = (part * 4 + group * 4 + h) * HEAD
                rows[2 * group + job, h * HALF : (h + 1) * HALF, :] = queries[job][
                    :, col : col + HEAD
                ]
    for h in range(4):
        place[0:1, h * HALF : (h + 1) * HALF] = lax.broadcasted_iota(jnp.int32, (1, HALF), 1) + 1
    if first:
        stat[:, 0:1, :] = jnp.full((2 * groups, 1, LANES), -1e30, jnp.float32)
        stat[:, 1:8, :] = jnp.zeros((2 * groups, 7, LANES), jnp.float32)
        acc[...] = jnp.zeros_like(acc)
    else:
        stat[...] = states_in[0][2 * part : 2 * part + 2 * groups]
        acc[...] = states_in[1][2 * part : 2 * part + 2 * groups]
    for i in range(TILES if given == 5 else 0):
        start = pl.multiple_of(meta[i] * HALF, HALF)
        tile = kv[i // 2].at[i % 2] if i < 8 else kv[4].at[i - 8]
        keys[pl.ds(start, HALF), :] = tile[:, :HEAD]
        values[pl.ds(start, HALF), :] = tile[:, HEAD:]

    def entry(b, i):
        return meta[TILES + 4 * lax.rem(b, BLOCKS) + i]

    def job_of(b):
        return entry(b, 0) + 2 * lax.div(b, BLOCKS)

    def score(b, out):
        start = pl.multiple_of(entry(b, 1) * HALF, 4 * HALF)
        k = keys[pl.ds(start, SPAN), :]
        scores = lax.dot_general(k, rows[job_of(b)], NT, preferred_element_type=jnp.float32)
        seen = entry(b, 2) + entry(b, 3) * place[0:1, :]
        key = lax.broadcasted_iota(jnp.int32, (SPAN, LANES), 0)
        scores = jnp.where(key < seen, scores, -jnp.inf)
        out[0:SPAN, :] = scores
        out[SPAN : SPAN + 1, :] = jnp.max(scores, axis=0, keepdims=True)

    def finish(b, src):
        job = job_of(b)
        start = pl.multiple_of(entry(b, 1) * HALF, 4 * HALF)
        v = values[pl.ds(start, SPAN), :]
        old = stat[job, 0:1, :]
        new = jnp.maximum(old, src[SPAN : SPAN + 1, :])
        weights = jnp.exp2((src[0:SPAN, :] - new) * EXP2_SCALE)
        shrink = jnp.exp2((old - new) * EXP2_SCALE)
        stat[job, 0:1, :] = new
        stat[job, 1:2, :] = stat[job, 1:2, :] * shrink + jnp.sum(weights, axis=0, keepdims=True)
        acc[job] = acc[job] * shrink + lax.dot_general(
            v, weights.astype(jnp.bfloat16), TN, preferred_element_type=jnp.float32
        )

    total = BLOCKS * groups
    score(0, even)

    @pl.loop(0, (total - 1) // 2)
    def _(i):
        score(2 * i + 1, odd)
        finish(2 * i, even)
        score(2 * i + 2, even)
        finish(2 * i + 1, odd)

    if total % 2:
        finish(total - 1, even)
    else:
        score(total - 1, odd)
        finish(total - 2, even)
        finish(total - 1, odd)
    if final:
        for group in range(groups):
            for job in range(2):
                for h in range(0, 4, 2):
                    cols = slice(h * HALF, (h + 2) * HALF)
                    done = acc[2 * group + job, :, cols] / stat[2 * group + job, 1:2, cols]
                    pair = done.T.astype(jnp.bfloat16)
                    at = (group * 4 + h) * HEAD
                    outs[job][:HALF, at : at + HEAD] = pair[:HALF]
                    outs[job][:HALF, at + HEAD : at + 2 * HEAD] = pair[HALF:]
        if outs[1].shape[0] > HALF:
            spare = outs[1].shape[0] - HALF
            outs[1][HALF:, :] = jnp.zeros((spare, outs[1].shape[1]), jnp.bfloat16)


def _attend(meta, kv, queries, states=(), groups=1, part=0, spare=0):
    final = bool(states)
    ordered = [(TILES * HALF, HEAD)] * (2 if len(kv) == 5 else 0)
    state_shape = [(2 * groups, 8, LANES), (2 * groups, HEAD, LANES)]
    if final:
        out_shape = [
            jax.ShapeDtypeStruct((HALF, groups * 4 * HEAD), jnp.bfloat16),
            jax.ShapeDtypeStruct((HALF + spare, groups * 4 * HEAD), jnp.bfloat16),
        ]
    else:
        out_shape = [jax.ShapeDtypeStruct(shape, jnp.float32) for shape in state_shape]
    if final:
        out_shape += [jax.ShapeDtypeStruct(shape, jnp.bfloat16) for shape in ordered]
        ordered = []
    near = [*kv, *queries, *states]
    out = pl.pallas_call(
        functools.partial(_attend_body, len(kv), not states, final, part),
        out_shape=out_shape,
        in_specs=[SMEM] + [VMEM] * len(near),
        out_specs=[VMEM] * len(out_shape),
        scratch_shapes=[pltpu.VMEM(shape, jnp.bfloat16) for shape in ordered]
        + [
            pltpu.VMEM((2 * groups, LANES, HEAD), jnp.bfloat16),
            pltpu.VMEM((SPAN + 8, LANES), jnp.float32),
            pltpu.VMEM((SPAN + 8, LANES), jnp.float32),
            pltpu.VMEM((8, LANES), jnp.int32),
        ]
        + ([pltpu.VMEM(shape, jnp.float32) for shape in state_shape] if final else []),
        compiler_params=pltpu.CompilerParams(vmem_limit_bytes=28 * 1024 * 1024),
        cost_estimate=pl.CostEstimate(
            flops=4 * groups * BLOCKS * SPAN * HEAD * LANES,
            bytes_accessed=4 * 1024 * 1024,
            transcendentals=groups * BLOCKS * SPAN * LANES,
        ),
        name="attend",
    )(meta, *near)
    return out[:2], out[2:]


def _blocks(early_count, early_own, late_count, late_own):
    early_blocks = early_count // 4 + 1 if early_own else (early_count + 3) // 4
    entries = []
    for b in range(BLOCKS):
        is_late = (b >= early_blocks).astype(jnp.int32)
        tile = 4 * (b - is_late * early_blocks)
        count = jnp.where(is_late == 1, late_count, early_count)
        own = jnp.where(is_late == 1, int(late_own), int(early_own))
        entries += [is_late, jnp.minimum(tile, TILES - 4), (count - tile) * HALF, own]
    return jnp.stack(entries).astype(jnp.int32)


def _angles(positions):
    half = HEAD // 2
    freq = rope_base ** (-2.0 * jnp.arange(half, dtype=jnp.float32) / HEAD)
    phase = positions.astype(jnp.float32)[:, None] * freq[None, :]
    return jnp.cos(phase), jnp.sin(phase)


def _after(value, *earlier):
    return lax.optimization_barrier((value, *earlier))[0]


def local(hidden, w_query, w_key, w_value, q_bias, k_bias, v_bias):
    seq = lax.axis_index("seq")
    tp = lax.axis_index("tp")
    y, x_hi, core = seq // 4, seq // 2 % 2, seq % 2
    x_lo, z = tp // 4, tp % 4
    weights = [w_query, w_key, w_value]
    q_bias, k_bias, v_bias = q_bias[None], k_bias[None], v_bias[None]

    def feature(lo, dz):
        return lo * 4 + (z + dz) % 4

    def tile_seq(dy, dx, dc):
        return ((y + dy) % 4 * 2 + (x_hi ^ dx)) * 2 + (core ^ dc)

    order = jnp.stack(
        [tile_seq(dy, dx, dc) for dc in (0, 1) for dy in (0, -1, 1, 2) for dx in (0, 1)]
    ).astype(jnp.int32)
    far_lo = 1 - x_lo

    def ints(*values):
        return jnp.stack(values).astype(jnp.int32)

    w_query, w_key, w_value = weights = [
        pltpu.with_memory_space_constraint(w, pltpu.HBM) for w in weights
    ]
    early, late = _stitch(
        [(HALF, DEPTH)] * 2, [(0, 0, HALF, 0, 0), (0, HALF, HALF, 1, 0)], hidden
    )
    side = _send(early, x_near)
    up, down = _send(early, z_up), _send(early, z_down)
    late = _send(late, mirror_cross)
    row = jnp.arange(HALF, dtype=jnp.int32)
    rope = _angles(seq * (2 * HALF) + row)
    late_rope = _angles((31 - 2 * seq) * HALF + row)
    up, *ropes = lax.optimization_barrier((up, *rope, *late_rope))
    rope, late_rope = ropes[:2], ropes[2:]
    whole = [(0, 0, HALF)], [(1, 0, HALF)], [(2, 0, HALF)], [(3, 0, HALF)]

    to_up, to_down = _stitch(
        [(HALF + PART, DEPTH)] * 2,
        [(0, 0, PART, 0, 0), (2, 0, HALF, 0, PART), (1, PART, PART, 1, 0), (2, 0, HALF, 1, PART)],
        up,
        down,
        side,
    )
    from_down, from_up = _send(to_up, z_up), _send(to_down, z_down)
    late_side = _send(late, x_near)
    acc = _project(
        ints(feature(x_lo, 0), feature(x_lo, -1), feature(x_lo, 1), feature(far_lo, 0)),
        [early, up, down, side],
        whole,
        weights,
    )
    (far,) = _stitch(
        [(HALF, DEPTH)],
        [(0, 0, PART, 0, 0), (1, 0, PART, 0, PART)],
        _after(from_down, acc),
        from_up,
    )
    last = _send(far, x_near)
    both = _after(_stitch(
        [(2 * HALF, DEPTH)], [(0, 0, HALF, 0, 0), (1, 0, HALF, 0, HALF)], late, late_side
    )[0], far)
    up, down = _send(both, z_up), _send(both, z_down)
    acc = _project(
        ints(feature(x_lo, 2), feature(far_lo, -1), feature(far_lo, 1)),
        [far, from_down, from_up],
        ([(0, 0, HALF)], [(1, PART, HALF)], [(2, PART, HALF)]),
        weights,
        acc,
    )
    late_acc = _project(
        ints(feature(far_lo, 0), feature(x_lo, 0)),
        [_after(late, acc), late_side],
        whole[:2],
        weights,
    )
    which = ints(feature(far_lo, 2))
    last = _after(last, late_acc)
    early_kv = _last_kv(which, [last], whole[:1], w_key, w_value, acc, k_bias, v_bias, *rope)
    early_q = _last_q(
        which, [_after(last, early_kv)], whole[:1], w_query, acc, q_bias, *rope
    )
    pair = _stack_pair(_after(early_kv, early_q), _send(early_kv, x_far))

    early_pairs = [pair, _send(pair, y_up), _send(pair, y_down), _send(pair, y_far)]
    to_up, to_down = _stitch(
        [(HALF, DEPTH)] * 2,
        [
            (0, 0, PART, 0, 0),
            (0, HALF, PART, 0, PART),
            (1, PART, PART, 1, 0),
            (1, HALF + PART, PART, 1, PART),
        ],
        _after(up, pair),
        down,
    )
    from_down, from_up = _send(to_up, z_up), _send(to_down, z_down)
    acc = _project(
        ints(feature(far_lo, -1), feature(x_lo, -1), feature(far_lo, 1), feature(x_lo, 1)),
        [_after(up, to_up), down],
        ([(0, 0, HALF)], [(0, HALF, HALF)], [(1, 0, HALF)], [(1, HALF, HALF)]),
        weights,
        late_acc,
    )
    which = ints(feature(far_lo, 2), feature(x_lo, 2))
    pieces = ([(0, 0, PART), (1, 0, PART)], [(0, PART, PART), (1, PART, PART)])
    late_kv = _last_kv(
        which, [from_down, from_up], pieces, w_key, w_value, acc, k_bias, v_bias, *late_rope
    )
    late_q = _last_q(
        which,
        [_after(from_down, late_kv), from_up],
        pieces,
        w_query,
        acc,
        q_bias,
        *late_rope,
    )

    early_pairs = [*early_pairs[:3], _after(early_pairs[3], late_kv)]
    early_keys = [*early_pairs, _send(_stack_pairs(early_pairs), other_core)]
    pair = _stack_pair(_after(late_kv, late_q), _send(late_kv, x_far))
    early_meta = jnp.concatenate([order, _blocks(seq, True, 16 - seq, False)])
    late_meta = jnp.concatenate([15 - order, _blocks(seq, False, 15 - seq, True)])
    late_pairs = [pair, _send(pair, y_up), _send(pair, y_down), _send(pair, y_far)]
    queries = (early_q, late_q)
    states, _ = _attend(early_meta, early_keys, queries, groups=2)
    late_pairs = [*late_pairs[:3], _after(late_pairs[3], states[0])]
    late_keys = [*late_pairs, _send(_stack_pairs(late_pairs), other_core)]
    (early_low, late_low), ordered = _attend(
        late_meta, late_keys, queries, states, part=0, spare=16
    )
    back_low = _send(late_low, mirror)
    (early_high, late_high), _ = _attend(late_meta, ordered, queries, states, part=1)
    back_high = _send(late_high, mirror)
    return jnp.concatenate(
        [
            jnp.concatenate([early_low, early_high], axis=1),
            jnp.concatenate([back_low[:HALF], back_high], axis=1),
        ],
        axis=0,
    )


def solution(mesh):
    return jax.shard_map(
        local,
        mesh=mesh,
        in_specs=(
            P("seq", "tp"),
            P(None, "tp"),
            P(None, "tp"),
            P(None, "tp"),
            P("tp"),
            P("tp"),
            P("tp"),
        ),
        out_specs=P("seq", "tp"),
        check_vma=False,
    )
```

time: 306 us -> 137 us (0.45)
  waiting for transfers between devices: 142 us -> 14.3 us
  matrix products: 75.1 us -> 0 us
  Pallas kernels: 0 us -> 65 us
  starting transfers between devices: 7.22 us -> 44.1 us
  other arithmetic: 26.6 us -> 2.84 us
  blocking collectives: 18 us -> 0 us
  between operations: 13.2 us -> 0.7 us
  local copies, waits for them, and re-layouts: 16.9 us -> 9.03 us
  loops' own time: 6.24 us -> 0 us
    all_gather x3 -> x0, waiting for transfers between devices: 142 us -> none  [the longest x1 77.3 us: local(): feature_block = lax.all_gather(hidden_in, 'tp', axis=1, tiled=True)]
    dot_general x19 -> x0, matrix products: 75.1 us -> none  [the longest x8 31.7 us: compute(): jnp.dot(weights.astype(jnp.bfloat16), value_block, preferred_element_type...]
    pallas_call x0 -> x20, Pallas kernels: none -> 65 us  [the longest x4 22.3 us: _project(): pl.pallas_call(functools.partial(_proj_body, len(arrays), pieces, acc is...]
    ppermute x0 -> x24, starting transfers between devices: none -> 44.1 us  [_send(): return lax.ppermute(value, AXES, pairs)]
    reduce_sum x8 -> x0, other arithmetic: 20.1 us -> none  [compute(): new_sum = old_sum * shrink + jnp.sum(weights, axis=1)]
    all_to_all x1 -> x0, blocking collectives: 18 us -> none  [local(): lax.all_to_all(mixed, 'seq', split_axis=0, concat_axis=0, tiled=True)]
    ppermute x0 -> x24, waiting for transfers between devices: none -> 14.3 us  [_send(): return lax.ppermute(value, AXES, pairs)]
    cond x40 -> x0, local copies, waits for them, and re-layouts: 9.14 us -> none
  transfers between devices with their start and end apart: 4 -> 24, of which waited for: 3 -> 5; matrix products, arithmetic and copies ran while one was open for 8% -> 2% of each run, Pallas kernels for 0% -> 40%
where the time goes in v1:
time: 137 us; the launch traced here: 136 us
  Pallas kernels  65 us (47%)
  starting transfers between devices  44.1 us (32%)
  waiting for transfers between devices  14.3 us (10%)
  local copies, waits for them, and re-layouts  9.03 us (7%)
  other arithmetic  2.84 us (2%)
    ppermute x24, starting transfers between devices, _send(): return lax.ppermute(value, AXES, pairs)  44.1 us
    pallas_call x4, Pallas kernels, _project(): pl.pallas_call(functools.partial(_proj_body, len(arrays), pieces, acc is...  22.3 us
    pallas_call x3, Pallas kernels, _attend(): pl.pallas_call(functools.partial(_attend_body, len(kv), not states, final...  20.6 us
    ppermute x24, waiting for transfers between devices, _send(): return lax.ppermute(value, AXES, pairs)  14.3 us
    unnamed x70, local copies, waits for them, and re-layouts  8.7 us
    pallas_call x9, Pallas kernels, _stitch(): pl.pallas_call(body, out_shape=[jax.ShapeDtypeStruct(shape, jnp.bfloat16)...  8.63 us
    pallas_call x2, Pallas kernels, _last_q(): pl.pallas_call(functools.partial(_last_q_body, len(arrays), pieces), out_...  8.6 us
    pallas_call x2, Pallas kernels, _last_kv(): pl.pallas_call(functools.partial(_last_kv_body, len(arrays), pieces), out...  4.93 us
  transfers between devices with their start and end apart: 24, of which 5 were waited for; matrix products, arithmetic and copies ran while one was open for 2% of the time, Pallas kernels for 40%

profile of v1, /device:TPU:1, one launch (start us, length us, event | category | flops | bytes accessed | tf_op | source)
XLA Modules:
  0.0 136.0 jit_solution(11486388111519145812)
XLA Ops:
  1.5 2.1 %collective-permute-start.4 = (bf16[192,1024]{1,0:T(8,128)(2,1)S(1)}, bf16[192,1024]{1,0:T(8,128)(2,1)S(1)}, u32[]{:S(2)}, u32[]{:S(2)}) collective-permute-start(bf16[192,1024]{1,0:T(8,128)(2,1)S(1)} %get-tuple-element.37.refs_0_), channel_id=1, source_target_pairs={{0,4},{1,5},{2,6},{3,7},{4,0},{5,1},{6,2},{7,3},{8,12},{9,13},{10,... | collective-permute-start | bytes 1179656 | tf_op jit(solution)/shard_map/ppermute | solution.py:45
  3.7 3.8 %collective-permute-start.3 = (bf16[192,1024]{1,0:T(8,128)(2,1)S(1)}, bf16[192,1024]{1,0:T(8,128)(2,1)S(1)}, u32[]{:S(2)}, u32[]{:S(2)}) collective-permute-start(bf16[192,1024]{1,0:T(8,128)(2,1)S(1)} %get-tuple-element.37.refs_0_), channel_id=1, source_target_pairs={{0,3},{1,0},{2,1},{3,2},{4,7},{5,4},{6,5},{7,6},{8,11},{9,8},{10,9... | collective-permute-start | bytes 1179656 | tf_op jit(solution)/shard_map/ppermute | solution.py:45
  7.4 5.4 %collective-permute-start = (bf16[192,1024]{1,0:T(8,128)(2,1)S(1)}, bf16[192,1024]{1,0:T(8,128)(2,1)S(1)}, u32[]{:S(2)}, u32[]{:S(2)}) collective-permute-start(bf16[192,1024]{1,0:T(8,128)(2,1)S(1)} %get-tuple-element.36), channel_id=1, source_target_pairs={{0,124},{1,125},{2,126},{3,127},{4,120},{5,121},{6,122},{7,123},{8... | collective-permute-start | bytes 1179656 | tf_op jit(solution)/shard_map/ppermute | solution.py:45
  12.8 1.5 %multiply_sine_fusion = (f32[192,64]{1,0:T(8,128)}, f32[192,64]{1,0:T(8,128)}, f32[192,64]{1,0:T(8,128)}, f32[192,64]{1,0:T(8,128)}) fusion(f32[192]{0:T(256)S(1)} %get-tuple-element.73, f32[64]{0:T(128)S(1)} %multiply_power_fusion, f32[192]{0:T(256)S(1)} %get-tuple-element.74), kind=kLoop, calls=%fused_computation.1 | loop fusion | flops 24576 | bytes 198400 | tf_op jit(solution)/shard_map/sin | solution.py:490
  14.3 3.7 %collective-permute-done.2.refs_0_.refs_1_ = bf16[192,1024]{1,0:T(8,128)(2,1)S(1)} collective-permute-done((bf16[192,1024]{1,0:T(8,128)(2,1)S(1)}, bf16[192,1024]{1,0:T(8,128)(2,1)S(1)}, u32[]{:S(2)}, u32[]{:S(2)}) %collective-permute-start.2) | collective-permute-done | bytes 393248 | tf_op jit(solution)/shard_map/ppermute | solution.py:45
  18.0 2.0 %stitch.11 = (bf16[288,1024]{1,0:T(8,128)(2,1)}, bf16[288,1024]{1,0:T(8,128)(2,1)}) custom-call(bf16[192,1024]{1,0:T(8,128)(2,1)S(1)} %collective-permute-done.2.refs_0_.refs_1_, bf16[192,1024]{1,0:T(8,128)(2,1)S(1)} %collective-permute-done.3.refs_1_.refs_2_, bf16[192,1024]{1,0:T(8,128)(2,1)S(1)} %collective-permute-done.4.refs_2_.refs_3_), custom_call_target="tpu_custom_call" | custom-call | tf_op jit(solution)/shard_map/stitch/pallas_call | solution.py:323
  20.1 2.7 %collective-permute-start.6 = (bf16[288,1024]{1,0:T(8,128)(2,1)}, bf16[288,1024]{1,0:T(8,128)(2,1)S(1)}, u32[]{:S(2)}, u32[]{:S(2)}) collective-permute-start(bf16[288,1024]{1,0:T(8,128)(2,1)} %get-tuple-element.41), channel_id=1, source_target_pairs={{0,3},{1,0},{2,1},{3,2},{4,7},{5,4},{6,5},{7,6},{8,11},{9,8},{10,9... | collective-permute-start | bytes 1769480 | tf_op jit(solution)/shard_map/ppermute | solution.py:45
  26.1 6.4 %project.4.refs_6_ = f32[192,1280]{1,0:T(8,128)S(1)} custom-call(s32[4]{0:T(128)S(1)} %pad_add_fusion.1.slices, bf16[192,1024]{1,0:T(8,128)(2,1)S(1)} %copy-done.22, bf16[192,1024]{1,0:T(8,128)(2,1)S(1)} %copy-done.9, bf16[192,1024]{1,0:T(8,128)(2,1)S(1)} %copy-done.7, bf16[192,1024]{1,0:T(8,128)(2,1)S(1)} %collective-permute-done.4.refs_2_.refs_3_, ...), custom_call_target="tpu_custom_call" | custom-call | flops 2013265920 | bytes 10485760 | tf_op jit(solution)/shard_map/project/pallas_call | solution.py:173
  32.5 1.3 stitch.10
  34.2 1.3 stitch.12.refs_0_
  36.3 2.7 %collective-permute-start.10 = (bf16[384,1024]{1,0:T(8,128)(2,1)}, bf16[384,1024]{1,0:T(8,128)(2,1)S(1)}, u32[]{:S(2)}, u32[]{:S(2)}) collective-permute-start(bf16[384,1024]{1,0:T(8,128)(2,1)} %stitch.10), channel_id=1, source_target_pairs={{0,3},{1,0},{2,1},{3,2},{4,7},{5,4},{6,5},{7,6},{8,11},{9,8},{10,9... | collective-permute-start | bytes 2359304 | tf_op jit(solution)/shard_map/ppermute | solution.py:45
  41.1 5.3 %project.5.refs_3_.refs_2_ = f32[192,1280]{1,0:T(8,128)S(1)} custom-call(s32[3]{0:T(128)S(1)} %pad_add_fusion.3.slices, bf16[192,1024]{1,0:T(8,128)(2,1)} %stitch.12.refs_0_, bf16[288,1024]{1,0:T(8,128)(2,1)S(1)} %collective-permute-done.5.refs_0_.refs_1_, bf16[288,1024]{1,0:T(8,128)(2,1)S(1)} %copy-done.1, ...), custom_call_target="tpu_custom_call", output_to_operand_aliasing={{}: (7, {})} | custom-call | flops 1509949440 | bytes 7864320 | tf_op jit(solution)/shard_map/project/pallas_call | solution.py:173
  46.5 4.1 %project.6.refs_5_ = f32[192,1280]{1,0:T(8,128)S(1)} custom-call(s32[2]{0:T(128)S(1)} %pad_add_fusion.2.slices, bf16[192,1024]{1,0:T(8,128)(2,1)S(1)} %copy-done.3, bf16[192,1024]{1,0:T(8,128)(2,1)S(1)} %copy-done.5, bf16[8192,1024]{1,0:T(8,128)(2,1)} %refs_2_.9, bf16[8192,128]{1,0:T(8,128)(2,1)} %refs_2_.8, bf16[8192,128]{1,0:T(8,128)(2,1)} %refs_3_.7), custom_call_target="tpu_custom_call" | custom-call | flops 1006632960 | bytes 5242880 | tf_op jit(solution)/shard_map/project/pallas_call | solution.py:173
  50.6 1.5 %last_kv.2.refs_0_ = bf16[192,256]{1,0:T(8,128)(2,1)S(1)} custom-call(s32[1]{0:T(128)} %bitcast.36.slices, bf16[192,1024]{1,0:T(8,128)(2,1)} %collective-permute-done.8.refs_0_, bf16[8192,128]{1,0:T(8,128)(2,1)} %refs_2_.8, bf16[8192,128]{1,0:T(8,128)(2,1)} %refs_3_.7, f32[192,1280]{1,0:T(8,128)S(1)} %project.5.refs_3_.refs_2_, f32[1,128]{1,0:T(1,128)S(1)} %bitcast.69, ...), custom_call_target="tpu_custom_call" | custom-call | flops 100663296 | bytes 524288 | tf_op jit(solution)/shard_map/last_kv/pallas_call | solution.py:224
  52.2 2.7 %collective-permute-start.9 = (bf16[192,256]{1,0:T(8,128)(2,1)S(1)}, bf16[192,256]{1,0:T(8,128)(2,1)S(1)}, u32[]{:S(2)}, u32[]{:S(2)}) collective-permute-start(bf16[192,256]{1,0:T(8,128)(2,1)S(1)} %last_kv.2.refs_0_), channel_id=1, source_target_pairs={{0,16},{1,17},{2,18},{3,19},{4,20},{5,21},{6,22},{7,23},{8,24},{9,... | collective-permute-start | bytes 294920 | tf_op jit(solution)/shard_map/ppermute | solution.py:45
  54.9 3.2 %last_q.2.refs_5_.refs_2_ = bf16[192,1024]{1,0:T(8,128)(2,1)S(1)} custom-call(s32[1]{0:T(128)} %bitcast.36.slices, bf16[192,1024]{1,0:T(8,128)(2,1)} %collective-permute-done.8.refs_0_, bf16[8192,1024]{1,0:T(8,128)(2,1)} %refs_2_.9, f32[192,1280]{1,0:T(8,128)S(1)} %project.5.refs_3_.refs_2_, f32[1,1024]{1,0:T(1,128)S(1)} %bitcast.67, ...), custom_call_target="tpu_custom_call" | custom-call | flops 402653184 | bytes 2097152 | tf_op jit(solution)/shard_map/last_q/pallas_call | solution.py:285
  61.1 2.9 %collective-permute-start.19 = (bf16[2,192,256]{2,1,0:T(8,128)(2,1)S(1)}, bf16[2,192,256]{2,1,0:T(8,128)(2,1)S(1)}, u32[]{:S(2)}, u32[]{:S(2)}) collective-permute-start(bf16[2,192,256]{2,1,0:T(8,128)(2,1)S(1)} %stitch.13.refs_0_), channel_id=1, source_target_pairs={{0,64},{1,65},{2,66},{3,67},{4,68},{5,69},{6,70},{7,71},{8,72},{9,... | collective-permute-start | bytes 589832 | tf_op jit(solution)/shard_map/ppermute | solution.py:45
  65.6 6.5 %project.7.refs_4_.refs_3_ = f32[192,1280]{1,0:T(8,128)S(1)} custom-call(s32[4]{0:T(128)S(1)} %pad_add_fusion.4.slices, bf16[384,1024]{1,0:T(8,128)(2,1)S(1)} %collective-permute-done.7.refs_0_, bf16[384,1024]{1,0:T(8,128)(2,1)S(1)} %collective-permute-done.10.refs_1_, bf16[8192,1024]{1,0:T(8,128)(2,1)} %refs_2_.9, ...), custom_call_target="tpu_custom_call", output_to_operand_aliasing={{}: (6, {})} | custom-call | flops 2013265920 | bytes 10485760 | tf_op jit(solution)/shard_map/project/pallas_call | solution.py:173
  72.1 3.4 %last_kv.3.refs_0_ = bf16[192,256]{1,0:T(8,128)(2,1)S(1)} custom-call(s32[2]{0:T(128)S(1)} %pad_add_fusion.slices, bf16[192,1024]{1,0:T(8,128)(2,1)S(1)} %collective-permute-done.11.refs_0_, bf16[192,1024]{1,0:T(8,128)(2,1)S(1)} %collective-permute-done.12.refs_1_, bf16[8192,128]{1,0:T(8,128)(2,1)} %refs_2_.8, bf16[8192,128]{1,0:T(8,128)(2,1)} %refs_3_.7, ...), custom_call_target="tpu_custom_call" | custom-call | flops 201326592 | bytes 1048576 | tf_op jit(solution)/shard_map/last_kv/pallas_call | solution.py:224
  76.6 5.7 %collective-permute-start.20 = (bf16[8,192,256]{2,1,0:T(8,128)(2,1)S(1)}, bf16[8,192,256]{2,1,0:T(8,128)(2,1)}, u32[]{:S(2)}, u32[]{:S(2)}) collective-permute-start(bf16[8,192,256]{2,1,0:T(8,128)(2,1)S(1)} %stitch.16), channel_id=1, source_target_pairs={{0,8},{1,9},{2,10},{3,11},{4,12},{5,13},{6,14},{7,15},{8,0},{9,1},... | collective-permute-start | bytes 2359304 | tf_op jit(solution)/shard_map/ppermute | solution.py:45
  82.4 2.5 %collective-permute-start.13 = (bf16[192,256]{1,0:T(8,128)(2,1)S(1)}, bf16[192,256]{1,0:T(8,128)(2,1)S(1)}, u32[]{:S(2)}, u32[]{:S(2)}) collective-permute-start(bf16[192,256]{1,0:T(8,128)(2,1)S(1)} %last_kv.3.refs_0_), channel_id=1, source_target_pairs={{0,16},{1,17},{2,18},{3,19},{4,20},{5,21},{6,22},{7,23},{8,24},{9,... | collective-permute-start | bytes 294920 | tf_op jit(solution)/shard_map/ppermute | solution.py:45
  85.1 5.4 %last_q.3.refs_6_.refs_3_ = bf16[192,1024]{1,0:T(8,128)(2,1)S(1)} custom-call(s32[2]{0:T(128)S(1)} %pad_add_fusion.slices, bf16[192,1024]{1,0:T(8,128)(2,1)S(1)} %collective-permute-done.11.refs_0_, bf16[192,1024]{1,0:T(8,128)(2,1)S(1)} %collective-permute-done.12.refs_1_, bf16[8192,1024]{1,0:T(8,128)(2,1)} %refs_2_.9, ...), custom_call_target="tpu_custom_call" | custom-call | flops 805306368 | bytes 4194304 | tf_op jit(solution)/shard_map/last_q/pallas_call | solution.py:285
  91.4 2.3 %collective-permute-start.15 = (bf16[2,192,256]{2,1,0:T(8,128)(2,1)S(1)}, bf16[2,192,256]{2,1,0:T(8,128)(2,1)S(1)}, u32[]{:S(2)}, u32[]{:S(2)}) collective-permute-start(bf16[2,192,256]{2,1,0:T(8,128)(2,1)S(1)} %stitch.15.refs_0_), channel_id=1, source_target_pairs={{0,96},{1,97},{2,98},{3,99},{4,100},{5,101},{6,102},{7,103},{8,104... | collective-permute-start | bytes 589832 | tf_op jit(solution)/shard_map/ppermute | solution.py:45
  93.8 10.1 %attend.3 = (f32[4,8,768]{2,1,0:T(8,128)S(1)}, f32[4,128,768]{2,1,0:T(8,128)S(1)}) custom-call(s32[36]{0:T(128)S(1)} %concatenate.17.meta, bf16[2,192,256]{2,1,0:T(8,128)(2,1)S(1)} %copy-done.15, bf16[2,192,256]{2,1,0:T(8,128)(2,1)S(1)} %copy-done.28, bf16[2,192,256]{2,1,0:T(8,128)(2,1)S(1)} %copy-done.26, bf16[2,192,256]{2,1,0:T(8,128)(2,1)S(1)} %copy-done.24, ...), custom_call_target="tpu_custom_call" | custom-call | flops 3019898880 | bytes 4194304 | tf_op jit(solution)/shard_map/attend/pallas_call | solution.py:450
  103.9 1.2 copy-done.32
  107.4 1.6 %collective-permute-done.21.refs_4_ = bf16[8,192,256]{2,1,0:T(8,128)(2,1)S(1)} collective-permute-done((bf16[8,192,256]{2,1,0:T(8,128)(2,1)S(1)}, bf16[8,192,256]{2,1,0:T(8,128)(2,1)S(1)}, u32[]{:S(2)}, u32[]{:S(2)}) %collective-permute-start.21) | collective-permute-done | bytes 786464 | tf_op jit(solution)/shard_map/ppermute | solution.py:45
  109.0 1.4 %copy-done.33 = f32[4,128,768]{2,1,0:T(8,128)S(1)} copy-done((f32[4,128,768]{2,1,0:T(8,128)S(1)}, f32[4,128,768]{2,1,0:T(8,128)}, u32[]{:S(2)}) %copy-start.33) | copy-done | bytes 1572888
  110.4 5.4 %attend.4 = (bf16[192,512]{1,0:T(8,128)(2,1)S(1)}, bf16[208,512]{1,0:T(8,128)(2,1)S(1)}, bf16[3072,128]{1,0:T(8,128)(2,1)S(1)}, bf16[3072,128]{1,0:T(8,128)(2,1)S(1)}) custom-call(s32[36]{0:T(128)S(1)} %concatenate.16.meta, bf16[2,192,256]{2,1,0:T(8,128)(2,1)S(1)} %stitch.15.refs_0_, bf16[2,192,256]{2,1,0:T(8,128)(2,1)S(1)} %collective-permute-done.14.refs_1_, ...), custom_call_target="tpu_custom_call" | custom-call | flops 1509949440 | bytes 4194304 | tf_op jit(solution)/shard_map/attend/pallas_call | solution.py:450
  115.8 3.7 %collective-permute-start.22 = (bf16[208,512]{1,0:T(8,128)(2,1)S(1)}, bf16[208,512]{1,0:T(8,128)(2,1)S(1)}, u32[]{:S(2)}, u32[]{:S(2)}) collective-permute-start(bf16[208,512]{1,0:T(8,128)(2,1)S(1)} %get-tuple-element.65), channel_id=1, source_target_pairs={{0,120},{1,121},{2,122},{3,123},{4,124},{5,125},{6,126},{7,127},{8... | collective-permute-start | bytes 638984 | tf_op jit(solution)/shard_map/ppermute | solution.py:45
  119.6 5.1 %attend.5 = (bf16[192,512]{1,0:T(8,128)(2,1)S(1)}, bf16[192,512]{1,0:T(8,128)(2,1)S(1)}) custom-call(s32[36]{0:T(128)S(1)} %concatenate.16.meta, bf16[3072,128]{1,0:T(8,128)(2,1)S(1)} %get-tuple-element.62.refs_0_, bf16[3072,128]{1,0:T(8,128)(2,1)S(1)} %get-tuple-element.63.refs_1_, bf16[192,1024]{1,0:T(8,128)(2,1)S(1)} %copy-done.18, ...), custom_call_target="tpu_custom_call" | custom-call | flops 1509949440 | bytes 4194304 | tf_op jit(solution)/shard_map/attend/pallas_call | solution.py:450
  124.7 1.8 %collective-permute-start.23 = (bf16[192,512]{1,0:T(8,128)(2,1)S(1)}, bf16[192,512]{1,0:T(8,128)(2,1)S(1)}, u32[]{:S(2)}, u32[]{:S(2)}) collective-permute-start(bf16[192,512]{1,0:T(8,128)(2,1)S(1)} %get-tuple-element.66), channel_id=1, source_target_pairs={{0,120},{1,121},{2,122},{3,123},{4,124},{5,125},{6,126},{7,127},{8... | collective-permute-start | bytes 589832 | tf_op jit(solution)/shard_map/ppermute | solution.py:45
  126.8 8.3 %collective-permute-done.23 = bf16[192,512]{1,0:T(8,128)(2,1)S(1)} collective-permute-done((bf16[192,512]{1,0:T(8,128)(2,1)S(1)}, bf16[192,512]{1,0:T(8,128)(2,1)S(1)}, u32[]{:S(2)}, u32[]{:S(2)}) %collective-permute-start.23) | collective-permute-done | bytes 196640 | tf_op jit(solution)/shard_map/ppermute | solution.py:45
  (120 shorter events, 18.4 us)
Async XLA Ops:
  1.5 18.5 %copy-start.21 = (bf16[192,1024]{1,0:T(8,128)(2,1)}, bf16[192,1024]{1,0:T(8,128)(2,1)S(1)}, u32[]{:S(2)}) copy-start(bf16[192,1024]{1,0:T(8,128)(2,1)S(1)} %get-tuple-element.37.refs_0_) | copy-start | bytes 1179652
  1.5 16.5 %collective-permute-start.4 = (bf16[192,1024]{1,0:T(8,128)(2,1)S(1)}, bf16[192,1024]{1,0:T(8,128)(2,1)S(1)}, u32[]{:S(2)}, u32[]{:S(2)}) collective-permute-start(bf16[192,1024]{1,0:T(8,128)(2,1)S(1)} %get-tuple-element.37.refs_0_), channel_id=1, source_target_pairs={{0,4},{1,5},{2,6},{3,7},{4,0},{5,1},{6,2},{7,3},{8,12},{9,13},{10,... | collective-permute-start | bytes 1179656 | tf_op jit(solution)/shard_map/ppermute | solution.py:45
  3.7 14.3 %collective-permute-start.3 = (bf16[192,1024]{1,0:T(8,128)(2,1)S(1)}, bf16[192,1024]{1,0:T(8,128)(2,1)S(1)}, u32[]{:S(2)}, u32[]{:S(2)}) collective-permute-start(bf16[192,1024]{1,0:T(8,128)(2,1)S(1)} %get-tuple-element.37.refs_0_), channel_id=1, source_target_pairs={{0,3},{1,0},{2,1},{3,2},{4,7},{5,4},{6,5},{7,6},{8,11},{9,8},{10,9... | collective-permute-start | bytes 1179656 | tf_op jit(solution)/shard_map/ppermute | solution.py:45
  7.4 10.6 %collective-permute-start.2 = (bf16[192,1024]{1,0:T(8,128)(2,1)S(1)}, bf16[192,1024]{1,0:T(8,128)(2,1)S(1)}, u32[]{:S(2)}, u32[]{:S(2)}) collective-permute-start(bf16[192,1024]{1,0:T(8,128)(2,1)S(1)} %get-tuple-element.37.refs_0_), channel_id=1, source_target_pairs={{0,1},{1,2},{2,3},{3,0},{4,5},{5,6},{6,7},{7,4},{8,9},{9,10},{10,1... | collective-permute-start | bytes 1179656 | tf_op jit(solution)/shard_map/ppermute | solution.py:45
  7.4 15.3 %collective-permute-start = (bf16[192,1024]{1,0:T(8,128)(2,1)S(1)}, bf16[192,1024]{1,0:T(8,128)(2,1)S(1)}, u32[]{:S(2)}, u32[]{:S(2)}) collective-permute-start(bf16[192,1024]{1,0:T(8,128)(2,1)S(1)} %get-tuple-element.36), channel_id=1, source_target_pairs={{0,124},{1,125},{2,126},{3,127},{4,120},{5,121},{6,122},{7,123},{8... | collective-permute-start | bytes 1179656 | tf_op jit(solution)/shard_map/ppermute | solution.py:45
  20.0 14.2 %collective-permute-start.5 = (bf16[288,1024]{1,0:T(8,128)(2,1)}, bf16[288,1024]{1,0:T(8,128)(2,1)S(1)}, u32[]{:S(2)}, u32[]{:S(2)}) collective-permute-start(bf16[288,1024]{1,0:T(8,128)(2,1)} %get-tuple-element.39), channel_id=1, source_target_pairs={{0,1},{1,2},{2,3},{3,0},{4,5},{5,6},{6,7},{7,4},{8,9},{9,10},{10,1... | collective-permute-start | bytes 1769480 | tf_op jit(solution)/shard_map/ppermute | solution.py:45
  20.1 14.1 %collective-permute-start.6 = (bf16[288,1024]{1,0:T(8,128)(2,1)}, bf16[288,1024]{1,0:T(8,128)(2,1)S(1)}, u32[]{:S(2)}, u32[]{:S(2)}) collective-permute-start(bf16[288,1024]{1,0:T(8,128)(2,1)} %get-tuple-element.41), channel_id=1, source_target_pairs={{0,3},{1,0},{2,1},{3,2},{4,7},{5,4},{6,5},{7,6},{8,11},{9,8},{10,9... | collective-permute-start | bytes 1769480 | tf_op jit(solution)/shard_map/ppermute | solution.py:45
  22.8 9.7 %copy-start.2 = (bf16[192,1024]{1,0:T(8,128)(2,1)}, bf16[192,1024]{1,0:T(8,128)(2,1)S(1)}, u32[]{:S(2)}) copy-start(bf16[192,1024]{1,0:T(8,128)(2,1)S(1)} %collective-permute-done.refs_0_) | copy-start | bytes 1179652
  22.8 9.7 %collective-permute-start.1 = (bf16[192,1024]{1,0:T(8,128)(2,1)S(1)}, bf16[192,1024]{1,0:T(8,128)(2,1)S(1)}, u32[]{:S(2)}, u32[]{:S(2)}) collective-permute-start(bf16[192,1024]{1,0:T(8,128)(2,1)S(1)} %collective-permute-done.refs_0_), channel_id=1, source_target_pairs={{0,4},{1,5},{2,6},{3,7},{4,0},{5,1},{6,2},{7,3},{8,12},{9,13},{10,... | collective-permute-start | bytes 1179656 | tf_op jit(solution)/shard_map/ppermute | solution.py:45
  36.3 22.1 %collective-permute-start.7 = (bf16[384,1024]{1,0:T(8,128)(2,1)}, bf16[384,1024]{1,0:T(8,128)(2,1)S(1)}, u32[]{:S(2)}, u32[]{:S(2)}) collective-permute-start(bf16[384,1024]{1,0:T(8,128)(2,1)} %stitch.10), channel_id=1, source_target_pairs={{0,1},{1,2},{2,3},{3,0},{4,5},{5,6},{6,7},{7,4},{8,9},{9,10},{10,1... | collective-permute-start | bytes 2359304 | tf_op jit(solution)/shard_map/ppermute | solution.py:45
  36.3 22.1 %collective-permute-start.10 = (bf16[384,1024]{1,0:T(8,128)(2,1)}, bf16[384,1024]{1,0:T(8,128)(2,1)S(1)}, u32[]{:S(2)}, u32[]{:S(2)}) collective-permute-start(bf16[384,1024]{1,0:T(8,128)(2,1)} %stitch.10), channel_id=1, source_target_pairs={{0,3},{1,0},{2,1},{3,2},{4,7},{5,4},{6,5},{7,6},{8,11},{9,8},{10,9... | collective-permute-start | bytes 2359304 | tf_op jit(solution)/shard_map/ppermute | solution.py:45
  39.0 11.6 %collective-permute-start.8 = (bf16[192,1024]{1,0:T(8,128)(2,1)}, bf16[192,1024]{1,0:T(8,128)(2,1)}, u32[]{:S(2)}, u32[]{:S(2)}) collective-permute-start(bf16[192,1024]{1,0:T(8,128)(2,1)} %stitch.12.refs_0_), channel_id=1, source_target_pairs={{0,4},{1,5},{2,6},{3,7},{4,0},{5,1},{6,2},{7,3},{8,12},{9,13},{10,... | collective-permute-start | bytes 1179656 | tf_op jit(solution)/shard_map/ppermute | solution.py:45
  52.2 5.9 %collective-permute-start.9 = (bf16[192,256]{1,0:T(8,128)(2,1)S(1)}, bf16[192,256]{1,0:T(8,128)(2,1)S(1)}, u32[]{:S(2)}, u32[]{:S(2)}) collective-permute-start(bf16[192,256]{1,0:T(8,128)(2,1)S(1)} %last_kv.2.refs_0_), channel_id=1, source_target_pairs={{0,16},{1,17},{2,18},{3,19},{4,20},{5,21},{6,22},{7,23},{8,24},{9,... | collective-permute-start | bytes 294920 | tf_op jit(solution)/shard_map/ppermute | solution.py:45
  58.4 17.2 %copy-start.14 = (bf16[2,192,256]{2,1,0:T(8,128)(2,1)}, bf16[2,192,256]{2,1,0:T(8,128)(2,1)S(1)}, u32[]{:S(2)}) copy-start(bf16[2,192,256]{2,1,0:T(8,128)(2,1)S(1)} %stitch.13.refs_0_) | copy-start | bytes 589828
  59.5 12.6 %collective-permute-start.12 = (bf16[192,1024]{1,0:T(8,128)(2,1)S(1)}, bf16[192,1024]{1,0:T(8,128)(2,1)S(1)}, u32[]{:S(2)}, u32[]{:S(2)}) collective-permute-start(bf16[192,1024]{1,0:T(8,128)(2,1)S(1)} %get-tuple-element.51), channel_id=1, source_target_pairs={{0,3},{1,0},{2,1},{3,2},{4,7},{5,4},{6,5},{7,6},{8,11},{9,8},{10,9... | collective-permute-start | bytes 1179656 | tf_op jit(solution)/shard_map/ppermute | solution.py:45
  60.3 11.7 %collective-permute-start.11 = (bf16[192,1024]{1,0:T(8,128)(2,1)S(1)}, bf16[192,1024]{1,0:T(8,128)(2,1)S(1)}, u32[]{:S(2)}, u32[]{:S(2)}) collective-permute-start(bf16[192,1024]{1,0:T(8,128)(2,1)S(1)} %get-tuple-element.50), channel_id=1, source_target_pairs={{0,1},{1,2},{2,3},{3,0},{4,5},{5,6},{6,7},{7,4},{8,9},{9,10},{10,1... | collective-permute-start | bytes 1179656 | tf_op jit(solution)/shard_map/ppermute | solution.py:45
  61.1 11.0 %copy-start.10 = (f32[192,64]{1,0:T(8,128)S(1)}, f32[192,64]{1,0:T(8,128)}, u32[]{:S(2)}) copy-start(f32[192,64]{1,0:T(8,128)} %get-tuple-element.54.refs_8_.refs_6_) | copy-start | bytes 147460
  61.1 11.0 %copy-start.11 = (f32[192,64]{1,0:T(8,128)S(1)}, f32[192,64]{1,0:T(8,128)}, u32[]{:S(2)}) copy-start(f32[192,64]{1,0:T(8,128)} %get-tuple-element.53.refs_7_.refs_5_) | copy-start | bytes 147460
  61.1 14.4 %collective-permute-start.19 = (bf16[2,192,256]{2,1,0:T(8,128)(2,1)S(1)}, bf16[2,192,256]{2,1,0:T(8,128)(2,1)S(1)}, u32[]{:S(2)}, u32[]{:S(2)}) collective-permute-start(bf16[2,192,256]{2,1,0:T(8,128)(2,1)S(1)} %stitch.13.refs_0_), channel_id=1, source_target_pairs={{0,64},{1,65},{2,66},{3,67},{4,68},{5,69},{6,70},{7,71},{8,72},{9,... | collective-permute-start | bytes 589832 | tf_op jit(solution)/shard_map/ppermute | solution.py:45
  64.1 11.4 %collective-permute-start.18 = (bf16[2,192,256]{2,1,0:T(8,128)(2,1)S(1)}, bf16[2,192,256]{2,1,0:T(8,128)(2,1)S(1)}, u32[]{:S(2)}, u32[]{:S(2)}) collective-permute-start(bf16[2,192,256]{2,1,0:T(8,128)(2,1)S(1)} %stitch.13.refs_0_), channel_id=1, source_target_pairs={{0,96},{1,97},{2,98},{3,99},{4,100},{5,101},{6,102},{7,103},{8,104... | collective-permute-start | bytes 589832 | tf_op jit(solution)/shard_map/ppermute | solution.py:45
  64.9 10.7 %collective-permute-start.17 = (bf16[2,192,256]{2,1,0:T(8,128)(2,1)S(1)}, bf16[2,192,256]{2,1,0:T(8,128)(2,1)S(1)}, u32[]{:S(2)}, u32[]{:S(2)}) collective-permute-start(bf16[2,192,256]{2,1,0:T(8,128)(2,1)S(1)} %stitch.13.refs_0_), channel_id=1, source_target_pairs={{0,32},{1,33},{2,34},{3,35},{4,36},{5,37},{6,38},{7,39},{8,40},{9,... | collective-permute-start | bytes 589832 | tf_op jit(solution)/shard_map/ppermute | solution.py:45
  76.6 17.1 %collective-permute-start.20 = (bf16[8,192,256]{2,1,0:T(8,128)(2,1)S(1)}, bf16[8,192,256]{2,1,0:T(8,128)(2,1)}, u32[]{:S(2)}, u32[]{:S(2)}) collective-permute-start(bf16[8,192,256]{2,1,0:T(8,128)(2,1)S(1)} %stitch.16), channel_id=1, source_target_pairs={{0,8},{1,9},{2,10},{3,11},{4,12},{5,13},{6,14},{7,15},{8,0},{9,1},... | collective-permute-start | bytes 2359304 | tf_op jit(solution)/shard_map/ppermute | solution.py:45
  82.4 8.2 %collective-permute-start.13 = (bf16[192,256]{1,0:T(8,128)(2,1)S(1)}, bf16[192,256]{1,0:T(8,128)(2,1)S(1)}, u32[]{:S(2)}, u32[]{:S(2)}) collective-permute-start(bf16[192,256]{1,0:T(8,128)(2,1)S(1)} %last_kv.3.refs_0_), channel_id=1, source_target_pairs={{0,16},{1,17},{2,18},{3,19},{4,20},{5,21},{6,22},{7,23},{8,24},{9,... | collective-permute-start | bytes 294920 | tf_op jit(solution)/shard_map/ppermute | solution.py:45
  85.0 8.7 %copy-start.15 = (bf16[2,192,256]{2,1,0:T(8,128)(2,1)S(1)}, bf16[2,192,256]{2,1,0:T(8,128)(2,1)}, u32[]{:S(2)}) copy-start(bf16[2,192,256]{2,1,0:T(8,128)(2,1)} %copy-done.14) | copy-start | bytes 589828
  90.5 13.4 %copy-start.19 = (bf16[192,1024]{1,0:T(8,128)(2,1)}, bf16[192,1024]{1,0:T(8,128)(2,1)S(1)}, u32[]{:S(2)}) copy-start(bf16[192,1024]{1,0:T(8,128)(2,1)S(1)} %last_q.3.refs_6_.refs_3_) | copy-start | bytes 1179652
  90.8 14.2 %collective-permute-start.16 = (bf16[2,192,256]{2,1,0:T(8,128)(2,1)S(1)}, bf16[2,192,256]{2,1,0:T(8,128)(2,1)S(1)}, u32[]{:S(2)}, u32[]{:S(2)}) collective-permute-start(bf16[2,192,256]{2,1,0:T(8,128)(2,1)S(1)} %stitch.15.refs_0_), channel_id=1, source_target_pairs={{0,64},{1,65},{2,66},{3,67},{4,68},{5,69},{6,70},{7,71},{8,72},{9,... | collective-permute-start | bytes 589832 | tf_op jit(solution)/shard_map/ppermute | solution.py:45
  91.4 13.7 %collective-permute-start.15 = (bf16[2,192,256]{2,1,0:T(8,128)(2,1)S(1)}, bf16[2,192,256]{2,1,0:T(8,128)(2,1)S(1)}, u32[]{:S(2)}, u32[]{:S(2)}) collective-permute-start(bf16[2,192,256]{2,1,0:T(8,128)(2,1)S(1)} %stitch.15.refs_0_), channel_id=1, source_target_pairs={{0,96},{1,97},{2,98},{3,99},{4,100},{5,101},{6,102},{7,103},{8,104... | collective-permute-start | bytes 589832 | tf_op jit(solution)/shard_map/ppermute | solution.py:45
  93.7 11.4 %collective-permute-start.14 = (bf16[2,192,256]{2,1,0:T(8,128)(2,1)S(1)}, bf16[2,192,256]{2,1,0:T(8,128)(2,1)S(1)}, u32[]{:S(2)}, u32[]{:S(2)}) collective-permute-start(bf16[2,192,256]{2,1,0:T(8,128)(2,1)S(1)} %stitch.15.refs_0_), channel_id=1, source_target_pairs={{0,32},{1,33},{2,34},{3,35},{4,36},{5,37},{6,38},{7,39},{8,40},{9,... | collective-permute-start | bytes 589832 | tf_op jit(solution)/shard_map/ppermute | solution.py:45
  106.2 2.9 %collective-permute-start.21 = (bf16[8,192,256]{2,1,0:T(8,128)(2,1)S(1)}, bf16[8,192,256]{2,1,0:T(8,128)(2,1)S(1)}, u32[]{:S(2)}, u32[]{:S(2)}) collective-permute-start(bf16[8,192,256]{2,1,0:T(8,128)(2,1)S(1)} %stitch.17), channel_id=1, source_target_pairs={{0,8},{1,9},{2,10},{3,11},{4,12},{5,13},{6,14},{7,15},{8,0},{9,1},... | collective-permute-start | bytes 2359304 | tf_op jit(solution)/shard_map/ppermute | solution.py:45
  110.4 9.1 %copy-start.34 = (f32[4,128,768]{2,1,0:T(8,128)S(1)}, f32[4,128,768]{2,1,0:T(8,128)}, u32[]{:S(2)}) copy-start(f32[4,128,768]{2,1,0:T(8,128)} %copy-done.32) | copy-start | bytes 4718596
  115.8 10.9 %collective-permute-start.22 = (bf16[208,512]{1,0:T(8,128)(2,1)S(1)}, bf16[208,512]{1,0:T(8,128)(2,1)S(1)}, u32[]{:S(2)}, u32[]{:S(2)}) collective-permute-start(bf16[208,512]{1,0:T(8,128)(2,1)S(1)} %get-tuple-element.65), channel_id=1, source_target_pairs={{0,120},{1,121},{2,122},{3,123},{4,124},{5,125},{6,126},{7,127},{8... | collective-permute-start | bytes 638984 | tf_op jit(solution)/shard_map/ppermute | solution.py:45
  124.7 10.4 %collective-permute-start.23 = (bf16[192,512]{1,0:T(8,128)(2,1)S(1)}, bf16[192,512]{1,0:T(8,128)(2,1)S(1)}, u32[]{:S(2)}, u32[]{:S(2)}) collective-permute-start(bf16[192,512]{1,0:T(8,128)(2,1)S(1)} %get-tuple-element.66), channel_id=1, source_target_pairs={{0,120},{1,121},{2,122},{3,123},{4,124},{5,125},{6,126},{7,127},{8... | collective-permute-start | bytes 589832 | tf_op jit(solution)/shard_map/ppermute | solution.py:45
  (27 other events, 119.0 us)

commit v2 on v1

--- a/solution.py
+++ b/solution.py
@@ -12,6 +12,7 @@
 GROUP = 8
 HALF = 192
 PART = HALF // 2
+ROWS = 2 * HALF
 DEPTH = 1024
 QCOLS = GROUP * HEAD
 ALLCOLS = QCOLS + 2 * HEAD
@@ -88,6 +89,10 @@
 VMEM = pl.BlockSpec(memory_space=pltpu.VMEM)
 HBM = pl.BlockSpec(memory_space=pl.ANY)
 SMEM = pl.BlockSpec(memory_space=pltpu.SMEM)
+
+
+def _in_hbm(value):
+    return pltpu.with_memory_space_constraint(value, pltpu.HBM)
 
 
 def _block(index):
@@ -134,16 +139,17 @@
 def _proj_body(arrays, pieces, started, slices, *refs):
     n = len(pieces)
     parts, far = refs[:arrays], refs[arrays : arrays + 3]
-    at = arrays + 3
-    acc_in = refs[at] if started else None
-    at += 1 if started else 0
-    acc, x, near = refs[at], refs[at + 1], refs[at + 2 : at + 5]
-    x_sem, w_sem = refs[at + 5 : at + 7]
+    refs = refs[arrays + 3 :]
+    acc_in, refs = (refs[0], refs[1:]) if started else (None, refs)
+    acc, x, near, (x_sem, w_sem, acc_sem) = refs[0], refs[1], refs[2:5], refs[5:8]
     x_loads = _piece_loads(parts, pieces, x, x_sem)
     w_loads = _weight_loads(slices, n, far, near, w_sem)
     for i in range(min(2, n)):
         _start(x_loads[i])
         _start(w_loads[i])
+    if started:
+        acc_load = pltpu.make_async_copy(acc_in, acc, acc_sem)
+        acc_load.start()
     spans = (slice(0, QCOLS), slice(QCOLS, QCOLS + HEAD), slice(QCOLS + HEAD, ALLCOLS))
     for i in range(n):
         _wait(x_loads[i])
@@ -151,156 +157,154 @@
         if i + 2 < n:
             _start(x_loads[i + 2])
             _start(w_loads[i + 2])
+        if started and i == 0:
+            acc_load.wait()
         for w, cols in zip(near, spans):
             term = jnp.dot(x[i], w[i], preferred_element_type=jnp.float32)
-            if i:
+            if i or started:
                 acc[:, cols] += term
-            elif started:
-                acc[:, cols] = acc_in[:, cols] + term
             else:
                 acc[:, cols] = term
 
 
 def _project(slices, arrays, pieces, weights, acc=None):
     n = len(pieces)
-    operands = [slices, *arrays, *weights]
-    in_specs = [SMEM] + [HBM] * (len(arrays) + 3)
-    aliases = {}
-    if acc is not None:
-        aliases[len(operands)] = 0
-        operands.append(acc)
-        in_specs.append(VMEM)
+    started = [] if acc is None else [acc]
     return pl.pallas_call(
         functools.partial(_proj_body, len(arrays), pieces, acc is not None),
-        out_shape=jax.ShapeDtypeStruct((HALF, ALLCOLS), jnp.float32),
-        in_specs=in_specs,
+        out_shape=jax.ShapeDtypeStruct((ROWS, ALLCOLS), jnp.float32),
+        in_specs=[SMEM] + [HBM] * (len(arrays) + 3 + len(started)),
         out_specs=VMEM,
-        input_output_aliases=aliases,
         scratch_shapes=[
-            pltpu.VMEM((n, HALF, DEPTH), jnp.bfloat16),
+            pltpu.VMEM((n, ROWS, DEPTH), jnp.bfloat16),
             pltpu.VMEM((n, DEPTH, QCOLS), jnp.bfloat16),
             pltpu.VMEM((n, DEPTH, HEAD), jnp.bfloat16),
             pltpu.VMEM((n, DEPTH, HEAD), jnp.bfloat16),
-            pltpu.SemaphoreType.DMA((n, 2)),
             pltpu.SemaphoreType.DMA((n, 3)),
+            pltpu.SemaphoreType.DMA((n, 3)),
+            pltpu.SemaphoreType.DMA,
         ],
-        compiler_params=pltpu.CompilerParams(vmem_limit_bytes=20 * 1024 * 1024),
+        compiler_params=pltpu.CompilerParams(vmem_limit_bytes=28 * 1024 * 1024),
         cost_estimate=pl.CostEstimate(
-            flops=2 * n * HALF * DEPTH * ALLCOLS,
+            flops=2 * n * ROWS * DEPTH * ALLCOLS,
             bytes_accessed=2 * n * DEPTH * ALLCOLS,
             transcendentals=0,
         ),
         name="project",
-    )(*operands)
+    )(slices, *map(_in_hbm, arrays), *weights, *started)
 
 
 def _rotate(u, cosine, sine):
-    cosine = jnp.concatenate([cosine[...], cosine[...]], axis=1)
-    sine = jnp.concatenate([-sine[...], sine[...]], axis=1)
-    return u * cosine + pltpu.roll(u, HEAD // 2, 1) * sine
+    return u * cosine[...] + pltpu.roll(u, HEAD // 2, 1) * sine[...]
 
 
 def _last_kv_body(arrays, pieces, slices, *refs):
     n = len(pieces)
-    parts, (w_k, w_v) = refs[:arrays], refs[arrays : arrays + 2]
-    acc, k_bias, v_bias, cosine, sine, out, x, near_k, near_v, x_sem, w_sem = refs[arrays + 2 :]
+    parts, (w_k, w_v), refs = refs[:arrays], refs[arrays : arrays + 2], refs[arrays + 2 :]
+    given, (k_bias, v_bias, cosine, sine, out), refs = refs[0], refs[1:6], refs[6:]
+    x, near_k, near_v, acc, x_sem, w_sem, sem = refs
     x_loads = _piece_loads(parts, pieces, x, x_sem)
     w_loads = _weight_loads(slices, n, (w_k, w_v), (near_k, near_v), w_sem)
-    for group in x_loads + w_loads:
+    others = [pltpu.make_async_copy(given.at[:, pl.ds(QCOLS, 2 * HEAD)], acc, sem)]
+    for group in x_loads + w_loads + [others]:
         _start(group)
-    k, v = acc[:, QCOLS : QCOLS + HEAD], acc[:, QCOLS + HEAD :]
+    k = v = 0
     for i in range(n):
         _wait(x_loads[i])
         _wait(w_loads[i])
         k += jnp.dot(x[i], near_k[i], preferred_element_type=jnp.float32)
         v += jnp.dot(x[i], near_v[i], preferred_element_type=jnp.float32)
-    out[:, :HEAD] = _rotate(k + k_bias[...], cosine, sine).astype(jnp.bfloat16)
-    out[:, HEAD:] = (v + v_bias[...]).astype(jnp.bfloat16)
+    _wait(others)
+    k += acc[:, :HEAD]
+    v += acc[:, HEAD:]
+    k = _rotate(k + k_bias[...], cosine, sine).astype(jnp.bfloat16)
+    v = (v + v_bias[...]).astype(jnp.bfloat16)
+    for half in range(2):
+        rows = slice(half * HALF, (half + 1) * HALF)
+        out[half, :, :HEAD] = k[rows]
+        out[half, :, HEAD:] = v[rows]
 
 
 def _last_kv(slices, arrays, pieces, w_k, w_v, acc, k_bias, v_bias, cosine, sine):
     n = len(pieces)
-    near = [acc, k_bias, v_bias, cosine, sine]
     return pl.pallas_call(
         functools.partial(_last_kv_body, len(arrays), pieces),
-        out_shape=jax.ShapeDtypeStruct((HALF, 2 * HEAD), jnp.bfloat16),
-        in_specs=[SMEM] + [HBM] * (len(arrays) + 2) + [VMEM] * len(near),
+        out_shape=jax.ShapeDtypeStruct((2, HALF, 2 * HEAD), jnp.bfloat16),
+        in_specs=[SMEM] + [HBM] * (len(arrays) + 3) + [VMEM] * 4,
         out_specs=VMEM,
         scratch_shapes=[
-            pltpu.VMEM((n, HALF, DEPTH), jnp.bfloat16),
+            pltpu.VMEM((n, ROWS, DEPTH), jnp.bfloat16),
             pltpu.VMEM((n, DEPTH, HEAD), jnp.bfloat16),
             pltpu.VMEM((n, DEPTH, HEAD), jnp.bfloat16),
+            pltpu.VMEM((ROWS, 2 * HEAD), jnp.float32),
+            pltpu.SemaphoreType.DMA((n, 4)),
             pltpu.SemaphoreType.DMA((n, 2)),
-            pltpu.SemaphoreType.DMA((n, 2)),
+            pltpu.SemaphoreType.DMA,
         ],
-        compiler_params=pltpu.CompilerParams(vmem_limit_bytes=8 * 1024 * 1024),
+        compiler_params=pltpu.CompilerParams(vmem_limit_bytes=12 * 1024 * 1024),
         cost_estimate=pl.CostEstimate(
-            flops=4 * n * HALF * DEPTH * HEAD,
+            flops=4 * n * ROWS * DEPTH * HEAD,
             bytes_accessed=4 * n * DEPTH * HEAD,
             transcendentals=0,
         ),
         name="last_kv",
-    )(slices, *arrays, w_k, w_v, *near)
+    )(slices, *map(_in_hbm, arrays), w_k, w_v, acc, k_bias, v_bias, cosine, sine)
 
 
 def _last_q_body(arrays, pieces, slices, *refs):
     n = len(pieces)
-    parts, w_q = refs[:arrays], refs[arrays]
-    acc, q_bias, cosine, sine, out, x, near, x_sem, w_sem = refs[arrays + 1 :]
+    parts, w_q, refs = refs[:arrays], refs[arrays], refs[arrays + 1 :]
+    given, (q_bias, cosine, sine, out), refs = refs[0], refs[1:5], refs[5:]
+    x, near, acc, x_sem, w_sem, sem = refs
     x_loads = _piece_loads(parts, pieces, x, x_sem)
-    for group in x_loads:
-        _start(group)
-    w_loads = []
-    for i in range(4):
-        cols = slice(i * 2 * HEAD, (i + 1) * 2 * HEAD)
-        w_loads.append(
-            [
-                pltpu.make_async_copy(
-                    w_q.at[_block(slices[j]), cols], near.at[i, j], w_sem.at[i, j]
-                )
-                for j in range(n)
-            ]
-        )
+    w_loads = _weight_loads(slices, n, (w_q,), (near,), w_sem)
+    others = [pltpu.make_async_copy(given.at[:, pl.ds(0, QCOLS)], acc, sem)]
+    _start(x_loads[0])
     _start(w_loads[0])
-    _start(w_loads[1])
-    for group in x_loads:
-        _wait(group)
-    for i in range(4):
-        both = slice(i * 2 * HEAD, (i + 1) * 2 * HEAD)
-        q = acc[:, both] + q_bias[:, both]
+    _start(others)
+    for i in range(1, n):
+        _start(x_loads[i])
+        _start(w_loads[i])
+    for i in range(n):
+        _wait(x_loads[i])
         _wait(w_loads[i])
-        if i + 2 < 4:
-            _start(w_loads[i + 2])
-        for j in range(n):
-            q += jnp.dot(x[j], near[i, j], preferred_element_type=jnp.float32)
+        if i == 0:
+            _wait(others)
+        if i < n - 1:
+            acc[...] += jnp.dot(x[i], near[i], preferred_element_type=jnp.float32)
+    for i in range(0, GROUP, 2):
+        both = slice(i * HEAD, (i + 2) * HEAD)
+        q = acc[:, both] + jnp.dot(x[n - 1], near[n - 1, :, both], preferred_element_type=jnp.float32)
+        q += q_bias[:, both]
         for j in range(2):
-            cols = slice((2 * i + j) * HEAD, (2 * i + j + 1) * HEAD)
+            cols = slice((i + j) * HEAD, (i + j + 1) * HEAD)
             u = q[:, j * HEAD : (j + 1) * HEAD]
             out[:, cols] = _rotate(u, cosine, sine).astype(jnp.bfloat16)
 
 
 def _last_q(slices, arrays, pieces, w_q, acc, q_bias, cosine, sine):
     n = len(pieces)
-    near = [acc, q_bias, cosine, sine]
     return pl.pallas_call(
         functools.partial(_last_q_body, len(arrays), pieces),
-        out_shape=jax.ShapeDtypeStruct((HALF, QCOLS), jnp.bfloat16),
-        in_specs=[SMEM] + [HBM] * (len(arrays) + 1) + [VMEM] * len(near),
+        out_shape=jax.ShapeDtypeStruct((ROWS, QCOLS), jnp.bfloat16),
+        in_specs=[SMEM] + [HBM] * (len(arrays) + 2) + [VMEM] * 3,
         out_specs=VMEM,
         scratch_shapes=[
-            pltpu.VMEM((n, HALF, DEPTH), jnp.bfloat16),
-            pltpu.VMEM((4, n, DEPTH, 2 * HEAD), jnp.bfloat16),
-            pltpu.SemaphoreType.DMA((n, 2)),
-            pltpu.SemaphoreType.DMA((4, n)),
+            pltpu.VMEM((n, ROWS, DEPTH), jnp.bfloat16),
+            pltpu.VMEM((n, DEPTH, QCOLS), jnp.bfloat16),
+            pltpu.VMEM((ROWS, QCOLS), jnp.float32),
+            pltpu.SemaphoreType.DMA((n, 4)),
+            pltpu.SemaphoreType.DMA((n, 1)),
+            pltpu.SemaphoreType.DMA,
         ],
-        compiler_params=pltpu.CompilerParams(vmem_limit_bytes=12 * 1024 * 1024),
+        compiler_params=pltpu.CompilerParams(vmem_limit_bytes=20 * 1024 * 1024),
         cost_estimate=pl.CostEstimate(
-            flops=2 * n * HALF * DEPTH * QCOLS,
+            flops=2 * n * ROWS * DEPTH * QCOLS,
             bytes_accessed=2 * n * DEPTH * QCOLS,
             transcendentals=0,
         ),
         name="last_q",
-    )(slices, *arrays, w_q, *near)
+    )(slices, *map(_in_hbm, arrays), w_q, acc, q_bias, cosine, sine)
 
 
 def _stitch(shapes, moves, *operands):
@@ -328,33 +332,29 @@
         scratch_shapes=[pltpu.SemaphoreType.DMA((len(moves),))],
         compiler_params=pltpu.CompilerParams(vmem_limit_bytes=4 * 1024 * 1024),
         name="stitch",
-    )(*operands)
-
-
-def _stack_pair(first, second):
-    return _stitch([(2, HALF, 2 * HEAD)], [(0, 0, 1, 0, 0), (1, 0, 1, 0, 1)], first, second)[0]
-
-
-def _stack_pairs(pairs):
+    )(*map(_in_hbm, operands))
+
+
+def _stack_tiles(arrays):
     moves = [(i, 0, 2, 0, 2 * i) for i in range(4)]
-    return _stitch([(8, HALF, 2 * HEAD)], moves, *pairs)[0]
-
-
-def _attend_body(given, first, final, part, meta, *refs):
+    return _stitch([(8, HALF, 2 * HEAD)], moves, *arrays)[0]
+
+
+def _attend_body(given, sort, first, final, part, meta, *refs):
     kv, refs = refs[:given], refs[given:]
-    queries, refs = refs[:2], refs[2:]
+    queries, refs = refs[0], refs[1:]
     states_in, refs = ((), refs) if first else (refs[:2], refs[2:])
     outs, refs = refs[:2], refs[2:]
-    keys, values = kv if given == 2 else refs[:2]
-    rows, even, odd, place = refs[0 if given == 2 else 2 :][:4]
+    keys, values = refs[:2] if sort else kv
+    rows, even, odd, place = refs[2 if sort else 0 :][:4]
     stat, acc = refs[-2:] if final else outs
     groups = acc.shape[0] // 2
     for group in range(groups):
         for job in range(2):
             for h in range(4):
                 col = (part * 4 + group * 4 + h) * HEAD
-                rows[2 * group + job, h * HALF : (h + 1) * HALF, :] = queries[job][
-                    :, col : col + HEAD
+                rows[2 * group + job, h * HALF : (h + 1) * HALF, :] = queries[
+                    job * HALF : (job + 1) * HALF, col : col + HEAD
                 ]
     for h in range(4):
         place[0:1, h * HALF : (h + 1) * HALF] = lax.broadcasted_iota(jnp.int32, (1, HALF), 1) + 1
@@ -365,9 +365,9 @@
     else:
         stat[...] = states_in[0][2 * part : 2 * part + 2 * groups]
         acc[...] = states_in[1][2 * part : 2 * part + 2 * groups]
-    for i in range(TILES if given == 5 else 0):
+    tiles = [array.at[i] for array in kv for i in range(array.shape[0])] if sort else []
+    for i, tile in enumerate(tiles):
         start = pl.multiple_of(meta[i] * HALF, HALF)
-        tile = kv[i // 2].at[i % 2] if i < 8 else kv[4].at[i - 8]
         keys[pl.ds(start, HALF), :] = tile[:, :HEAD]
         values[pl.ds(start, HALF), :] = tile[:, HEAD:]
 
@@ -434,7 +434,8 @@
 
 def _attend(meta, kv, queries, states=(), groups=1, part=0, spare=0):
     final = bool(states)
-    ordered = [(TILES * HALF, HEAD)] * (2 if len(kv) == 5 else 0)
+    sort = len(kv[0].shape) == 3
+    ordered = [(TILES * HALF, HEAD)] * (2 if sort else 0)
     state_shape = [(2 * groups, 8, LANES), (2 * groups, HEAD, LANES)]
     if final:
         out_shape = [
@@ -446,9 +447,9 @@
     if final:
         out_shape += [jax.ShapeDtypeStruct(shape, jnp.bfloat16) for shape in ordered]
         ordered = []
-    near = [*kv, *queries, *states]
+    near = [*kv, queries, *states]
     out = pl.pallas_call(
-        functools.partial(_attend_body, len(kv), not states, final, part),
+        functools.partial(_attend_body, len(kv), sort, not states, final, part),
         out_shape=out_shape,
         in_specs=[SMEM] + [VMEM] * len(near),
         out_specs=[VMEM] * len(out_shape),
@@ -487,7 +488,8 @@
     half = HEAD // 2
     freq = rope_base ** (-2.0 * jnp.arange(half, dtype=jnp.float32) / HEAD)
     phase = positions.astype(jnp.float32)[:, None] * freq[None, :]
-    return jnp.cos(phase), jnp.sin(phase)
+    cosine, sine = jnp.cos(phase), jnp.sin(phase)
+    return jnp.concatenate([cosine, cosine], axis=1), jnp.concatenate([-sine, sine], axis=1)
 
 
 def _after(value, *earlier):
@@ -508,9 +510,10 @@
     def tile_seq(dy, dx, dc):
         return ((y + dy) % 4 * 2 + (x_hi ^ dx)) * 2 + (core ^ dc)
 
-    order = jnp.stack(
-        [tile_seq(dy, dx, dc) for dc in (0, 1) for dy in (0, -1, 1, 2) for dx in (0, 1)]
-    ).astype(jnp.int32)
+    def places(dc):
+        seqs = [tile_seq(dy, dx, dc) for dx in (0, 1) for dy in (0, -1, 1, 2)]
+        return jnp.stack([p for s in seqs for p in (s, 15 - s)]).astype(jnp.int32)
+
     far_lo = 1 - x_lo
 
     def ints(*values):
@@ -526,60 +529,50 @@
     up, down = _send(early, z_up), _send(early, z_down)
     late = _send(late, mirror_cross)
     row = jnp.arange(HALF, dtype=jnp.int32)
-    rope = _angles(seq * (2 * HALF) + row)
-    late_rope = _angles((31 - 2 * seq) * HALF + row)
-    up, *ropes = lax.optimization_barrier((up, *rope, *late_rope))
-    rope, late_rope = ropes[:2], ropes[2:]
-    whole = [(0, 0, HALF)], [(1, 0, HALF)], [(2, 0, HALF)], [(3, 0, HALF)]
+    rope = _angles(jnp.concatenate([seq * ROWS + row, (31 - 2 * seq) * HALF + row]))
+    up, *rope = lax.optimization_barrier((up, *rope))
 
     to_up, to_down = _stitch(
-        [(HALF + PART, DEPTH)] * 2,
-        [(0, 0, PART, 0, 0), (2, 0, HALF, 0, PART), (1, PART, PART, 1, 0), (2, 0, HALF, 1, PART)],
+        [(HALF, DEPTH)] * 2,
+        [
+            (0, 0, PART, 0, 0),
+            (2, 0, PART, 0, PART),
+            (1, PART, PART, 1, 0),
+            (2, 0, PART, 1, PART),
+        ],
         up,
         down,
         side,
     )
     from_down, from_up = _send(to_up, z_up), _send(to_down, z_down)
     late_side = _send(late, x_near)
+
+    across, both = _stitch(
+        [(ROWS, DEPTH)] * 2,
+        [
+            (2, 0, PART, 0, 0),
+            (3, 0, PART, 0, PART),
+            (0, PART, PART, 0, HALF),
+            (1, PART, PART, 0, HALF + PART),
+            (4, 0, HALF, 1, 0),
+            (5, 0, HALF, 1, HALF),
+        ],
+        up,
+        down,
+        from_down,
+        from_up,
+        late,
+        late_side,
+    )
+    late_up, late_down = _send(both, z_up), _send(both, z_down)
+    got = _send(across, x_near)
     acc = _project(
-        ints(feature(x_lo, 0), feature(x_lo, -1), feature(x_lo, 1), feature(far_lo, 0)),
-        [early, up, down, side],
-        whole,
+        ints(feature(x_lo, 0), feature(far_lo, 0)),
+        [_after(early, across), late_side, side, late],
+        ([(0, 0, HALF), (1, 0, HALF)], [(2, 0, HALF), (3, 0, HALF)]),
         weights,
     )
-    (far,) = _stitch(
-        [(HALF, DEPTH)],
-        [(0, 0, PART, 0, 0), (1, 0, PART, 0, PART)],
-        _after(from_down, acc),
-        from_up,
-    )
-    last = _send(far, x_near)
-    both = _after(_stitch(
-        [(2 * HALF, DEPTH)], [(0, 0, HALF, 0, 0), (1, 0, HALF, 0, HALF)], late, late_side
-    )[0], far)
-    up, down = _send(both, z_up), _send(both, z_down)
-    acc = _project(
-        ints(feature(x_lo, 2), feature(far_lo, -1), feature(far_lo, 1)),
-        [far, from_down, from_up],
-        ([(0, 0, HALF)], [(1, PART, HALF)], [(2, PART, HALF)]),
-        weights,
-        acc,
-    )
-    late_acc = _project(
-        ints(feature(far_lo, 0), feature(x_lo, 0)),
-        [_after(late, acc), late_side],
-        whole[:2],
-        weights,
-    )
-    which = ints(feature(far_lo, 2))
-    last = _after(last, late_acc)
-    early_kv = _last_kv(which, [last], whole[:1], w_key, w_value, acc, k_bias, v_bias, *rope)
-    early_q = _last_q(
-        which, [_after(last, early_kv)], whole[:1], w_query, acc, q_bias, *rope
-    )
-    pair = _stack_pair(_after(early_kv, early_q), _send(early_kv, x_far))
-
-    early_pairs = [pair, _send(pair, y_up), _send(pair, y_down), _send(pair, y_far)]
+
     to_up, to_down = _stitch(
         [(HALF, DEPTH)] * 2,
         [
@@ -588,47 +581,46 @@
             (1, PART, PART, 1, 0),
             (1, HALF + PART, PART, 1, PART),
         ],
-        _after(up, pair),
-        down,
-    )
-    from_down, from_up = _send(to_up, z_up), _send(to_down, z_down)
+        _after(late_up, acc),
+        late_down,
+    )
+    late_from_down, late_from_up = _send(to_up, z_up), _send(to_down, z_down)
     acc = _project(
-        ints(feature(far_lo, -1), feature(x_lo, -1), feature(far_lo, 1), feature(x_lo, 1)),
-        [_after(up, to_up), down],
-        ([(0, 0, HALF)], [(0, HALF, HALF)], [(1, 0, HALF)], [(1, HALF, HALF)]),
+        ints(feature(x_lo, -1), feature(x_lo, 1), feature(far_lo, -1), feature(far_lo, 1)),
+        [_after(up, to_up), down, from_down, from_up, got, late_up, late_down],
+        (
+            [(0, 0, HALF), (5, HALF, HALF)],
+            [(1, 0, HALF), (6, HALF, HALF)],
+            [(2, PART, PART), (4, HALF, PART), (5, 0, HALF)],
+            [(3, PART, PART), (4, HALF + PART, PART), (6, 0, HALF)],
+        ),
         weights,
-        late_acc,
+        acc,
     )
     which = ints(feature(far_lo, 2), feature(x_lo, 2))
-    pieces = ([(0, 0, PART), (1, 0, PART)], [(0, PART, PART), (1, PART, PART)])
-    late_kv = _last_kv(
-        which, [from_down, from_up], pieces, w_key, w_value, acc, k_bias, v_bias, *late_rope
-    )
-    late_q = _last_q(
-        which,
-        [_after(from_down, late_kv), from_up],
-        pieces,
-        w_query,
-        acc,
-        q_bias,
-        *late_rope,
-    )
-
-    early_pairs = [*early_pairs[:3], _after(early_pairs[3], late_kv)]
-    early_keys = [*early_pairs, _send(_stack_pairs(early_pairs), other_core)]
-    pair = _stack_pair(_after(late_kv, late_q), _send(late_kv, x_far))
-    early_meta = jnp.concatenate([order, _blocks(seq, True, 16 - seq, False)])
-    late_meta = jnp.concatenate([15 - order, _blocks(seq, False, 15 - seq, True)])
-    late_pairs = [pair, _send(pair, y_up), _send(pair, y_down), _send(pair, y_far)]
-    queries = (early_q, late_q)
-    states, _ = _attend(early_meta, early_keys, queries, groups=2)
-    late_pairs = [*late_pairs[:3], _after(late_pairs[3], states[0])]
-    late_keys = [*late_pairs, _send(_stack_pairs(late_pairs), other_core)]
+    arrays = [got, from_down, from_up, late_from_down, late_from_up]
+    pieces = (
+        [(0, 0, HALF), (3, 0, PART), (4, 0, PART)],
+        [(1, 0, PART), (2, 0, PART), (3, PART, PART), (4, PART, PART)],
+    )
+    kv = _last_kv(which, arrays, pieces, w_key, w_value, acc, k_bias, v_bias, *rope)
+    far_kv = _send(kv, x_far)
+    near_kv = [kv, _send(kv, y_up), _send(kv, y_down), _send(kv, y_far)]
+    queries = _last_q(which, [_after(got, kv), *arrays[1:]], pieces, w_query, acc, q_bias, *rope)
+    far_kv = _after(far_kv, queries)
+    far_kv = [far_kv, _send(far_kv, y_up), _send(far_kv, y_down), _send(far_kv, y_far)]
+    near_tiles = _stack_tiles(near_kv)
+    far_tiles = _stack_tiles(far_kv)
+    other_kv = [_send(near_tiles, other_core), _send(far_tiles, other_core)]
+
+    meta = jnp.concatenate([places(0), _blocks(seq, True, 15 - seq, True)])
+    other_meta = jnp.concatenate([places(1), _blocks(seq, False, 16 - seq, False)])
+    states, _ = _attend(_after(meta, far_tiles), [near_tiles, far_tiles], queries, groups=2)
     (early_low, late_low), ordered = _attend(
-        late_meta, late_keys, queries, states, part=0, spare=16
+        other_meta, other_kv, queries, states, part=0, spare=16
     )
     back_low = _send(late_low, mirror)
-    (early_high, late_high), _ = _attend(late_meta, ordered, queries, states, part=1)
+    (early_high, late_high), _ = _attend(other_meta, ordered, queries, states, part=1)
     back_high = _send(late_high, mirror)
     return jnp.concatenate(
         [

time: 137 us -> 133 us (0.971)
  Pallas kernels: 65 us -> 49.8 us
  waiting for transfers between devices: 14.3 us -> 28.6 us
    ppermute x24 -> x23, waiting for transfers between devices: 14.3 us -> 28.6 us  [_send(): return lax.ppermute(value, AXES, pairs)]
    pallas_call x4 -> x2, Pallas kernels: 22.3 us -> 13.2 us  [_project(): pl.pallas_call(functools.partial(_proj_body, len(arrays), pieces, acc is...]
    pallas_call x2 -> x1, Pallas kernels: 8.6 us -> 4.7 us  [_last_q(): pl.pallas_call(functools.partial(_last_q_body, len(arrays), pieces), out_...]
    sin x1 -> x0, other arithmetic: 1.45 us -> none  [_angles(): return (jnp.cos(phase), jnp.sin(phase))]
    pallas_call x2 -> x1, Pallas kernels: 4.93 us -> 3.49 us  [_last_kv(): pl.pallas_call(functools.partial(_last_kv_body, len(arrays), pieces), out...]
    unnamed x70 -> x44, local copies, waits for them, and re-layouts: 8.7 us -> 7.51 us
    pallas_call x9 -> x6, Pallas kernels: 8.63 us -> 7.65 us  [_stitch(): pl.pallas_call(body, out_shape=[jax.ShapeDtypeStruct(shape, jnp.bfloat16)...]
    ppermute x24 -> x23, starting transfers between devices: 44.1 us -> 43.5 us  [_send(): return lax.ppermute(value, AXES, pairs)]
  transfers between devices with their start and end apart: 24 -> 23, of which waited for: 5 -> 7; matrix products, arithmetic and copies ran while one was open for 2% -> 1% of each run, Pallas kernels for 40% -> 28%
where the time goes in v2:
time: 133 us; the launch traced here: 132 us
  Pallas kernels  49.8 us (37%)
  starting transfers between devices  43.5 us (33%)
  waiting for transfers between devices  28.6 us (22%)
  local copies, waits for them, and re-layouts  7.76 us (6%)
  other arithmetic  2.31 us (2%)
    ppermute x23, starting transfers between devices, _send(): return lax.ppermute(value, AXES, pairs)  43.5 us
    ppermute x23, waiting for transfers between devices, _send(): return lax.ppermute(value, AXES, pairs)  28.6 us
    pallas_call x3, Pallas kernels, _attend(): pl.pallas_call(functools.partial(_attend_body, len(kv), sort, not states,...  20.7 us
    pallas_call x2, Pallas kernels, _project(): pl.pallas_call(functools.partial(_proj_body, len(arrays), pieces, acc is...  13.2 us
    pallas_call x6, Pallas kernels, _stitch(): pl.pallas_call(body, out_shape=[jax.ShapeDtypeStruct(shape, jnp.bfloat16)...  7.65 us
    unnamed x44, local copies, waits for them, and re-layouts  7.51 us
    pallas_call x1, Pallas kernels, _last_q(): pl.pallas_call(functools.partial(_last_q_body, len(arrays), pieces), out_...  4.7 us
    pallas_call x1, Pallas kernels, _last_kv(): pl.pallas_call(functools.partial(_last_kv_body, len(arrays), pieces), out...  3.49 us
  transfers between devices with their start and end apart: 23, of which 7 were waited for; matrix products, arithmetic and copies ran while one was open for 1% of the time, Pallas kernels for 28%

profile of v2, /device:TPU:1, one launch (start us, length us, event | category | flops | bytes accessed | tf_op | source)
XLA Modules:
  0.0 132.3 jit_solution(5993561798716357264)
XLA Ops:
  0.0 1.1 stitch.6
  1.1 2.1 %collective-permute-start.2 = (bf16[192,1024]{1,0:T(8,128)(2,1)S(1)}, bf16[192,1024]{1,0:T(8,128)(2,1)S(1)}, u32[]{:S(2)}, u32[]{:S(2)}) collective-permute-start(bf16[192,1024]{1,0:T(8,128)(2,1)S(1)} %get-tuple-element.37.refs_0_), channel_id=1, source_target_pairs={{0,4},{1,5},{2,6},{3,7},{4,0},{5,1},{6,2},{7,3},{8,12},{9,13},{10,... | collective-permute-start | bytes 1179656 | tf_op jit(solution)/shard_map/ppermute | solution.py:46
  3.3 3.8 %collective-permute-start.1 = (bf16[192,1024]{1,0:T(8,128)(2,1)S(1)}, bf16[192,1024]{1,0:T(8,128)(2,1)S(1)}, u32[]{:S(2)}, u32[]{:S(2)}) collective-permute-start(bf16[192,1024]{1,0:T(8,128)(2,1)S(1)} %get-tuple-element.37.refs_0_), channel_id=1, source_target_pairs={{0,3},{1,0},{2,1},{3,2},{4,7},{5,4},{6,5},{7,6},{8,11},{9,8},{10,9... | collective-permute-start | bytes 1179656 | tf_op jit(solution)/shard_map/ppermute | solution.py:46
  7.0 5.4 %collective-permute-start.5 = (bf16[192,1024]{1,0:T(8,128)(2,1)S(1)}, bf16[192,1024]{1,0:T(8,128)(2,1)S(1)}, u32[]{:S(2)}, u32[]{:S(2)}) collective-permute-start(bf16[192,1024]{1,0:T(8,128)(2,1)S(1)} %get-tuple-element.34), channel_id=1, source_target_pairs={{0,124},{1,125},{2,126},{3,127},{4,120},{5,121},{6,122},{7,123},{8... | collective-permute-start | bytes 1179656 | tf_op jit(solution)/shard_map/ppermute | solution.py:46
  13.5 4.1 %collective-permute-done.refs_0_ = bf16[192,1024]{1,0:T(8,128)(2,1)S(1)} collective-permute-done((bf16[192,1024]{1,0:T(8,128)(2,1)S(1)}, bf16[192,1024]{1,0:T(8,128)(2,1)S(1)}, u32[]{:S(2)}, u32[]{:S(2)}) %collective-permute-start) | collective-permute-done | bytes 393248 | tf_op jit(solution)/shard_map/ppermute | solution.py:46
  19.2 1.3 stitch.7
  20.6 1.6 %collective-permute-done.5.refs_4_.refs_3_ = bf16[192,1024]{1,0:T(8,128)(2,1)S(1)} collective-permute-done((bf16[192,1024]{1,0:T(8,128)(2,1)S(1)}, bf16[192,1024]{1,0:T(8,128)(2,1)S(1)}, u32[]{:S(2)}, u32[]{:S(2)}) %collective-permute-start.5) | collective-permute-done | bytes 393248 | tf_op jit(solution)/shard_map/ppermute | solution.py:46
  22.2 3.0 %collective-permute-start.4 = (bf16[192,1024]{1,0:T(8,128)(2,1)S(1)}, bf16[192,1024]{1,0:T(8,128)(2,1)S(1)}, u32[]{:S(2)}, u32[]{:S(2)}) collective-permute-start(bf16[192,1024]{1,0:T(8,128)(2,1)S(1)} %get-tuple-element.33), channel_id=1, source_target_pairs={{0,3},{1,0},{2,1},{3,2},{4,7},{5,4},{6,5},{7,6},{8,11},{9,8},{10,9... | collective-permute-start | bytes 1179656 | tf_op jit(solution)/shard_map/ppermute | solution.py:46
  25.1 7.0 %collective-permute-done.6.refs_5_.refs_1_ = bf16[192,1024]{1,0:T(8,128)(2,1)S(1)} collective-permute-done((bf16[192,1024]{1,0:T(8,128)(2,1)S(1)}, bf16[192,1024]{1,0:T(8,128)(2,1)S(1)}, u32[]{:S(2)}, u32[]{:S(2)}) %collective-permute-start.6) | collective-permute-done | bytes 393248 | tf_op jit(solution)/shard_map/ppermute | solution.py:46
  33.8 1.5 %stitch.8 = (bf16[384,1024]{1,0:T(8,128)(2,1)S(1)}, bf16[384,1024]{1,0:T(8,128)(2,1)S(1)}) custom-call(bf16[192,1024]{1,0:T(8,128)(2,1)} %copy-done.9, bf16[192,1024]{1,0:T(8,128)(2,1)} %copy-done.8, bf16[192,1024]{1,0:T(8,128)(2,1)} %copy-done.6, bf16[192,1024]{1,0:T(8,128)(2,1)} %copy-done.7, bf16[192,1024]{1,0:T(8,128)(2,1)} %copy-done.12, ...), custom_call_target="tpu_custom_call" | custom-call | tf_op jit(solution)/shard_map/stitch/pallas_call | solution.py:327
  35.4 3.1 %collective-permute-start.9 = (bf16[384,1024]{1,0:T(8,128)(2,1)S(1)}, bf16[384,1024]{1,0:T(8,128)(2,1)}, u32[]{:S(2)}, u32[]{:S(2)}) collective-permute-start(bf16[384,1024]{1,0:T(8,128)(2,1)S(1)} %get-tuple-element.36), channel_id=1, source_target_pairs={{0,3},{1,0},{2,1},{3,2},{4,7},{5,4},{6,5},{7,6},{8,11},{9,8},{10,9... | collective-permute-start | bytes 2359304 | tf_op jit(solution)/shard_map/ppermute | solution.py:46
  38.5 1.5 %collective-permute-start.7 = (bf16[384,1024]{1,0:T(8,128)(2,1)S(1)}, bf16[384,1024]{1,0:T(8,128)(2,1)S(1)}, u32[]{:S(2)}, u32[]{:S(2)}) collective-permute-start(bf16[384,1024]{1,0:T(8,128)(2,1)S(1)} %get-tuple-element.35), channel_id=1, source_target_pairs={{0,4},{1,5},{2,6},{3,7},{4,0},{5,1},{6,2},{7,3},{8,12},{9,13},{10,... | collective-permute-start | bytes 2359304 | tf_op jit(solution)/shard_map/ppermute | solution.py:46
  40.1 5.2 %project.2.refs_10_ = f32[384,1280]{1,0:T(8,128)S(1)} custom-call(s32[2]{0:T(128)S(1)} %pad_add_fusion.1.slices, bf16[192,1024]{1,0:T(8,128)(2,1)} %copy-done.1, bf16[192,1024]{1,0:T(8,128)(2,1)} %copy-done.13, bf16[192,1024]{1,0:T(8,128)(2,1)} %copy-done.14, bf16[192,1024]{1,0:T(8,128)(2,1)} %copy-done.12, bf16[8192,1024]{1,0:T(8,128)(2,1)} %refs_5_.5, ...), custom_call_target="tpu_custom_call" | custom-call | flops 2013265920 | bytes 5242880 | tf_op jit(solution)/shard_map/project/pallas_call | solution.py:173
  45.4 9.2 %collective-permute-done.8.refs_0_.refs_5_ = bf16[384,1024]{1,0:T(8,128)(2,1)} collective-permute-done((bf16[384,1024]{1,0:T(8,128)(2,1)S(1)}, bf16[384,1024]{1,0:T(8,128)(2,1)}, u32[]{:S(2)}, u32[]{:S(2)}) %collective-permute-start.8) | collective-permute-done | bytes 786464 | tf_op jit(solution)/shard_map/ppermute | solution.py:46
  54.6 1.3 stitch.9
  55.8 2.5 %collective-permute-start.11 = (bf16[192,1024]{1,0:T(8,128)(2,1)S(1)}, bf16[192,1024]{1,0:T(8,128)(2,1)S(1)}, u32[]{:S(2)}, u32[]{:S(2)}) collective-permute-start(bf16[192,1024]{1,0:T(8,128)(2,1)S(1)} %get-tuple-element.40), channel_id=1, source_target_pairs={{0,3},{1,0},{2,1},{3,2},{4,7},{5,4},{6,5},{7,6},{8,11},{9,8},{10,9... | collective-permute-start | bytes 1179656 | tf_op jit(solution)/shard_map/ppermute | solution.py:46
  59.3 8.0 %project.3.refs_7_.refs_6_ = f32[384,1280]{1,0:T(8,128)S(1)} custom-call(s32[4]{0:T(128)S(1)} %pad_add_fusion.2.slices, bf16[192,1024]{1,0:T(8,128)(2,1)} %copy-done.9, bf16[192,1024]{1,0:T(8,128)(2,1)} %copy-done.8, bf16[192,1024]{1,0:T(8,128)(2,1)} %copy-done.6, bf16[192,1024]{1,0:T(8,128)(2,1)} %copy-done.7, bf16[384,1024]{1,0:T(8,128)(2,1)} %copy-done.5, ...), custom_call_target="tpu_custom_call" | custom-call | flops 4026531840 | bytes 10485760 | tf_op jit(solution)/shard_map/project/pallas_call | solution.py:173
  68.2 3.5 %last_kv.1.refs_0_ = bf16[2,192,256]{2,1,0:T(8,128)(2,1)S(1)} custom-call(s32[2]{0:T(128)S(1)} %pad_add_fusion.slices, bf16[384,1024]{1,0:T(8,128)(2,1)} %copy-done.5, bf16[192,1024]{1,0:T(8,128)(2,1)} %copy-done.6, bf16[192,1024]{1,0:T(8,128)(2,1)} %copy-done.7, bf16[192,1024]{1,0:T(8,128)(2,1)} %copy-done.11, bf16[192,1024]{1,0:T(8,128)(2,1)} %copy-done.10, ...), custom_call_target="tpu_custom_call" | custom-call | flops 402653184 | bytes 1048576 | tf_op jit(solution)/shard_map/last_kv/pallas_call | solution.py:230
  71.8 1.3 collective-permute-start.14
  74.7 4.7 %last_q.1.refs_2_ = bf16[384,1024]{1,0:T(8,128)(2,1)S(1)} custom-call(s32[2]{0:T(128)S(1)} %pad_add_fusion.slices, bf16[384,1024]{1,0:T(8,128)(2,1)} %copy-done.5, bf16[192,1024]{1,0:T(8,128)(2,1)} %copy-done.6, bf16[192,1024]{1,0:T(8,128)(2,1)} %copy-done.7, bf16[192,1024]{1,0:T(8,128)(2,1)} %copy-done.11, bf16[192,1024]{1,0:T(8,128)(2,1)} %copy-done.10, ...), custom_call_target="tpu_custom_call" | custom-call | flops 1610612736 | bytes 4194304 | tf_op jit(solution)/shard_map/last_q/pallas_call | solution.py:287
  79.5 1.9 %collective-permute-start.19 = (bf16[2,192,256]{2,1,0:T(8,128)(2,1)S(1)}, bf16[2,192,256]{2,1,0:T(8,128)(2,1)S(1)}, u32[]{:S(2)}, u32[]{:S(2)}) collective-permute-start(bf16[2,192,256]{2,1,0:T(8,128)(2,1)S(1)} %collective-permute-done.16.refs_0_), channel_id=1, source_target_pairs={{0,64},{1,65},{2,66},{3,67},{4,68},{5,69},{6,70},{7,71},{8,72},{9,... | collective-permute-start | bytes 589832 | tf_op jit(solution)/shard_map/ppermute | solution.py:46
  81.4 2.0 %collective-permute-start.18 = (bf16[2,192,256]{2,1,0:T(8,128)(2,1)S(1)}, bf16[2,192,256]{2,1,0:T(8,128)(2,1)S(1)}, u32[]{:S(2)}, u32[]{:S(2)}) collective-permute-start(bf16[2,192,256]{2,1,0:T(8,128)(2,1)S(1)} %collective-permute-done.16.refs_0_), channel_id=1, source_target_pairs={{0,96},{1,97},{2,98},{3,99},{4,100},{5,101},{6,102},{7,103},{8,104... | collective-permute-start | bytes 589832 | tf_op jit(solution)/shard_map/ppermute | solution.py:46
  84.8 1.3 stitch.10.refs_0_
  86.1 5.9 %collective-permute-start.15 = (bf16[8,192,256]{2,1,0:T(8,128)(2,1)S(1)}, bf16[8,192,256]{2,1,0:T(8,128)(2,1)S(1)}, u32[]{:S(2)}, u32[]{:S(2)}) collective-permute-start(bf16[8,192,256]{2,1,0:T(8,128)(2,1)S(1)} %stitch.10.refs_0_), channel_id=1, source_target_pairs={{0,8},{1,9},{2,10},{3,11},{4,12},{5,13},{6,14},{7,15},{8,0},{9,1},... | collective-permute-start | bytes 2359304 | tf_op jit(solution)/shard_map/ppermute | solution.py:46
  93.4 1.3 stitch.11.refs_1_
  94.7 3.4 %collective-permute-start.20 = (bf16[8,192,256]{2,1,0:T(8,128)(2,1)S(1)}, bf16[8,192,256]{2,1,0:T(8,128)(2,1)}, u32[]{:S(2)}, u32[]{:S(2)}) collective-permute-start(bf16[8,192,256]{2,1,0:T(8,128)(2,1)S(1)} %stitch.11.refs_1_), channel_id=1, source_target_pairs={{0,8},{1,9},{2,10},{3,11},{4,12},{5,13},{6,14},{7,15},{8,0},{9,1},... | collective-permute-start | bytes 2359304 | tf_op jit(solution)/shard_map/ppermute | solution.py:46
  98.4 9.5 %attend.3 = (f32[4,8,768]{2,1,0:T(8,128)S(1)}, f32[4,128,768]{2,1,0:T(8,128)S(1)}) custom-call(s32[36]{0:T(128)S(1)} %concatenate.32.meta, bf16[8,192,256]{2,1,0:T(8,128)(2,1)S(1)} %stitch.10.refs_0_, bf16[8,192,256]{2,1,0:T(8,128)(2,1)S(1)} %stitch.11.refs_1_, bf16[384,1024]{1,0:T(8,128)(2,1)S(1)} %last_q.1.refs_2_), custom_call_target="tpu_custom_call" | custom-call | flops 3019898880 | bytes 4194304 | tf_op jit(solution)/shard_map/attend/pallas_call | solution.py:451
  107.9 6.0 %attend.4 = (bf16[192,512]{1,0:T(8,128)(2,1)S(1)}, bf16[208,512]{1,0:T(8,128)(2,1)S(1)}, bf16[3072,128]{1,0:T(8,128)(2,1)S(1)}, bf16[3072,128]{1,0:T(8,128)(2,1)S(1)}) custom-call(s32[36]{0:T(128)S(1)} %concatenate.28.meta, bf16[8,192,256]{2,1,0:T(8,128)(2,1)S(1)} %collective-permute-done.15.refs_0_, bf16[8,192,256]{2,1,0:T(8,128)(2,1)} %collective-permute-done.20.refs_1_, ...), custom_call_target="tpu_custom_call" | custom-call | flops 1509949440 | bytes 4194304 | tf_op jit(solution)/shard_map/attend/pallas_call | solution.py:451
  114.0 1.8 %collective-permute-start.21 = (bf16[208,512]{1,0:T(8,128)(2,1)S(1)}, bf16[208,512]{1,0:T(8,128)(2,1)S(1)}, u32[]{:S(2)}, u32[]{:S(2)}) collective-permute-start(bf16[208,512]{1,0:T(8,128)(2,1)S(1)} %get-tuple-element.53), channel_id=1, source_target_pairs={{0,120},{1,121},{2,122},{3,123},{4,124},{5,125},{6,126},{7,127},{8... | collective-permute-start | bytes 638984 | tf_op jit(solution)/shard_map/ppermute | solution.py:46
  115.7 5.2 %attend.5 = (bf16[192,512]{1,0:T(8,128)(2,1)S(1)}, bf16[192,512]{1,0:T(8,128)(2,1)S(1)}) custom-call(s32[36]{0:T(128)S(1)} %concatenate.28.meta, bf16[3072,128]{1,0:T(8,128)(2,1)S(1)} %get-tuple-element.50.refs_0_, bf16[3072,128]{1,0:T(8,128)(2,1)S(1)} %get-tuple-element.51.refs_1_, bf16[384,1024]{1,0:T(8,128)(2,1)S(1)} %last_q.1.refs_2_, ...), custom_call_target="tpu_custom_call" | custom-call | flops 1509949440 | bytes 4194304 | tf_op jit(solution)/shard_map/attend/pallas_call | solution.py:451
  120.9 4.0 %collective-permute-start.22 = (bf16[192,512]{1,0:T(8,128)(2,1)S(1)}, bf16[192,512]{1,0:T(8,128)(2,1)S(1)}, u32[]{:S(2)}, u32[]{:S(2)}) collective-permute-start(bf16[192,512]{1,0:T(8,128)(2,1)S(1)} %get-tuple-element.54), channel_id=1, source_target_pairs={{0,120},{1,121},{2,122},{3,123},{4,124},{5,125},{6,126},{7,127},{8... | collective-permute-start | bytes 589832 | tf_op jit(solution)/shard_map/ppermute | solution.py:46
  125.1 6.3 %collective-permute-done.22 = bf16[192,512]{1,0:T(8,128)(2,1)S(1)} collective-permute-done((bf16[192,512]{1,0:T(8,128)(2,1)S(1)}, bf16[192,512]{1,0:T(8,128)(2,1)S(1)}, u32[]{:S(2)}, u32[]{:S(2)}) %collective-permute-start.22) | collective-permute-done | bytes 196640 | tf_op jit(solution)/shard_map/ppermute | solution.py:46
  (84 shorter events, 12.4 us)
Async XLA Ops:
  1.1 34.2 %copy-start.1 = (bf16[192,1024]{1,0:T(8,128)(2,1)}, bf16[192,1024]{1,0:T(8,128)(2,1)S(1)}, u32[]{:S(2)}) copy-start(bf16[192,1024]{1,0:T(8,128)(2,1)S(1)} %get-tuple-element.37.refs_0_) | copy-start | bytes 1179652
  1.1 16.5 %collective-permute-start.2 = (bf16[192,1024]{1,0:T(8,128)(2,1)S(1)}, bf16[192,1024]{1,0:T(8,128)(2,1)S(1)}, u32[]{:S(2)}, u32[]{:S(2)}) collective-permute-start(bf16[192,1024]{1,0:T(8,128)(2,1)S(1)} %get-tuple-element.37.refs_0_), channel_id=1, source_target_pairs={{0,4},{1,5},{2,6},{3,7},{4,0},{5,1},{6,2},{7,3},{8,12},{9,13},{10,... | collective-permute-start | bytes 1179656 | tf_op jit(solution)/shard_map/ppermute | solution.py:46
  3.3 14.3 %collective-permute-start.1 = (bf16[192,1024]{1,0:T(8,128)(2,1)S(1)}, bf16[192,1024]{1,0:T(8,128)(2,1)S(1)}, u32[]{:S(2)}, u32[]{:S(2)}) collective-permute-start(bf16[192,1024]{1,0:T(8,128)(2,1)S(1)} %get-tuple-element.37.refs_0_), channel_id=1, source_target_pairs={{0,3},{1,0},{2,1},{3,2},{4,7},{5,4},{6,5},{7,6},{8,11},{9,8},{10,9... | collective-permute-start | bytes 1179656 | tf_op jit(solution)/shard_map/ppermute | solution.py:46
  7.0 10.6 %collective-permute-start = (bf16[192,1024]{1,0:T(8,128)(2,1)S(1)}, bf16[192,1024]{1,0:T(8,128)(2,1)S(1)}, u32[]{:S(2)}, u32[]{:S(2)}) collective-permute-start(bf16[192,1024]{1,0:T(8,128)(2,1)S(1)} %get-tuple-element.37.refs_0_), channel_id=1, source_target_pairs={{0,1},{1,2},{2,3},{3,0},{4,5},{5,6},{6,7},{7,4},{8,9},{9,10},{10,1... | collective-permute-start | bytes 1179656 | tf_op jit(solution)/shard_map/ppermute | solution.py:46
  7.0 15.1 %collective-permute-start.5 = (bf16[192,1024]{1,0:T(8,128)(2,1)S(1)}, bf16[192,1024]{1,0:T(8,128)(2,1)S(1)}, u32[]{:S(2)}, u32[]{:S(2)}) collective-permute-start(bf16[192,1024]{1,0:T(8,128)(2,1)S(1)} %get-tuple-element.34), channel_id=1, source_target_pairs={{0,124},{1,125},{2,126},{3,127},{4,120},{5,121},{6,122},{7,123},{8... | collective-permute-start | bytes 1179656 | tf_op jit(solution)/shard_map/ppermute | solution.py:46
  20.5 11.7 %collective-permute-start.3 = (bf16[192,1024]{1,0:T(8,128)(2,1)S(1)}, bf16[192,1024]{1,0:T(8,128)(2,1)S(1)}, u32[]{:S(2)}, u32[]{:S(2)}) collective-permute-start(bf16[192,1024]{1,0:T(8,128)(2,1)S(1)} %get-tuple-element.32), channel_id=1, source_target_pairs={{0,1},{1,2},{2,3},{3,0},{4,5},{5,6},{6,7},{7,4},{8,9},{9,10},{10,1... | collective-permute-start | bytes 1179656 | tf_op jit(solution)/shard_map/ppermute | solution.py:46
  22.2 10.0 %copy-start.12 = (bf16[192,1024]{1,0:T(8,128)(2,1)}, bf16[192,1024]{1,0:T(8,128)(2,1)S(1)}, u32[]{:S(2)}) copy-start(bf16[192,1024]{1,0:T(8,128)(2,1)S(1)} %collective-permute-done.5.refs_4_.refs_3_) | copy-start | bytes 1179652
  22.2 10.0 %collective-permute-start.6 = (bf16[192,1024]{1,0:T(8,128)(2,1)S(1)}, bf16[192,1024]{1,0:T(8,128)(2,1)S(1)}, u32[]{:S(2)}, u32[]{:S(2)}) collective-permute-start(bf16[192,1024]{1,0:T(8,128)(2,1)S(1)} %collective-permute-done.5.refs_4_.refs_3_), channel_id=1, source_target_pairs={{0,4},{1,5},{2,6},{3,7},{4,0},{5,1},{6,2},{7,3},{8,12},{9,13},{10,... | collective-permute-start | bytes 1179656 | tf_op jit(solution)/shard_map/ppermute | solution.py:46
  22.2 10.3 %collective-permute-start.4 = (bf16[192,1024]{1,0:T(8,128)(2,1)S(1)}, bf16[192,1024]{1,0:T(8,128)(2,1)S(1)}, u32[]{:S(2)}, u32[]{:S(2)}) collective-permute-start(bf16[192,1024]{1,0:T(8,128)(2,1)S(1)} %get-tuple-element.33), channel_id=1, source_target_pairs={{0,3},{1,0},{2,1},{3,2},{4,7},{5,4},{6,5},{7,6},{8,11},{9,8},{10,9... | collective-permute-start | bytes 1179656 | tf_op jit(solution)/shard_map/ppermute | solution.py:46
  32.2 0.9 copy-start.6
  35.3 19.2 %collective-permute-start.8 = (bf16[384,1024]{1,0:T(8,128)(2,1)S(1)}, bf16[384,1024]{1,0:T(8,128)(2,1)}, u32[]{:S(2)}, u32[]{:S(2)}) collective-permute-start(bf16[384,1024]{1,0:T(8,128)(2,1)S(1)} %get-tuple-element.36), channel_id=1, source_target_pairs={{0,1},{1,2},{2,3},{3,0},{4,5},{5,6},{6,7},{7,4},{8,9},{9,10},{10,1... | collective-permute-start | bytes 2359304 | tf_op jit(solution)/shard_map/ppermute | solution.py:46
  35.4 19.1 %collective-permute-start.9 = (bf16[384,1024]{1,0:T(8,128)(2,1)S(1)}, bf16[384,1024]{1,0:T(8,128)(2,1)}, u32[]{:S(2)}, u32[]{:S(2)}) collective-permute-start(bf16[384,1024]{1,0:T(8,128)(2,1)S(1)} %get-tuple-element.36), channel_id=1, source_target_pairs={{0,3},{1,0},{2,1},{3,2},{4,7},{5,4},{6,5},{7,6},{8,11},{9,8},{10,9... | collective-permute-start | bytes 2359304 | tf_op jit(solution)/shard_map/ppermute | solution.py:46
  38.5 19.9 %collective-permute-start.7 = (bf16[384,1024]{1,0:T(8,128)(2,1)S(1)}, bf16[384,1024]{1,0:T(8,128)(2,1)S(1)}, u32[]{:S(2)}, u32[]{:S(2)}) collective-permute-start(bf16[384,1024]{1,0:T(8,128)(2,1)S(1)} %get-tuple-element.35), channel_id=1, source_target_pairs={{0,4},{1,5},{2,6},{3,7},{4,0},{5,1},{6,2},{7,3},{8,12},{9,13},{10,... | collective-permute-start | bytes 2359304 | tf_op jit(solution)/shard_map/ppermute | solution.py:46
  55.8 11.5 %collective-permute-start.11 = (bf16[192,1024]{1,0:T(8,128)(2,1)S(1)}, bf16[192,1024]{1,0:T(8,128)(2,1)S(1)}, u32[]{:S(2)}, u32[]{:S(2)}) collective-permute-start(bf16[192,1024]{1,0:T(8,128)(2,1)S(1)} %get-tuple-element.40), channel_id=1, source_target_pairs={{0,3},{1,0},{2,1},{3,2},{4,7},{5,4},{6,5},{7,6},{8,11},{9,8},{10,9... | collective-permute-start | bytes 1179656 | tf_op jit(solution)/shard_map/ppermute | solution.py:46
  58.4 9.0 %collective-permute-start.10 = (bf16[192,1024]{1,0:T(8,128)(2,1)S(1)}, bf16[192,1024]{1,0:T(8,128)(2,1)S(1)}, u32[]{:S(2)}, u32[]{:S(2)}) collective-permute-start(bf16[192,1024]{1,0:T(8,128)(2,1)S(1)} %get-tuple-element.39), channel_id=1, source_target_pairs={{0,1},{1,2},{2,3},{3,0},{4,5},{5,6},{6,7},{7,4},{8,9},{9,10},{10,1... | collective-permute-start | bytes 1179656 | tf_op jit(solution)/shard_map/ppermute | solution.py:46
  58.4 9.8 %copy-start.3 = (f32[128]{0:T(128)S(1)}, f32[128]{0:T(128)}, u32[]{:S(2)}) copy-start(f32[128]{0:T(128)} %param.12) | copy-start | bytes 1540
  58.4 9.8 %copy-start.4 = (f32[128]{0:T(128)S(1)}, f32[128]{0:T(128)}, u32[]{:S(2)}) copy-start(f32[128]{0:T(128)} %param.13) | copy-start | bytes 1540
  58.4 0.9 copy-start.5
  68.2 6.5 %copy-start.2 = (f32[1024]{0:T(1024)S(1)}, f32[1024]{0:T(1024)}, u32[]{:S(2)}) copy-start(f32[1024]{0:T(1024)} %param.11) | copy-start | bytes 12292
  71.7 7.7 %copy-start = (bf16[2,192,256]{2,1,0:T(8,128)(2,1)}, bf16[2,192,256]{2,1,0:T(8,128)(2,1)S(1)}, u32[]{:S(2)}) copy-start(bf16[2,192,256]{2,1,0:T(8,128)(2,1)S(1)} %last_kv.1.refs_0_) | copy-start | bytes 589828
  71.7 7.7 %collective-permute-start.16 = (bf16[2,192,256]{2,1,0:T(8,128)(2,1)S(1)}, bf16[2,192,256]{2,1,0:T(8,128)(2,1)S(1)}, u32[]{:S(2)}, u32[]{:S(2)}) collective-permute-start(bf16[2,192,256]{2,1,0:T(8,128)(2,1)S(1)} %last_kv.1.refs_0_), channel_id=1, source_target_pairs={{0,16},{1,17},{2,18},{3,19},{4,20},{5,21},{6,22},{7,23},{8,24},{9,... | collective-permute-start | bytes 589832 | tf_op jit(solution)/shard_map/ppermute | solution.py:46
  71.8 11.6 %collective-permute-start.14 = (bf16[2,192,256]{2,1,0:T(8,128)(2,1)S(1)}, bf16[2,192,256]{2,1,0:T(8,128)(2,1)S(1)}, u32[]{:S(2)}, u32[]{:S(2)}) collective-permute-start(bf16[2,192,256]{2,1,0:T(8,128)(2,1)S(1)} %last_kv.1.refs_0_), channel_id=1, source_target_pairs={{0,64},{1,65},{2,66},{3,67},{4,68},{5,69},{6,70},{7,71},{8,72},{9,... | collective-permute-start | bytes 589832 | tf_op jit(solution)/shard_map/ppermute | solution.py:46
  73.1 10.3 %collective-permute-start.13 = (bf16[2,192,256]{2,1,0:T(8,128)(2,1)S(1)}, bf16[2,192,256]{2,1,0:T(8,128)(2,1)S(1)}, u32[]{:S(2)}, u32[]{:S(2)}) collective-permute-start(bf16[2,192,256]{2,1,0:T(8,128)(2,1)S(1)} %last_kv.1.refs_0_), channel_id=1, source_target_pairs={{0,96},{1,97},{2,98},{3,99},{4,100},{5,101},{6,102},{7,103},{8,104... | collective-permute-start | bytes 589832 | tf_op jit(solution)/shard_map/ppermute | solution.py:46
  74.1 9.3 %collective-permute-start.12 = (bf16[2,192,256]{2,1,0:T(8,128)(2,1)S(1)}, bf16[2,192,256]{2,1,0:T(8,128)(2,1)S(1)}, u32[]{:S(2)}, u32[]{:S(2)}) collective-permute-start(bf16[2,192,256]{2,1,0:T(8,128)(2,1)S(1)} %last_kv.1.refs_0_), channel_id=1, source_target_pairs={{0,32},{1,33},{2,34},{3,35},{4,36},{5,37},{6,38},{7,39},{8,40},{9,... | collective-permute-start | bytes 589832 | tf_op jit(solution)/shard_map/ppermute | solution.py:46
  79.5 12.6 %copy-start.15 = (bf16[2,192,256]{2,1,0:T(8,128)(2,1)}, bf16[2,192,256]{2,1,0:T(8,128)(2,1)S(1)}, u32[]{:S(2)}) copy-start(bf16[2,192,256]{2,1,0:T(8,128)(2,1)S(1)} %collective-permute-done.16.refs_0_) | copy-start | bytes 589828
  79.5 12.5 %collective-permute-start.19 = (bf16[2,192,256]{2,1,0:T(8,128)(2,1)S(1)}, bf16[2,192,256]{2,1,0:T(8,128)(2,1)S(1)}, u32[]{:S(2)}, u32[]{:S(2)}) collective-permute-start(bf16[2,192,256]{2,1,0:T(8,128)(2,1)S(1)} %collective-permute-done.16.refs_0_), channel_id=1, source_target_pairs={{0,64},{1,65},{2,66},{3,67},{4,68},{5,69},{6,70},{7,71},{8,72},{9,... | collective-permute-start | bytes 589832 | tf_op jit(solution)/shard_map/ppermute | solution.py:46
  81.4 10.7 %collective-permute-start.18 = (bf16[2,192,256]{2,1,0:T(8,128)(2,1)S(1)}, bf16[2,192,256]{2,1,0:T(8,128)(2,1)S(1)}, u32[]{:S(2)}, u32[]{:S(2)}) collective-permute-start(bf16[2,192,256]{2,1,0:T(8,128)(2,1)S(1)} %collective-permute-done.16.refs_0_), channel_id=1, source_target_pairs={{0,96},{1,97},{2,98},{3,99},{4,100},{5,101},{6,102},{7,103},{8,104... | collective-permute-start | bytes 589832 | tf_op jit(solution)/shard_map/ppermute | solution.py:46
  83.4 8.6 %collective-permute-start.17 = (bf16[2,192,256]{2,1,0:T(8,128)(2,1)S(1)}, bf16[2,192,256]{2,1,0:T(8,128)(2,1)S(1)}, u32[]{:S(2)}, u32[]{:S(2)}) collective-permute-start(bf16[2,192,256]{2,1,0:T(8,128)(2,1)S(1)} %collective-permute-done.16.refs_0_), channel_id=1, source_target_pairs={{0,32},{1,33},{2,34},{3,35},{4,36},{5,37},{6,38},{7,39},{8,40},{9,... | collective-permute-start | bytes 589832 | tf_op jit(solution)/shard_map/ppermute | solution.py:46
  86.1 21.8 %collective-permute-start.15 = (bf16[8,192,256]{2,1,0:T(8,128)(2,1)S(1)}, bf16[8,192,256]{2,1,0:T(8,128)(2,1)S(1)}, u32[]{:S(2)}, u32[]{:S(2)}) collective-permute-start(bf16[8,192,256]{2,1,0:T(8,128)(2,1)S(1)} %stitch.10.refs_0_), channel_id=1, source_target_pairs={{0,8},{1,9},{2,10},{3,11},{4,12},{5,13},{6,14},{7,15},{8,0},{9,1},... | collective-permute-start | bytes 2359304 | tf_op jit(solution)/shard_map/ppermute | solution.py:46
  94.7 13.2 %collective-permute-start.20 = (bf16[8,192,256]{2,1,0:T(8,128)(2,1)S(1)}, bf16[8,192,256]{2,1,0:T(8,128)(2,1)}, u32[]{:S(2)}, u32[]{:S(2)}) collective-permute-start(bf16[8,192,256]{2,1,0:T(8,128)(2,1)S(1)} %stitch.11.refs_1_), channel_id=1, source_target_pairs={{0,8},{1,9},{2,10},{3,11},{4,12},{5,13},{6,14},{7,15},{8,0},{9,1},... | collective-permute-start | bytes 2359304 | tf_op jit(solution)/shard_map/ppermute | solution.py:46
  114.0 11.1 %collective-permute-start.21 = (bf16[208,512]{1,0:T(8,128)(2,1)S(1)}, bf16[208,512]{1,0:T(8,128)(2,1)S(1)}, u32[]{:S(2)}, u32[]{:S(2)}) collective-permute-start(bf16[208,512]{1,0:T(8,128)(2,1)S(1)} %get-tuple-element.53), channel_id=1, source_target_pairs={{0,120},{1,121},{2,122},{3,123},{4,124},{5,125},{6,126},{7,127},{8... | collective-permute-start | bytes 638984 | tf_op jit(solution)/shard_map/ppermute | solution.py:46
  120.9 10.4 %collective-permute-start.22 = (bf16[192,512]{1,0:T(8,128)(2,1)S(1)}, bf16[192,512]{1,0:T(8,128)(2,1)S(1)}, u32[]{:S(2)}, u32[]{:S(2)}) collective-permute-start(bf16[192,512]{1,0:T(8,128)(2,1)S(1)} %get-tuple-element.54), channel_id=1, source_target_pairs={{0,120},{1,121},{2,122},{3,123},{4,124},{5,125},{6,126},{7,127},{8... | collective-permute-start | bytes 589832 | tf_op jit(solution)/shard_map/ppermute | solution.py:46
  (13 other events, 9.7 us)

commit v3 on v2

--- a/solution.py
+++ b/solution.py
@@ -20,6 +20,7 @@
 TILES = 16
 SPAN = 4 * HALF
 BLOCKS = 5
+WHOLE = 3
 AXES = ("seq", "tp")
 VMEM_LIMIT = 48 * 1024 * 1024
 EXP2_SCALE = float(HEAD) ** (-0.5) * math.log2(math.e)
@@ -371,25 +372,26 @@
         keys[pl.ds(start, HALF), :] = tile[:, :HEAD]
         values[pl.ds(start, HALF), :] = tile[:, HEAD:]
 
-    def entry(b, i):
-        return meta[TILES + 4 * lax.rem(b, BLOCKS) + i]
-
-    def job_of(b):
-        return entry(b, 0) + 2 * lax.div(b, BLOCKS)
-
-    def score(b, out):
-        start = pl.multiple_of(entry(b, 1) * HALF, 4 * HALF)
+    def entry(block, i):
+        return meta[TILES + 4 * block[1] + i]
+
+    def job_of(block):
+        return entry(block, 0) + 2 * block[0]
+
+    def score(block, out, mask):
+        start = pl.multiple_of(entry(block, 1) * HALF, 4 * HALF)
         k = keys[pl.ds(start, SPAN), :]
-        scores = lax.dot_general(k, rows[job_of(b)], NT, preferred_element_type=jnp.float32)
-        seen = entry(b, 2) + entry(b, 3) * place[0:1, :]
-        key = lax.broadcasted_iota(jnp.int32, (SPAN, LANES), 0)
-        scores = jnp.where(key < seen, scores, -jnp.inf)
+        scores = lax.dot_general(k, rows[job_of(block)], NT, preferred_element_type=jnp.float32)
+        if mask:
+            seen = entry(block, 2) + entry(block, 3) * place[0:1, :]
+            key = lax.broadcasted_iota(jnp.int32, (SPAN, LANES), 0)
+            scores = jnp.where(key < seen, scores, -jnp.inf)
         out[0:SPAN, :] = scores
         out[SPAN : SPAN + 1, :] = jnp.max(scores, axis=0, keepdims=True)
 
-    def finish(b, src):
-        job = job_of(b)
-        start = pl.multiple_of(entry(b, 1) * HALF, 4 * HALF)
+    def finish(block, src):
+        job = job_of(block)
+        start = pl.multiple_of(entry(block, 1) * HALF, 4 * HALF)
         v = values[pl.ds(start, SPAN), :]
         old = stat[job, 0:1, :]
         new = jnp.maximum(old, src[SPAN : SPAN + 1, :])
@@ -401,22 +403,27 @@
             v, weights.astype(jnp.bfloat16), TN, preferred_element_type=jnp.float32
         )
 
-    total = BLOCKS * groups
-    score(0, even)
-
-    @pl.loop(0, (total - 1) // 2)
+    def whole(b):
+        return lax.div(b, WHOLE), lax.rem(b, WHOLE)
+
+    last = [(g, p) for g in range(groups) for p in range(WHOLE, BLOCKS)]
+    loops = (WHOLE * groups - 1) // 2
+    score((0, 0), even, False)
+
+    @pl.loop(0, loops)
     def _(i):
-        score(2 * i + 1, odd)
-        finish(2 * i, even)
-        score(2 * i + 2, even)
-        finish(2 * i + 1, odd)
-
-    if total % 2:
-        finish(total - 1, even)
-    else:
-        score(total - 1, odd)
-        finish(total - 2, even)
-        finish(total - 1, odd)
+        score(whole(2 * i + 1), odd, False)
+        finish(whole(2 * i), even)
+        score(whole(2 * i + 2), even, False)
+        finish(whole(2 * i + 1), odd)
+
+    rest = [(b // WHOLE, b % WHOLE) for b in range(2 * loops, WHOLE * groups)]
+    steps = [(block, False) for block in rest] + [(block, True) for block in last]
+    buffers = (even, odd)
+    for i, (block, _) in enumerate(steps):
+        if i + 1 < len(steps):
+            score(steps[i + 1][0], buffers[(i + 1) % 2], steps[i + 1][1])
+        finish(block, buffers[i % 2])
     if final:
         for group in range(groups):
             for job in range(2):
@@ -472,16 +479,20 @@
     return out[:2], out[2:]
 
 
-def _blocks(early_count, early_own, late_count, late_own):
-    early_blocks = early_count // 4 + 1 if early_own else (early_count + 3) // 4
+def _blocks(early_count, late_count, own):
+    early_whole, late_whole = early_count // 4, late_count // 4
+    four = early_whole + late_whole == 4
+    blocks = []
+    for b in range(WHOLE):
+        late = (b >= early_whole).astype(jnp.int32)
+        blocks.append((late, b - late * early_whole))
+    blocks.append((four.astype(jnp.int32), jnp.where(four, late_whole - 1, early_whole)))
+    blocks.append((1, late_whole))
     entries = []
-    for b in range(BLOCKS):
-        is_late = (b >= early_blocks).astype(jnp.int32)
-        tile = 4 * (b - is_late * early_blocks)
-        count = jnp.where(is_late == 1, late_count, early_count)
-        own = jnp.where(is_late == 1, int(late_own), int(early_own))
-        entries += [is_late, jnp.minimum(tile, TILES - 4), (count - tile) * HALF, own]
-    return jnp.stack(entries).astype(jnp.int32)
+    for late, block in blocks:
+        count = jnp.where(late == 1, late_count, early_count)
+        entries += [late, jnp.minimum(4 * block, TILES - 4), (count - 4 * block) * HALF, int(own)]
+    return jnp.stack([jnp.asarray(e, jnp.int32) for e in entries])
 
 
 def _angles(positions):
@@ -613,8 +624,8 @@
     far_tiles = _stack_tiles(far_kv)
     other_kv = [_send(near_tiles, other_core), _send(far_tiles, other_core)]
 
-    meta = jnp.concatenate([places(0), _blocks(seq, True, 15 - seq, True)])
-    other_meta = jnp.concatenate([places(1), _blocks(seq, False, 16 - seq, False)])
+    meta = jnp.concatenate([places(0), _blocks(seq, 15 - seq, True)])
+    other_meta = jnp.concatenate([places(1), _blocks(seq, 16 - seq, False)])
     states, _ = _attend(_after(meta, far_tiles), [near_tiles, far_tiles], queries, groups=2)
     (early_low, late_low), ordered = _attend(
         other_meta, other_kv, queries, states, part=0, spare=16

time: 133 us -> 130 us (0.977)
  Pallas kernels: 49.8 us -> 47.6 us
    pallas_call x3, Pallas kernels: 20.7 us -> 18.6 us  [_attend(): pl.pallas_call(functools.partial(_attend_body, len(kv), sort, not states,...]
where the time goes in v3:
time: 130 us
  Pallas kernels  47.6 us (37%)
  starting transfers between devices  43.5 us (33%)
  waiting for transfers between devices  28.6 us (22%)
  local copies, waits for them, and re-layouts  7.76 us (6%)
  other arithmetic  2.31 us (2%)
    ppermute x23, starting transfers between devices, _send(): return lax.ppermute(value, AXES, pairs)  43.5 us
    ppermute x23, waiting for transfers between devices, _send(): return lax.ppermute(value, AXES, pairs)  28.6 us
    pallas_call x3, Pallas kernels, _attend(): pl.pallas_call(functools.partial(_attend_body, len(kv), sort, not states,...  18.6 us
    pallas_call x2, Pallas kernels, _project(): pl.pallas_call(functools.partial(_proj_body, len(arrays), pieces, acc is...  13.2 us
    pallas_call x6, Pallas kernels, _stitch(): pl.pallas_call(body, out_shape=[jax.ShapeDtypeStruct(shape, jnp.bfloat16)...  7.65 us
    unnamed x44, local copies, waits for them, and re-layouts  7.51 us
    pallas_call x1, Pallas kernels, _last_q(): pl.pallas_call(functools.partial(_last_q_body, len(arrays), pieces), out_...  4.7 us
    pallas_call x1, Pallas kernels, _last_kv(): pl.pallas_call(functools.partial(_last_kv_body, len(arrays), pieces), out...  3.49 us
  transfers between devices with their start and end apart: 23, of which 7 were waited for; matrix products, arithmetic and copies ran while one was open for 1% of the time, Pallas kernels for 28%

profile of v3, /device:TPU:1, one launch (start us, length us, event | category | flops | bytes accessed | tf_op | source)
XLA Modules:
  0.0 130.2 jit_solution(5248949532368960648)
XLA Ops:
  0.0 1.1 stitch.6
  1.1 2.1 %collective-permute-start.2 = (bf16[192,1024]{1,0:T(8,128)(2,1)S(1)}, bf16[192,1024]{1,0:T(8,128)(2,1)S(1)}, u32[]{:S(2)}, u32[]{:S(2)}) collective-permute-start(bf16[192,1024]{1,0:T(8,128)(2,1)S(1)} %get-tuple-element.37.refs_0_), channel_id=1, source_target_pairs={{0,4},{1,5},{2,6},{3,7},{4,0},{5,1},{6,2},{7,3},{8,12},{9,13},{10,... | collective-permute-start | bytes 1179656 | tf_op jit(solution)/shard_map/ppermute | solution.py:47
  3.3 3.8 %collective-permute-start.1 = (bf16[192,1024]{1,0:T(8,128)(2,1)S(1)}, bf16[192,1024]{1,0:T(8,128)(2,1)S(1)}, u32[]{:S(2)}, u32[]{:S(2)}) collective-permute-start(bf16[192,1024]{1,0:T(8,128)(2,1)S(1)} %get-tuple-element.37.refs_0_), channel_id=1, source_target_pairs={{0,3},{1,0},{2,1},{3,2},{4,7},{5,4},{6,5},{7,6},{8,11},{9,8},{10,9... | collective-permute-start | bytes 1179656 | tf_op jit(solution)/shard_map/ppermute | solution.py:47
  7.0 5.4 %collective-permute-start.5 = (bf16[192,1024]{1,0:T(8,128)(2,1)S(1)}, bf16[192,1024]{1,0:T(8,128)(2,1)S(1)}, u32[]{:S(2)}, u32[]{:S(2)}) collective-permute-start(bf16[192,1024]{1,0:T(8,128)(2,1)S(1)} %get-tuple-element.34), channel_id=1, source_target_pairs={{0,124},{1,125},{2,126},{3,127},{4,120},{5,121},{6,122},{7,123},{8... | collective-permute-start | bytes 1179656 | tf_op jit(solution)/shard_map/ppermute | solution.py:47
  13.5 4.1 %collective-permute-done.refs_0_ = bf16[192,1024]{1,0:T(8,128)(2,1)S(1)} collective-permute-done((bf16[192,1024]{1,0:T(8,128)(2,1)S(1)}, bf16[192,1024]{1,0:T(8,128)(2,1)S(1)}, u32[]{:S(2)}, u32[]{:S(2)}) %collective-permute-start) | collective-permute-done | bytes 393248 | tf_op jit(solution)/shard_map/ppermute | solution.py:47
  19.2 1.3 stitch.7
  20.6 1.6 %collective-permute-done.5.refs_4_.refs_3_ = bf16[192,1024]{1,0:T(8,128)(2,1)S(1)} collective-permute-done((bf16[192,1024]{1,0:T(8,128)(2,1)S(1)}, bf16[192,1024]{1,0:T(8,128)(2,1)S(1)}, u32[]{:S(2)}, u32[]{:S(2)}) %collective-permute-start.5) | collective-permute-done | bytes 393248 | tf_op jit(solution)/shard_map/ppermute | solution.py:47
  22.2 3.0 %collective-permute-start.4 = (bf16[192,1024]{1,0:T(8,128)(2,1)S(1)}, bf16[192,1024]{1,0:T(8,128)(2,1)S(1)}, u32[]{:S(2)}, u32[]{:S(2)}) collective-permute-start(bf16[192,1024]{1,0:T(8,128)(2,1)S(1)} %get-tuple-element.33), channel_id=1, source_target_pairs={{0,3},{1,0},{2,1},{3,2},{4,7},{5,4},{6,5},{7,6},{8,11},{9,8},{10,9... | collective-permute-start | bytes 1179656 | tf_op jit(solution)/shard_map/ppermute | solution.py:47
  25.1 7.0 %collective-permute-done.6.refs_5_.refs_1_ = bf16[192,1024]{1,0:T(8,128)(2,1)S(1)} collective-permute-done((bf16[192,1024]{1,0:T(8,128)(2,1)S(1)}, bf16[192,1024]{1,0:T(8,128)(2,1)S(1)}, u32[]{:S(2)}, u32[]{:S(2)}) %collective-permute-start.6) | collective-permute-done | bytes 393248 | tf_op jit(solution)/shard_map/ppermute | solution.py:47
  33.8 1.5 %stitch.8 = (bf16[384,1024]{1,0:T(8,128)(2,1)S(1)}, bf16[384,1024]{1,0:T(8,128)(2,1)S(1)}) custom-call(bf16[192,1024]{1,0:T(8,128)(2,1)} %copy-done.9, bf16[192,1024]{1,0:T(8,128)(2,1)} %copy-done.8, bf16[192,1024]{1,0:T(8,128)(2,1)} %copy-done.6, bf16[192,1024]{1,0:T(8,128)(2,1)} %copy-done.7, bf16[192,1024]{1,0:T(8,128)(2,1)} %copy-done.12, ...), custom_call_target="tpu_custom_call" | custom-call | tf_op jit(solution)/shard_map/stitch/pallas_call | solution.py:328
  35.4 3.1 %collective-permute-start.9 = (bf16[384,1024]{1,0:T(8,128)(2,1)S(1)}, bf16[384,1024]{1,0:T(8,128)(2,1)}, u32[]{:S(2)}, u32[]{:S(2)}) collective-permute-start(bf16[384,1024]{1,0:T(8,128)(2,1)S(1)} %get-tuple-element.36), channel_id=1, source_target_pairs={{0,3},{1,0},{2,1},{3,2},{4,7},{5,4},{6,5},{7,6},{8,11},{9,8},{10,9... | collective-permute-start | bytes 2359304 | tf_op jit(solution)/shard_map/ppermute | solution.py:47
  38.5 1.5 %collective-permute-start.7 = (bf16[384,1024]{1,0:T(8,128)(2,1)S(1)}, bf16[384,1024]{1,0:T(8,128)(2,1)S(1)}, u32[]{:S(2)}, u32[]{:S(2)}) collective-permute-start(bf16[384,1024]{1,0:T(8,128)(2,1)S(1)} %get-tuple-element.35), channel_id=1, source_target_pairs={{0,4},{1,5},{2,6},{3,7},{4,0},{5,1},{6,2},{7,3},{8,12},{9,13},{10,... | collective-permute-start | bytes 2359304 | tf_op jit(solution)/shard_map/ppermute | solution.py:47
  40.1 5.2 %project.2.refs_10_ = f32[384,1280]{1,0:T(8,128)S(1)} custom-call(s32[2]{0:T(128)S(1)} %pad_add_fusion.1.slices, bf16[192,1024]{1,0:T(8,128)(2,1)} %copy-done.1, bf16[192,1024]{1,0:T(8,128)(2,1)} %copy-done.13, bf16[192,1024]{1,0:T(8,128)(2,1)} %copy-done.14, bf16[192,1024]{1,0:T(8,128)(2,1)} %copy-done.12, bf16[8192,1024]{1,0:T(8,128)(2,1)} %refs_5_.5, ...), custom_call_target="tpu_custom_call" | custom-call | flops 2013265920 | bytes 5242880 | tf_op jit(solution)/shard_map/project/pallas_call | solution.py:174
  45.4 9.2 %collective-permute-done.8.refs_0_.refs_5_ = bf16[384,1024]{1,0:T(8,128)(2,1)} collective-permute-done((bf16[384,1024]{1,0:T(8,128)(2,1)S(1)}, bf16[384,1024]{1,0:T(8,128)(2,1)}, u32[]{:S(2)}, u32[]{:S(2)}) %collective-permute-start.8) | collective-permute-done | bytes 786464 | tf_op jit(solution)/shard_map/ppermute | solution.py:47
  54.6 1.3 stitch.9
  55.8 2.5 %collective-permute-start.11 = (bf16[192,1024]{1,0:T(8,128)(2,1)S(1)}, bf16[192,1024]{1,0:T(8,128)(2,1)S(1)}, u32[]{:S(2)}, u32[]{:S(2)}) collective-permute-start(bf16[192,1024]{1,0:T(8,128)(2,1)S(1)} %get-tuple-element.40), channel_id=1, source_target_pairs={{0,3},{1,0},{2,1},{3,2},{4,7},{5,4},{6,5},{7,6},{8,11},{9,8},{10,9... | collective-permute-start | bytes 1179656 | tf_op jit(solution)/shard_map/ppermute | solution.py:47
  59.3 8.0 %project.3.refs_7_.refs_6_ = f32[384,1280]{1,0:T(8,128)S(1)} custom-call(s32[4]{0:T(128)S(1)} %pad_add_fusion.2.slices, bf16[192,1024]{1,0:T(8,128)(2,1)} %copy-done.9, bf16[192,1024]{1,0:T(8,128)(2,1)} %copy-done.8, bf16[192,1024]{1,0:T(8,128)(2,1)} %copy-done.6, bf16[192,1024]{1,0:T(8,128)(2,1)} %copy-done.7, bf16[384,1024]{1,0:T(8,128)(2,1)} %copy-done.5, ...), custom_call_target="tpu_custom_call" | custom-call | flops 4026531840 | bytes 10485760 | tf_op jit(solution)/shard_map/project/pallas_call | solution.py:174
  68.2 3.5 %last_kv.1.refs_0_ = bf16[2,192,256]{2,1,0:T(8,128)(2,1)S(1)} custom-call(s32[2]{0:T(128)S(1)} %pad_add_fusion.slices, bf16[384,1024]{1,0:T(8,128)(2,1)} %copy-done.5, bf16[192,1024]{1,0:T(8,128)(2,1)} %copy-done.6, bf16[192,1024]{1,0:T(8,128)(2,1)} %copy-done.7, bf16[192,1024]{1,0:T(8,128)(2,1)} %copy-done.11, bf16[192,1024]{1,0:T(8,128)(2,1)} %copy-done.10, ...), custom_call_target="tpu_custom_call" | custom-call | flops 402653184 | bytes 1048576 | tf_op jit(solution)/shard_map/last_kv/pallas_call | solution.py:231
  71.8 1.3 %collective-permute-start.14 = (bf16[2,192,256]{2,1,0:T(8,128)(2,1)S(1)}, bf16[2,192,256]{2,1,0:T(8,128)(2,1)S(1)}, u32[]{:S(2)}, u32[]{:S(2)}) collective-permute-start(bf16[2,192,256]{2,1,0:T(8,128)(2,1)S(1)} %last_kv.1.refs_0_), channel_id=1, source_target_pairs={{0,64},{1,65},{2,66},{3,67},{4,68},{5,69},{6,70},{7,71},{8,72},{9,... | collective-permute-start | bytes 589832 | tf_op jit(solution)/shard_map/ppermute | solution.py:47
  74.7 4.7 %last_q.1.refs_2_ = bf16[384,1024]{1,0:T(8,128)(2,1)S(1)} custom-call(s32[2]{0:T(128)S(1)} %pad_add_fusion.slices, bf16[384,1024]{1,0:T(8,128)(2,1)} %copy-done.5, bf16[192,1024]{1,0:T(8,128)(2,1)} %copy-done.6, bf16[192,1024]{1,0:T(8,128)(2,1)} %copy-done.7, bf16[192,1024]{1,0:T(8,128)(2,1)} %copy-done.11, bf16[192,1024]{1,0:T(8,128)(2,1)} %copy-done.10, ...), custom_call_target="tpu_custom_call" | custom-call | flops 1610612736 | bytes 4194304 | tf_op jit(solution)/shard_map/last_q/pallas_call | solution.py:288
  79.5 1.9 %collective-permute-start.19 = (bf16[2,192,256]{2,1,0:T(8,128)(2,1)S(1)}, bf16[2,192,256]{2,1,0:T(8,128)(2,1)S(1)}, u32[]{:S(2)}, u32[]{:S(2)}) collective-permute-start(bf16[2,192,256]{2,1,0:T(8,128)(2,1)S(1)} %collective-permute-done.16.refs_0_), channel_id=1, source_target_pairs={{0,64},{1,65},{2,66},{3,67},{4,68},{5,69},{6,70},{7,71},{8,72},{9,... | collective-permute-start | bytes 589832 | tf_op jit(solution)/shard_map/ppermute | solution.py:47
  81.4 2.0 %collective-permute-start.18 = (bf16[2,192,256]{2,1,0:T(8,128)(2,1)S(1)}, bf16[2,192,256]{2,1,0:T(8,128)(2,1)S(1)}, u32[]{:S(2)}, u32[]{:S(2)}) collective-permute-start(bf16[2,192,256]{2,1,0:T(8,128)(2,1)S(1)} %collective-permute-done.16.refs_0_), channel_id=1, source_target_pairs={{0,96},{1,97},{2,98},{3,99},{4,100},{5,101},{6,102},{7,103},{8,104... | collective-permute-start | bytes 589832 | tf_op jit(solution)/shard_map/ppermute | solution.py:47
  84.8 1.3 stitch.10.refs_0_
  86.1 5.9 %collective-permute-start.15 = (bf16[8,192,256]{2,1,0:T(8,128)(2,1)S(1)}, bf16[8,192,256]{2,1,0:T(8,128)(2,1)S(1)}, u32[]{:S(2)}, u32[]{:S(2)}) collective-permute-start(bf16[8,192,256]{2,1,0:T(8,128)(2,1)S(1)} %stitch.10.refs_0_), channel_id=1, source_target_pairs={{0,8},{1,9},{2,10},{3,11},{4,12},{5,13},{6,14},{7,15},{8,0},{9,1},... | collective-permute-start | bytes 2359304 | tf_op jit(solution)/shard_map/ppermute | solution.py:47
  93.4 1.3 stitch.11.refs_1_
  94.7 3.4 %collective-permute-start.20 = (bf16[8,192,256]{2,1,0:T(8,128)(2,1)S(1)}, bf16[8,192,256]{2,1,0:T(8,128)(2,1)}, u32[]{:S(2)}, u32[]{:S(2)}) collective-permute-start(bf16[8,192,256]{2,1,0:T(8,128)(2,1)S(1)} %stitch.11.refs_1_), channel_id=1, source_target_pairs={{0,8},{1,9},{2,10},{3,11},{4,12},{5,13},{6,14},{7,15},{8,0},{9,1},... | collective-permute-start | bytes 2359304 | tf_op jit(solution)/shard_map/ppermute | solution.py:47
  98.4 8.4 %attend.3 = (f32[4,8,768]{2,1,0:T(8,128)S(1)}, f32[4,128,768]{2,1,0:T(8,128)S(1)}) custom-call(s32[36]{0:T(128)S(1)} %concatenate.32.meta, bf16[8,192,256]{2,1,0:T(8,128)(2,1)S(1)} %stitch.10.refs_0_, bf16[8,192,256]{2,1,0:T(8,128)(2,1)S(1)} %stitch.11.refs_1_, bf16[384,1024]{1,0:T(8,128)(2,1)S(1)} %last_q.1.refs_2_), custom_call_target="tpu_custom_call" | custom-call | flops 3019898880 | bytes 4194304 | tf_op jit(solution)/shard_map/attend/pallas_call | solution.py:458
  106.8 5.5 %attend.4 = (bf16[192,512]{1,0:T(8,128)(2,1)S(1)}, bf16[208,512]{1,0:T(8,128)(2,1)S(1)}, bf16[3072,128]{1,0:T(8,128)(2,1)S(1)}, bf16[3072,128]{1,0:T(8,128)(2,1)S(1)}) custom-call(s32[36]{0:T(128)S(1)} %concatenate.28.meta, bf16[8,192,256]{2,1,0:T(8,128)(2,1)S(1)} %collective-permute-done.15.refs_0_, bf16[8,192,256]{2,1,0:T(8,128)(2,1)} %collective-permute-done.20.refs_1_, ...), custom_call_target="tpu_custom_call" | custom-call | flops 1509949440 | bytes 4194304 | tf_op jit(solution)/shard_map/attend/pallas_call | solution.py:458
  112.3 1.7 %collective-permute-start.21 = (bf16[208,512]{1,0:T(8,128)(2,1)S(1)}, bf16[208,512]{1,0:T(8,128)(2,1)S(1)}, u32[]{:S(2)}, u32[]{:S(2)}) collective-permute-start(bf16[208,512]{1,0:T(8,128)(2,1)S(1)} %get-tuple-element.53), channel_id=1, source_target_pairs={{0,120},{1,121},{2,122},{3,123},{4,124},{5,125},{6,126},{7,127},{8... | collective-permute-start | bytes 638984 | tf_op jit(solution)/shard_map/ppermute | solution.py:47
  114.0 4.7 %attend.5 = (bf16[192,512]{1,0:T(8,128)(2,1)S(1)}, bf16[192,512]{1,0:T(8,128)(2,1)S(1)}) custom-call(s32[36]{0:T(128)S(1)} %concatenate.28.meta, bf16[3072,128]{1,0:T(8,128)(2,1)S(1)} %get-tuple-element.50.refs_0_, bf16[3072,128]{1,0:T(8,128)(2,1)S(1)} %get-tuple-element.51.refs_1_, bf16[384,1024]{1,0:T(8,128)(2,1)S(1)} %last_q.1.refs_2_, ...), custom_call_target="tpu_custom_call" | custom-call | flops 1509949440 | bytes 4194304 | tf_op jit(solution)/shard_map/attend/pallas_call | solution.py:458
  118.7 4.0 %collective-permute-start.22 = (bf16[192,512]{1,0:T(8,128)(2,1)S(1)}, bf16[192,512]{1,0:T(8,128)(2,1)S(1)}, u32[]{:S(2)}, u32[]{:S(2)}) collective-permute-start(bf16[192,512]{1,0:T(8,128)(2,1)S(1)} %get-tuple-element.54), channel_id=1, source_target_pairs={{0,120},{1,121},{2,122},{3,123},{4,124},{5,125},{6,126},{7,127},{8... | collective-permute-start | bytes 589832 | tf_op jit(solution)/shard_map/ppermute | solution.py:47
  123.4 5.8 %collective-permute-done.22 = bf16[192,512]{1,0:T(8,128)(2,1)S(1)} collective-permute-done((bf16[192,512]{1,0:T(8,128)(2,1)S(1)}, bf16[192,512]{1,0:T(8,128)(2,1)S(1)}, u32[]{:S(2)}, u32[]{:S(2)}) %collective-permute-start.22) | collective-permute-done | bytes 196640 | tf_op jit(solution)/shard_map/ppermute | solution.py:47
  (85 shorter events, 12.8 us)
Async XLA Ops:
  1.1 34.2 %copy-start.1 = (bf16[192,1024]{1,0:T(8,128)(2,1)}, bf16[192,1024]{1,0:T(8,128)(2,1)S(1)}, u32[]{:S(2)}) copy-start(bf16[192,1024]{1,0:T(8,128)(2,1)S(1)} %get-tuple-element.37.refs_0_) | copy-start | bytes 1179652
  1.1 16.5 %collective-permute-start.2 = (bf16[192,1024]{1,0:T(8,128)(2,1)S(1)}, bf16[192,1024]{1,0:T(8,128)(2,1)S(1)}, u32[]{:S(2)}, u32[]{:S(2)}) collective-permute-start(bf16[192,1024]{1,0:T(8,128)(2,1)S(1)} %get-tuple-element.37.refs_0_), channel_id=1, source_target_pairs={{0,4},{1,5},{2,6},{3,7},{4,0},{5,1},{6,2},{7,3},{8,12},{9,13},{10,... | collective-permute-start | bytes 1179656 | tf_op jit(solution)/shard_map/ppermute | solution.py:47
  3.3 14.3 %collective-permute-start.1 = (bf16[192,1024]{1,0:T(8,128)(2,1)S(1)}, bf16[192,1024]{1,0:T(8,128)(2,1)S(1)}, u32[]{:S(2)}, u32[]{:S(2)}) collective-permute-start(bf16[192,1024]{1,0:T(8,128)(2,1)S(1)} %get-tuple-element.37.refs_0_), channel_id=1, source_target_pairs={{0,3},{1,0},{2,1},{3,2},{4,7},{5,4},{6,5},{7,6},{8,11},{9,8},{10,9... | collective-permute-start | bytes 1179656 | tf_op jit(solution)/shard_map/ppermute | solution.py:47
  7.0 10.6 %collective-permute-start = (bf16[192,1024]{1,0:T(8,128)(2,1)S(1)}, bf16[192,1024]{1,0:T(8,128)(2,1)S(1)}, u32[]{:S(2)}, u32[]{:S(2)}) collective-permute-start(bf16[192,1024]{1,0:T(8,128)(2,1)S(1)} %get-tuple-element.37.refs_0_), channel_id=1, source_target_pairs={{0,1},{1,2},{2,3},{3,0},{4,5},{5,6},{6,7},{7,4},{8,9},{9,10},{10,1... | collective-permute-start | bytes 1179656 | tf_op jit(solution)/shard_map/ppermute | solution.py:47
  7.0 15.1 %collective-permute-start.5 = (bf16[192,1024]{1,0:T(8,128)(2,1)S(1)}, bf16[192,1024]{1,0:T(8,128)(2,1)S(1)}, u32[]{:S(2)}, u32[]{:S(2)}) collective-permute-start(bf16[192,1024]{1,0:T(8,128)(2,1)S(1)} %get-tuple-element.34), channel_id=1, source_target_pairs={{0,124},{1,125},{2,126},{3,127},{4,120},{5,121},{6,122},{7,123},{8... | collective-permute-start | bytes 1179656 | tf_op jit(solution)/shard_map/ppermute | solution.py:47
  20.5 11.7 %collective-permute-start.3 = (bf16[192,1024]{1,0:T(8,128)(2,1)S(1)}, bf16[192,1024]{1,0:T(8,128)(2,1)S(1)}, u32[]{:S(2)}, u32[]{:S(2)}) collective-permute-start(bf16[192,1024]{1,0:T(8,128)(2,1)S(1)} %get-tuple-element.32), channel_id=1, source_target_pairs={{0,1},{1,2},{2,3},{3,0},{4,5},{5,6},{6,7},{7,4},{8,9},{9,10},{10,1... | collective-permute-start | bytes 1179656 | tf_op jit(solution)/shard_map/ppermute | solution.py:47
  22.2 10.0 %copy-start.12 = (bf16[192,1024]{1,0:T(8,128)(2,1)}, bf16[192,1024]{1,0:T(8,128)(2,1)S(1)}, u32[]{:S(2)}) copy-start(bf16[192,1024]{1,0:T(8,128)(2,1)S(1)} %collective-permute-done.5.refs_4_.refs_3_) | copy-start | bytes 1179652
  22.2 10.0 %collective-permute-start.6 = (bf16[192,1024]{1,0:T(8,128)(2,1)S(1)}, bf16[192,1024]{1,0:T(8,128)(2,1)S(1)}, u32[]{:S(2)}, u32[]{:S(2)}) collective-permute-start(bf16[192,1024]{1,0:T(8,128)(2,1)S(1)} %collective-permute-done.5.refs_4_.refs_3_), channel_id=1, source_target_pairs={{0,4},{1,5},{2,6},{3,7},{4,0},{5,1},{6,2},{7,3},{8,12},{9,13},{10,... | collective-permute-start | bytes 1179656 | tf_op jit(solution)/shard_map/ppermute | solution.py:47
  22.2 10.3 %collective-permute-start.4 = (bf16[192,1024]{1,0:T(8,128)(2,1)S(1)}, bf16[192,1024]{1,0:T(8,128)(2,1)S(1)}, u32[]{:S(2)}, u32[]{:S(2)}) collective-permute-start(bf16[192,1024]{1,0:T(8,128)(2,1)S(1)} %get-tuple-element.33), channel_id=1, source_target_pairs={{0,3},{1,0},{2,1},{3,2},{4,7},{5,4},{6,5},{7,6},{8,11},{9,8},{10,9... | collective-permute-start | bytes 1179656 | tf_op jit(solution)/shard_map/ppermute | solution.py:47
  32.2 0.9 copy-start.6
  35.3 19.2 %collective-permute-start.8 = (bf16[384,1024]{1,0:T(8,128)(2,1)S(1)}, bf16[384,1024]{1,0:T(8,128)(2,1)}, u32[]{:S(2)}, u32[]{:S(2)}) collective-permute-start(bf16[384,1024]{1,0:T(8,128)(2,1)S(1)} %get-tuple-element.36), channel_id=1, source_target_pairs={{0,1},{1,2},{2,3},{3,0},{4,5},{5,6},{6,7},{7,4},{8,9},{9,10},{10,1... | collective-permute-start | bytes 2359304 | tf_op jit(solution)/shard_map/ppermute | solution.py:47
  35.4 19.1 %collective-permute-start.9 = (bf16[384,1024]{1,0:T(8,128)(2,1)S(1)}, bf16[384,1024]{1,0:T(8,128)(2,1)}, u32[]{:S(2)}, u32[]{:S(2)}) collective-permute-start(bf16[384,1024]{1,0:T(8,128)(2,1)S(1)} %get-tuple-element.36), channel_id=1, source_target_pairs={{0,3},{1,0},{2,1},{3,2},{4,7},{5,4},{6,5},{7,6},{8,11},{9,8},{10,9... | collective-permute-start | bytes 2359304 | tf_op jit(solution)/shard_map/ppermute | solution.py:47
  38.5 19.9 %collective-permute-start.7 = (bf16[384,1024]{1,0:T(8,128)(2,1)S(1)}, bf16[384,1024]{1,0:T(8,128)(2,1)S(1)}, u32[]{:S(2)}, u32[]{:S(2)}) collective-permute-start(bf16[384,1024]{1,0:T(8,128)(2,1)S(1)} %get-tuple-element.35), channel_id=1, source_target_pairs={{0,4},{1,5},{2,6},{3,7},{4,0},{5,1},{6,2},{7,3},{8,12},{9,13},{10,... | collective-permute-start | bytes 2359304 | tf_op jit(solution)/shard_map/ppermute | solution.py:47
  55.8 11.5 %collective-permute-start.11 = (bf16[192,1024]{1,0:T(8,128)(2,1)S(1)}, bf16[192,1024]{1,0:T(8,128)(2,1)S(1)}, u32[]{:S(2)}, u32[]{:S(2)}) collective-permute-start(bf16[192,1024]{1,0:T(8,128)(2,1)S(1)} %get-tuple-element.40), channel_id=1, source_target_pairs={{0,3},{1,0},{2,1},{3,2},{4,7},{5,4},{6,5},{7,6},{8,11},{9,8},{10,9... | collective-permute-start | bytes 1179656 | tf_op jit(solution)/shard_map/ppermute | solution.py:47
  58.4 9.0 %collective-permute-start.10 = (bf16[192,1024]{1,0:T(8,128)(2,1)S(1)}, bf16[192,1024]{1,0:T(8,128)(2,1)S(1)}, u32[]{:S(2)}, u32[]{:S(2)}) collective-permute-start(bf16[192,1024]{1,0:T(8,128)(2,1)S(1)} %get-tuple-element.39), channel_id=1, source_target_pairs={{0,1},{1,2},{2,3},{3,0},{4,5},{5,6},{6,7},{7,4},{8,9},{9,10},{10,1... | collective-permute-start | bytes 1179656 | tf_op jit(solution)/shard_map/ppermute | solution.py:47
  58.4 9.8 %copy-start.3 = (f32[128]{0:T(128)S(1)}, f32[128]{0:T(128)}, u32[]{:S(2)}) copy-start(f32[128]{0:T(128)} %param.12) | copy-start | bytes 1540
  58.4 9.8 %copy-start.4 = (f32[128]{0:T(128)S(1)}, f32[128]{0:T(128)}, u32[]{:S(2)}) copy-start(f32[128]{0:T(128)} %param.13) | copy-start | bytes 1540
  58.4 0.9 copy-start.5
  68.2 6.5 %copy-start.2 = (f32[1024]{0:T(1024)S(1)}, f32[1024]{0:T(1024)}, u32[]{:S(2)}) copy-start(f32[1024]{0:T(1024)} %param.11) | copy-start | bytes 12292
  71.7 7.7 %copy-start = (bf16[2,192,256]{2,1,0:T(8,128)(2,1)}, bf16[2,192,256]{2,1,0:T(8,128)(2,1)S(1)}, u32[]{:S(2)}) copy-start(bf16[2,192,256]{2,1,0:T(8,128)(2,1)S(1)} %last_kv.1.refs_0_) | copy-start | bytes 589828
  71.7 7.7 %collective-permute-start.16 = (bf16[2,192,256]{2,1,0:T(8,128)(2,1)S(1)}, bf16[2,192,256]{2,1,0:T(8,128)(2,1)S(1)}, u32[]{:S(2)}, u32[]{:S(2)}) collective-permute-start(bf16[2,192,256]{2,1,0:T(8,128)(2,1)S(1)} %last_kv.1.refs_0_), channel_id=1, source_target_pairs={{0,16},{1,17},{2,18},{3,19},{4,20},{5,21},{6,22},{7,23},{8,24},{9,... | collective-permute-start | bytes 589832 | tf_op jit(solution)/shard_map/ppermute | solution.py:47
  71.8 11.6 %collective-permute-start.14 = (bf16[2,192,256]{2,1,0:T(8,128)(2,1)S(1)}, bf16[2,192,256]{2,1,0:T(8,128)(2,1)S(1)}, u32[]{:S(2)}, u32[]{:S(2)}) collective-permute-start(bf16[2,192,256]{2,1,0:T(8,128)(2,1)S(1)} %last_kv.1.refs_0_), channel_id=1, source_target_pairs={{0,64},{1,65},{2,66},{3,67},{4,68},{5,69},{6,70},{7,71},{8,72},{9,... | collective-permute-start | bytes 589832 | tf_op jit(solution)/shard_map/ppermute | solution.py:47
  73.1 10.3 %collective-permute-start.13 = (bf16[2,192,256]{2,1,0:T(8,128)(2,1)S(1)}, bf16[2,192,256]{2,1,0:T(8,128)(2,1)S(1)}, u32[]{:S(2)}, u32[]{:S(2)}) collective-permute-start(bf16[2,192,256]{2,1,0:T(8,128)(2,1)S(1)} %last_kv.1.refs_0_), channel_id=1, source_target_pairs={{0,96},{1,97},{2,98},{3,99},{4,100},{5,101},{6,102},{7,103},{8,104... | collective-permute-start | bytes 589832 | tf_op jit(solution)/shard_map/ppermute | solution.py:47
  74.1 9.3 %collective-permute-start.12 = (bf16[2,192,256]{2,1,0:T(8,128)(2,1)S(1)}, bf16[2,192,256]{2,1,0:T(8,128)(2,1)S(1)}, u32[]{:S(2)}, u32[]{:S(2)}) collective-permute-start(bf16[2,192,256]{2,1,0:T(8,128)(2,1)S(1)} %last_kv.1.refs_0_), channel_id=1, source_target_pairs={{0,32},{1,33},{2,34},{3,35},{4,36},{5,37},{6,38},{7,39},{8,40},{9,... | collective-permute-start | bytes 589832 | tf_op jit(solution)/shard_map/ppermute | solution.py:47
  79.5 12.6 %copy-start.15 = (bf16[2,192,256]{2,1,0:T(8,128)(2,1)}, bf16[2,192,256]{2,1,0:T(8,128)(2,1)S(1)}, u32[]{:S(2)}) copy-start(bf16[2,192,256]{2,1,0:T(8,128)(2,1)S(1)} %collective-permute-done.16.refs_0_) | copy-start | bytes 589828
  79.5 12.5 %collective-permute-start.19 = (bf16[2,192,256]{2,1,0:T(8,128)(2,1)S(1)}, bf16[2,192,256]{2,1,0:T(8,128)(2,1)S(1)}, u32[]{:S(2)}, u32[]{:S(2)}) collective-permute-start(bf16[2,192,256]{2,1,0:T(8,128)(2,1)S(1)} %collective-permute-done.16.refs_0_), channel_id=1, source_target_pairs={{0,64},{1,65},{2,66},{3,67},{4,68},{5,69},{6,70},{7,71},{8,72},{9,... | collective-permute-start | bytes 589832 | tf_op jit(solution)/shard_map/ppermute | solution.py:47
  81.4 10.7 %collective-permute-start.18 = (bf16[2,192,256]{2,1,0:T(8,128)(2,1)S(1)}, bf16[2,192,256]{2,1,0:T(8,128)(2,1)S(1)}, u32[]{:S(2)}, u32[]{:S(2)}) collective-permute-start(bf16[2,192,256]{2,1,0:T(8,128)(2,1)S(1)} %collective-permute-done.16.refs_0_), channel_id=1, source_target_pairs={{0,96},{1,97},{2,98},{3,99},{4,100},{5,101},{6,102},{7,103},{8,104... | collective-permute-start | bytes 589832 | tf_op jit(solution)/shard_map/ppermute | solution.py:47
  83.4 8.6 %collective-permute-start.17 = (bf16[2,192,256]{2,1,0:T(8,128)(2,1)S(1)}, bf16[2,192,256]{2,1,0:T(8,128)(2,1)S(1)}, u32[]{:S(2)}, u32[]{:S(2)}) collective-permute-start(bf16[2,192,256]{2,1,0:T(8,128)(2,1)S(1)} %collective-permute-done.16.refs_0_), channel_id=1, source_target_pairs={{0,32},{1,33},{2,34},{3,35},{4,36},{5,37},{6,38},{7,39},{8,40},{9,... | collective-permute-start | bytes 589832 | tf_op jit(solution)/shard_map/ppermute | solution.py:47
  86.1 20.7 %collective-permute-start.15 = (bf16[8,192,256]{2,1,0:T(8,128)(2,1)S(1)}, bf16[8,192,256]{2,1,0:T(8,128)(2,1)S(1)}, u32[]{:S(2)}, u32[]{:S(2)}) collective-permute-start(bf16[8,192,256]{2,1,0:T(8,128)(2,1)S(1)} %stitch.10.refs_0_), channel_id=1, source_target_pairs={{0,8},{1,9},{2,10},{3,11},{4,12},{5,13},{6,14},{7,15},{8,0},{9,1},... | collective-permute-start | bytes 2359304 | tf_op jit(solution)/shard_map/ppermute | solution.py:47
  94.7 12.1 %collective-permute-start.20 = (bf16[8,192,256]{2,1,0:T(8,128)(2,1)S(1)}, bf16[8,192,256]{2,1,0:T(8,128)(2,1)}, u32[]{:S(2)}, u32[]{:S(2)}) collective-permute-start(bf16[8,192,256]{2,1,0:T(8,128)(2,1)S(1)} %stitch.11.refs_1_), channel_id=1, source_target_pairs={{0,8},{1,9},{2,10},{3,11},{4,12},{5,13},{6,14},{7,15},{8,0},{9,1},... | collective-permute-start | bytes 2359304 | tf_op jit(solution)/shard_map/ppermute | solution.py:47
  112.3 11.0 %collective-permute-start.21 = (bf16[208,512]{1,0:T(8,128)(2,1)S(1)}, bf16[208,512]{1,0:T(8,128)(2,1)S(1)}, u32[]{:S(2)}, u32[]{:S(2)}) collective-permute-start(bf16[208,512]{1,0:T(8,128)(2,1)S(1)} %get-tuple-element.53), channel_id=1, source_target_pairs={{0,120},{1,121},{2,122},{3,123},{4,124},{5,125},{6,126},{7,127},{8... | collective-permute-start | bytes 638984 | tf_op jit(solution)/shard_map/ppermute | solution.py:47
  118.7 10.5 %collective-permute-start.22 = (bf16[192,512]{1,0:T(8,128)(2,1)S(1)}, bf16[192,512]{1,0:T(8,128)(2,1)S(1)}, u32[]{:S(2)}, u32[]{:S(2)}) collective-permute-start(bf16[192,512]{1,0:T(8,128)(2,1)S(1)} %get-tuple-element.54), channel_id=1, source_target_pairs={{0,120},{1,121},{2,122},{3,123},{4,124},{5,125},{6,126},{7,127},{8... | collective-permute-start | bytes 589832 | tf_op jit(solution)/shard_map/ppermute | solution.py:47
  (13 other events, 9.7 us)

commit v4 on v3

--- a/solution.py
+++ b/solution.py
@@ -17,7 +17,6 @@
 QCOLS = GROUP * HEAD
 ALLCOLS = QCOLS + 2 * HEAD
 LANES = 4 * HALF
-TILES = 16
 SPAN = 4 * HALF
 BLOCKS = 5
 WHOLE = 3
@@ -127,6 +126,19 @@
     ]
 
 
+def _side_by_side(slices, n, far, near, sem):
+    loads = []
+    for i in range(n):
+        at, group = 0, []
+        for j, src in enumerate(far):
+            width = src.shape[1]
+            dst = near.at[i, :, pl.ds(at, width)]
+            group.append(pltpu.make_async_copy(src.at[_block(slices[i]), :], dst, sem.at[i, j]))
+            at += width
+        loads.append(group)
+    return loads
+
+
 def _start(group):
     for copy in group:
         copy.start()
@@ -145,9 +157,8 @@
     acc, x, near, (x_sem, w_sem, acc_sem) = refs[0], refs[1], refs[2:5], refs[5:8]
     x_loads = _piece_loads(parts, pieces, x, x_sem)
     w_loads = _weight_loads(slices, n, far, near, w_sem)
-    for i in range(min(2, n)):
-        _start(x_loads[i])
-        _start(w_loads[i])
+    for group in [x_loads[0], w_loads[0], *x_loads[1:], w_loads[1]]:
+        _start(group)
     if started:
         acc_load = pltpu.make_async_copy(acc_in, acc, acc_sem)
         acc_load.start()
@@ -156,7 +167,6 @@
         _wait(x_loads[i])
         _wait(w_loads[i])
         if i + 2 < n:
-            _start(x_loads[i + 2])
             _start(w_loads[i + 2])
         if started and i == 0:
             acc_load.wait()
@@ -203,21 +213,20 @@
     n = len(pieces)
     parts, (w_k, w_v), refs = refs[:arrays], refs[arrays : arrays + 2], refs[arrays + 2 :]
     given, (k_bias, v_bias, cosine, sine, out), refs = refs[0], refs[1:6], refs[6:]
-    x, near_k, near_v, acc, x_sem, w_sem, sem = refs
+    x, near, acc, x_sem, w_sem, sem = refs
     x_loads = _piece_loads(parts, pieces, x, x_sem)
-    w_loads = _weight_loads(slices, n, (w_k, w_v), (near_k, near_v), w_sem)
+    w_loads = _side_by_side(slices, n, (w_k, w_v), near, w_sem)
     others = [pltpu.make_async_copy(given.at[:, pl.ds(QCOLS, 2 * HEAD)], acc, sem)]
     for group in x_loads + w_loads + [others]:
         _start(group)
-    k = v = 0
+    both = 0
     for i in range(n):
         _wait(x_loads[i])
         _wait(w_loads[i])
-        k += jnp.dot(x[i], near_k[i], preferred_element_type=jnp.float32)
-        v += jnp.dot(x[i], near_v[i], preferred_element_type=jnp.float32)
+        both += jnp.dot(x[i], near[i], preferred_element_type=jnp.float32)
     _wait(others)
-    k += acc[:, :HEAD]
-    v += acc[:, HEAD:]
+    both += acc[...]
+    k, v = both[:, :HEAD], both[:, HEAD:]
     k = _rotate(k + k_bias[...], cosine, sine).astype(jnp.bfloat16)
     v = (v + v_bias[...]).astype(jnp.bfloat16)
     for half in range(2):
@@ -235,8 +244,7 @@
         out_specs=VMEM,
         scratch_shapes=[
             pltpu.VMEM((n, ROWS, DEPTH), jnp.bfloat16),
-            pltpu.VMEM((n, DEPTH, HEAD), jnp.bfloat16),
-            pltpu.VMEM((n, DEPTH, HEAD), jnp.bfloat16),
+            pltpu.VMEM((n, DEPTH, 2 * HEAD), jnp.bfloat16),
             pltpu.VMEM((ROWS, 2 * HEAD), jnp.float32),
             pltpu.SemaphoreType.DMA((n, 4)),
             pltpu.SemaphoreType.DMA((n, 2)),
@@ -341,13 +349,10 @@
     return _stitch([(8, HALF, 2 * HEAD)], moves, *arrays)[0]
 
 
-def _attend_body(given, sort, first, final, part, meta, *refs):
-    kv, refs = refs[:given], refs[given:]
-    queries, refs = refs[0], refs[1:]
+def _attend_body(first, final, part, meta, near, far, queries, *refs):
     states_in, refs = ((), refs) if first else (refs[:2], refs[2:])
     outs, refs = refs[:2], refs[2:]
-    keys, values = refs[:2] if sort else kv
-    rows, even, odd, place = refs[2 if sort else 0 :][:4]
+    rows, even, odd, place = refs[:4]
     stat, acc = refs[-2:] if final else outs
     groups = acc.shape[0] // 2
     for group in range(groups):
@@ -366,33 +371,37 @@
     else:
         stat[...] = states_in[0][2 * part : 2 * part + 2 * groups]
         acc[...] = states_in[1][2 * part : 2 * part + 2 * groups]
-    tiles = [array.at[i] for array in kv for i in range(array.shape[0])] if sort else []
-    for i, tile in enumerate(tiles):
-        start = pl.multiple_of(meta[i] * HALF, HALF)
-        keys[pl.ds(start, HALF), :] = tile[:, :HEAD]
-        values[pl.ds(start, HALF), :] = tile[:, HEAD:]
-
     def entry(block, i):
-        return meta[TILES + 4 * block[1] + i]
+        return meta[22 + 2 * block[1] + i]
+
+    def tiles(block, cols):
+        j = jnp.minimum(entry(block, 1), 3)
+        return jnp.concatenate(
+            [array[meta[8 * i + 2 * j + t], :, cols] for i, array in enumerate((near, far)) for t in range(2)],
+            axis=0,
+        )
 
     def job_of(block):
         return entry(block, 0) + 2 * block[0]
 
     def score(block, out, mask):
-        start = pl.multiple_of(entry(block, 1) * HALF, 4 * HALF)
-        k = keys[pl.ds(start, SPAN), :]
+        k = tiles(block, slice(0, HEAD))
         scores = lax.dot_general(k, rows[job_of(block)], NT, preferred_element_type=jnp.float32)
         if mask:
-            seen = entry(block, 2) + entry(block, 3) * place[0:1, :]
-            key = lax.broadcasted_iota(jnp.int32, (SPAN, LANES), 0)
-            scores = jnp.where(key < seen, scores, -jnp.inf)
+            mine = meta[20 + entry(block, 0)]
+            key = lax.broadcasted_iota(jnp.int32, (HALF, LANES), 0)
+            parts = []
+            for t in range(4):
+                tile = 8 * entry(block, 1) + meta[16 + t]
+                seen = jnp.where(tile < mine, HALF, 0) + jnp.where(tile == mine, 1, 0) * place[0:1, :]
+                parts.append(jnp.where(key < seen, scores[t * HALF : (t + 1) * HALF], -jnp.inf))
+            scores = jnp.concatenate(parts, axis=0)
         out[0:SPAN, :] = scores
         out[SPAN : SPAN + 1, :] = jnp.max(scores, axis=0, keepdims=True)
 
     def finish(block, src):
         job = job_of(block)
-        start = pl.multiple_of(entry(block, 1) * HALF, 4 * HALF)
-        v = values[pl.ds(start, SPAN), :]
+        v = tiles(block, slice(HEAD, 2 * HEAD))
         old = stat[job, 0:1, :]
         new = jnp.maximum(old, src[SPAN : SPAN + 1, :])
         weights = jnp.exp2((src[0:SPAN, :] - new) * EXP2_SCALE)
@@ -439,10 +448,8 @@
             outs[1][HALF:, :] = jnp.zeros((spare, outs[1].shape[1]), jnp.bfloat16)
 
 
-def _attend(meta, kv, queries, states=(), groups=1, part=0, spare=0):
+def _attend(meta, near, far, queries, states=(), groups=2, part=0, spare=0):
     final = bool(states)
-    sort = len(kv[0].shape) == 3
-    ordered = [(TILES * HALF, HEAD)] * (2 if sort else 0)
     state_shape = [(2 * groups, 8, LANES), (2 * groups, HEAD, LANES)]
     if final:
         out_shape = [
@@ -451,17 +458,13 @@
         ]
     else:
         out_shape = [jax.ShapeDtypeStruct(shape, jnp.float32) for shape in state_shape]
-    if final:
-        out_shape += [jax.ShapeDtypeStruct(shape, jnp.bfloat16) for shape in ordered]
-        ordered = []
-    near = [*kv, queries, *states]
-    out = pl.pallas_call(
-        functools.partial(_attend_body, len(kv), sort, not states, final, part),
+    operands = [near, far, queries, *states]
+    return pl.pallas_call(
+        functools.partial(_attend_body, not states, final, part),
         out_shape=out_shape,
-        in_specs=[SMEM] + [VMEM] * len(near),
+        in_specs=[SMEM] + [VMEM] * len(operands),
         out_specs=[VMEM] * len(out_shape),
-        scratch_shapes=[pltpu.VMEM(shape, jnp.bfloat16) for shape in ordered]
-        + [
+        scratch_shapes=[
             pltpu.VMEM((2 * groups, LANES, HEAD), jnp.bfloat16),
             pltpu.VMEM((SPAN + 8, LANES), jnp.float32),
             pltpu.VMEM((SPAN + 8, LANES), jnp.float32),
@@ -475,11 +478,10 @@
             transcendentals=groups * BLOCKS * SPAN * LANES,
         ),
         name="attend",
-    )(meta, *near)
-    return out[:2], out[2:]
-
-
-def _blocks(early_count, late_count, own):
+    )(meta, *operands)
+
+
+def _meta(order, lowest, early_query, late_query, early_count, late_count):
     early_whole, late_whole = early_count // 4, late_count // 4
     four = early_whole + late_whole == 4
     blocks = []
@@ -488,11 +490,10 @@
         blocks.append((late, b - late * early_whole))
     blocks.append((four.astype(jnp.int32), jnp.where(four, late_whole - 1, early_whole)))
     blocks.append((1, late_whole))
-    entries = []
+    entries = [*lowest, early_query, late_query]
     for late, block in blocks:
-        count = jnp.where(late == 1, late_count, early_count)
-        entries += [late, jnp.minimum(4 * block, TILES - 4), (count - 4 * block) * HALF, int(own)]
-    return jnp.stack([jnp.asarray(e, jnp.int32) for e in entries])
+        entries += [late, block]
+    return jnp.concatenate([order, jnp.stack([jnp.asarray(e, jnp.int32) for e in entries])])
 
 
 def _angles(positions):
@@ -521,9 +522,16 @@
     def tile_seq(dy, dx, dc):
         return ((y + dy) % 4 * 2 + (x_hi ^ dx)) * 2 + (core ^ dc)
 
-    def places(dc):
-        seqs = [tile_seq(dy, dx, dc) for dx in (0, 1) for dy in (0, -1, 1, 2)]
-        return jnp.stack([p for s in seqs for p in (s, 15 - s)]).astype(jnp.int32)
+    def order(dc):
+        where, lowest = [], []
+        for dx in (0, 1):
+            seqs = [tile_seq(dy, dx, dc) for dy in (0, -1, 1, 2)]
+            ranks = jnp.stack([t // 4 for s in seqs for t in (2 * s, 31 - 2 * s)])
+            at = jnp.arange(8, dtype=jnp.int32)
+            where.append(jnp.sum(jnp.where(ranks[None, :] == at[:, None], at[None, :], 0), axis=1))
+            a = 4 * (x_hi ^ dx) + 2 * (core ^ dc)
+            lowest += [jnp.minimum(a, 7 - a), jnp.maximum(a, 7 - a)]
+        return jnp.concatenate(where).astype(jnp.int32), lowest
 
     far_lo = 1 - x_lo
 
@@ -541,7 +549,10 @@
     late = _send(late, mirror_cross)
     row = jnp.arange(HALF, dtype=jnp.int32)
     rope = _angles(jnp.concatenate([seq * ROWS + row, (31 - 2 * seq) * HALF + row]))
-    up, *rope = lax.optimization_barrier((up, *rope))
+    mine = seq * 2, 31 - seq * 2
+    meta = _meta(*order(0), *mine, seq, 15 - seq)
+    other_meta = _meta(*order(1), *mine, seq, 16 - seq)
+    up, meta, other_meta, *rope = lax.optimization_barrier((up, meta, other_meta, *rope))
 
     to_up, to_down = _stitch(
         [(HALF, DEPTH)] * 2,
@@ -624,14 +635,12 @@
     far_tiles = _stack_tiles(far_kv)
     other_kv = [_send(near_tiles, other_core), _send(far_tiles, other_core)]
 
-    meta = jnp.concatenate([places(0), _blocks(seq, 15 - seq, True)])
-    other_meta = jnp.concatenate([places(1), _blocks(seq, 16 - seq, False)])
-    states, _ = _attend(_after(meta, far_tiles), [near_tiles, far_tiles], queries, groups=2)
-    (early_low, late_low), ordered = _attend(
-        other_meta, other_kv, queries, states, part=0, spare=16
-    )
+    states = _attend(_after(meta, far_tiles), near_tiles, far_tiles, queries)
+    early_low, late_low = _attend(other_meta, *other_kv, queries, states, groups=1, spare=16)
     back_low = _send(late_low, mirror)
-    (early_high, late_high), _ = _attend(other_meta, ordered, queries, states, part=1)
+    early_high, late_high = _attend(
+        _after(other_meta, late_low), *other_kv, queries, states, groups=1, part=1
+    )
     back_high = _send(late_high, mirror)
     return jnp.concatenate(
         [

time: 130 us -> 129 us (level)
  transfers between devices with their start and end apart: 23 -> 23, of which waited for: 7 -> 7; matrix products, arithmetic and copies ran while one was open for 1% -> 2% of each run, Pallas kernels for 28% -> 28%
where the time goes in v4:
time: 129 us
  Pallas kernels  46.5 us (36%)
  starting transfers between devices  43.7 us (34%)
  waiting for transfers between devices  27.9 us (22%)
  local copies, waits for them, and re-layouts  8.07 us (6%)
  other arithmetic  2.62 us (2%)
    ppermute x23, starting transfers between devices, _send(): return lax.ppermute(value, AXES, pairs)  43.7 us
    ppermute x23, waiting for transfers between devices, _send(): return lax.ppermute(value, AXES, pairs)  27.9 us
    pallas_call x3, Pallas kernels, _attend(): pl.pallas_call(functools.partial(_attend_body, not states, final, part),...  17.5 us
    pallas_call x2, Pallas kernels, _project(): pl.pallas_call(functools.partial(_proj_body, len(arrays), pieces, acc is...  13.6 us
    pallas_call x6, Pallas kernels, _stitch(): pl.pallas_call(body, out_shape=[jax.ShapeDtypeStruct(shape, jnp.bfloat16)...  7.65 us
    unnamed x44, local copies, waits for them, and re-layouts  7.53 us
    pallas_call x1, Pallas kernels, _last_q(): pl.pallas_call(functools.partial(_last_q_body, len(arrays), pieces), out_...  4.71 us
    pallas_call x1, Pallas kernels, _last_kv(): pl.pallas_call(functools.partial(_last_kv_body, len(arrays), pieces), out...  3.08 us
  transfers between devices with their start and end apart: 23, of which 7 were waited for; matrix products, arithmetic and copies ran while one was open for 2% of the time, Pallas kernels for 28%

profile of v4, /device:TPU:1, one launch (start us, length us, event | category | flops | bytes accessed | tf_op | source)
XLA Modules:
  0.0 129.1 jit_solution(11571004631854064970)
XLA Ops:
  0.0 1.1 stitch.6
  1.1 2.1 %collective-permute-start.2 = (bf16[192,1024]{1,0:T(8,128)(2,1)S(1)}, bf16[192,1024]{1,0:T(8,128)(2,1)S(1)}, u32[]{:S(2)}, u32[]{:S(2)}) collective-permute-start(bf16[192,1024]{1,0:T(8,128)(2,1)S(1)} %get-tuple-element.39.refs_0_), channel_id=1, source_target_pairs={{0,4},{1,5},{2,6},{3,7},{4,0},{5,1},{6,2},{7,3},{8,12},{9,13},{10,... | collective-permute-start | bytes 1179656 | tf_op jit(solution)/shard_map/ppermute | solution.py:46
  3.3 3.8 %collective-permute-start.1 = (bf16[192,1024]{1,0:T(8,128)(2,1)S(1)}, bf16[192,1024]{1,0:T(8,128)(2,1)S(1)}, u32[]{:S(2)}, u32[]{:S(2)}) collective-permute-start(bf16[192,1024]{1,0:T(8,128)(2,1)S(1)} %get-tuple-element.39.refs_0_), channel_id=1, source_target_pairs={{0,3},{1,0},{2,1},{3,2},{4,7},{5,4},{6,5},{7,6},{8,11},{9,8},{10,9... | collective-permute-start | bytes 1179656 | tf_op jit(solution)/shard_map/ppermute | solution.py:46
  7.0 5.4 %collective-permute-start.5 = (bf16[192,1024]{1,0:T(8,128)(2,1)S(1)}, bf16[192,1024]{1,0:T(8,128)(2,1)S(1)}, u32[]{:S(2)}, u32[]{:S(2)}) collective-permute-start(bf16[192,1024]{1,0:T(8,128)(2,1)S(1)} %get-tuple-element.36), channel_id=1, source_target_pairs={{0,124},{1,125},{2,126},{3,127},{4,120},{5,121},{6,122},{7,123},{8... | collective-permute-start | bytes 1179656 | tf_op jit(solution)/shard_map/ppermute | solution.py:46
  14.4 3.2 %collective-permute-done.refs_0_ = bf16[192,1024]{1,0:T(8,128)(2,1)S(1)} collective-permute-done((bf16[192,1024]{1,0:T(8,128)(2,1)S(1)}, bf16[192,1024]{1,0:T(8,128)(2,1)S(1)}, u32[]{:S(2)}, u32[]{:S(2)}) %collective-permute-start) | collective-permute-done | bytes 393248 | tf_op jit(solution)/shard_map/ppermute | solution.py:46
  19.2 1.3 stitch.7
  20.6 1.6 %collective-permute-done.5.refs_4_.refs_3_ = bf16[192,1024]{1,0:T(8,128)(2,1)S(1)} collective-permute-done((bf16[192,1024]{1,0:T(8,128)(2,1)S(1)}, bf16[192,1024]{1,0:T(8,128)(2,1)S(1)}, u32[]{:S(2)}, u32[]{:S(2)}) %collective-permute-start.5) | collective-permute-done | bytes 393248 | tf_op jit(solution)/shard_map/ppermute | solution.py:46
  22.2 3.0 %collective-permute-start.4 = (bf16[192,1024]{1,0:T(8,128)(2,1)S(1)}, bf16[192,1024]{1,0:T(8,128)(2,1)S(1)}, u32[]{:S(2)}, u32[]{:S(2)}) collective-permute-start(bf16[192,1024]{1,0:T(8,128)(2,1)S(1)} %get-tuple-element.35), channel_id=1, source_target_pairs={{0,3},{1,0},{2,1},{3,2},{4,7},{5,4},{6,5},{7,6},{8,11},{9,8},{10,9... | collective-permute-start | bytes 1179656 | tf_op jit(solution)/shard_map/ppermute | solution.py:46
  25.1 7.0 %collective-permute-done.6.refs_5_.refs_1_ = bf16[192,1024]{1,0:T(8,128)(2,1)S(1)} collective-permute-done((bf16[192,1024]{1,0:T(8,128)(2,1)S(1)}, bf16[192,1024]{1,0:T(8,128)(2,1)S(1)}, u32[]{:S(2)}, u32[]{:S(2)}) %collective-permute-start.6) | collective-permute-done | bytes 393248 | tf_op jit(solution)/shard_map/ppermute | solution.py:46
  33.8 1.5 %stitch.8 = (bf16[384,1024]{1,0:T(8,128)(2,1)S(1)}, bf16[384,1024]{1,0:T(8,128)(2,1)S(1)}) custom-call(bf16[192,1024]{1,0:T(8,128)(2,1)} %copy-done.9, bf16[192,1024]{1,0:T(8,128)(2,1)} %copy-done.8, bf16[192,1024]{1,0:T(8,128)(2,1)} %copy-done.6, bf16[192,1024]{1,0:T(8,128)(2,1)} %copy-done.7, bf16[192,1024]{1,0:T(8,128)(2,1)} %copy-done.12, ...), custom_call_target="tpu_custom_call" | custom-call | tf_op jit(solution)/shard_map/stitch/pallas_call | solution.py:336
  35.4 3.1 %collective-permute-start.9 = (bf16[384,1024]{1,0:T(8,128)(2,1)S(1)}, bf16[384,1024]{1,0:T(8,128)(2,1)}, u32[]{:S(2)}, u32[]{:S(2)}) collective-permute-start(bf16[384,1024]{1,0:T(8,128)(2,1)S(1)} %get-tuple-element.38), channel_id=1, source_target_pairs={{0,3},{1,0},{2,1},{3,2},{4,7},{5,4},{6,5},{7,6},{8,11},{9,8},{10,9... | collective-permute-start | bytes 2359304 | tf_op jit(solution)/shard_map/ppermute | solution.py:46
  38.5 1.5 %collective-permute-start.7 = (bf16[384,1024]{1,0:T(8,128)(2,1)S(1)}, bf16[384,1024]{1,0:T(8,128)(2,1)S(1)}, u32[]{:S(2)}, u32[]{:S(2)}) collective-permute-start(bf16[384,1024]{1,0:T(8,128)(2,1)S(1)} %get-tuple-element.37), channel_id=1, source_target_pairs={{0,4},{1,5},{2,6},{3,7},{4,0},{5,1},{6,2},{7,3},{8,12},{9,13},{10,... | collective-permute-start | bytes 2359304 | tf_op jit(solution)/shard_map/ppermute | solution.py:46
  40.1 5.2 %project.2.refs_10_ = f32[384,1280]{1,0:T(8,128)S(1)} custom-call(s32[2]{0:T(128)S(1)} %pad_add_fusion.1.slices, bf16[192,1024]{1,0:T(8,128)(2,1)} %copy-done.1, bf16[192,1024]{1,0:T(8,128)(2,1)} %copy-done.13, bf16[192,1024]{1,0:T(8,128)(2,1)} %copy-done.14, bf16[192,1024]{1,0:T(8,128)(2,1)} %copy-done.12, bf16[8192,1024]{1,0:T(8,128)(2,1)} %refs_5_.5, ...), custom_call_target="tpu_custom_call" | custom-call | flops 2013265920 | bytes 5242880 | tf_op jit(solution)/shard_map/project/pallas_call | solution.py:184
  45.3 9.2 %collective-permute-done.8.refs_0_.refs_5_ = bf16[384,1024]{1,0:T(8,128)(2,1)} collective-permute-done((bf16[384,1024]{1,0:T(8,128)(2,1)S(1)}, bf16[384,1024]{1,0:T(8,128)(2,1)}, u32[]{:S(2)}, u32[]{:S(2)}) %collective-permute-start.8) | collective-permute-done | bytes 786464 | tf_op jit(solution)/shard_map/ppermute | solution.py:46
  54.6 1.3 stitch.9
  55.8 2.5 %collective-permute-start.11 = (bf16[192,1024]{1,0:T(8,128)(2,1)S(1)}, bf16[192,1024]{1,0:T(8,128)(2,1)S(1)}, u32[]{:S(2)}, u32[]{:S(2)}) collective-permute-start(bf16[192,1024]{1,0:T(8,128)(2,1)S(1)} %get-tuple-element.42), channel_id=1, source_target_pairs={{0,3},{1,0},{2,1},{3,2},{4,7},{5,4},{6,5},{7,6},{8,11},{9,8},{10,9... | collective-permute-start | bytes 1179656 | tf_op jit(solution)/shard_map/ppermute | solution.py:46
  59.3 8.3 %project.3.refs_7_.refs_6_ = f32[384,1280]{1,0:T(8,128)S(1)} custom-call(s32[4]{0:T(128)S(1)} %pad_add_fusion.2.slices, bf16[192,1024]{1,0:T(8,128)(2,1)} %copy-done.9, bf16[192,1024]{1,0:T(8,128)(2,1)} %copy-done.8, bf16[192,1024]{1,0:T(8,128)(2,1)} %copy-done.6, bf16[192,1024]{1,0:T(8,128)(2,1)} %copy-done.7, bf16[384,1024]{1,0:T(8,128)(2,1)} %copy-done.5, ...), custom_call_target="tpu_custom_call" | custom-call | flops 4026531840 | bytes 10485760 | tf_op jit(solution)/shard_map/project/pallas_call | solution.py:184
  68.6 3.1 %last_kv.1.refs_0_ = bf16[2,192,256]{2,1,0:T(8,128)(2,1)S(1)} custom-call(s32[2]{0:T(128)S(1)} %pad_add_fusion.slices, bf16[384,1024]{1,0:T(8,128)(2,1)} %copy-done.5, bf16[192,1024]{1,0:T(8,128)(2,1)} %copy-done.6, bf16[192,1024]{1,0:T(8,128)(2,1)} %copy-done.7, bf16[192,1024]{1,0:T(8,128)(2,1)} %copy-done.11, bf16[192,1024]{1,0:T(8,128)(2,1)} %copy-done.10, ...), custom_call_target="tpu_custom_call" | custom-call | flops 402653184 | bytes 1048576 | tf_op jit(solution)/shard_map/last_kv/pallas_call | solution.py:240
  71.8 1.3 %collective-permute-start.14 = (bf16[2,192,256]{2,1,0:T(8,128)(2,1)S(1)}, bf16[2,192,256]{2,1,0:T(8,128)(2,1)S(1)}, u32[]{:S(2)}, u32[]{:S(2)}) collective-permute-start(bf16[2,192,256]{2,1,0:T(8,128)(2,1)S(1)} %last_kv.1.refs_0_), channel_id=1, source_target_pairs={{0,64},{1,65},{2,66},{3,67},{4,68},{5,69},{6,70},{7,71},{8,72},{9,... | collective-permute-start | bytes 589832 | tf_op jit(solution)/shard_map/ppermute | solution.py:46
  74.6 4.7 %last_q.1.queries = bf16[384,1024]{1,0:T(8,128)(2,1)S(1)} custom-call(s32[2]{0:T(128)S(1)} %pad_add_fusion.slices, bf16[384,1024]{1,0:T(8,128)(2,1)} %copy-done.5, bf16[192,1024]{1,0:T(8,128)(2,1)} %copy-done.6, bf16[192,1024]{1,0:T(8,128)(2,1)} %copy-done.7, bf16[192,1024]{1,0:T(8,128)(2,1)} %copy-done.11, bf16[192,1024]{1,0:T(8,128)(2,1)} %copy-done.10, ...), custom_call_target="tpu_custom_call" | custom-call | flops 1610612736 | bytes 4194304 | tf_op jit(solution)/shard_map/last_q/pallas_call | solution.py:296
  79.4 1.9 %collective-permute-start.19 = (bf16[2,192,256]{2,1,0:T(8,128)(2,1)S(1)}, bf16[2,192,256]{2,1,0:T(8,128)(2,1)S(1)}, u32[]{:S(2)}, u32[]{:S(2)}) collective-permute-start(bf16[2,192,256]{2,1,0:T(8,128)(2,1)S(1)} %collective-permute-done.16.refs_0_), channel_id=1, source_target_pairs={{0,64},{1,65},{2,66},{3,67},{4,68},{5,69},{6,70},{7,71},{8,72},{9,... | collective-permute-start | bytes 589832 | tf_op jit(solution)/shard_map/ppermute | solution.py:46
  81.2 2.1 %collective-permute-start.18 = (bf16[2,192,256]{2,1,0:T(8,128)(2,1)S(1)}, bf16[2,192,256]{2,1,0:T(8,128)(2,1)S(1)}, u32[]{:S(2)}, u32[]{:S(2)}) collective-permute-start(bf16[2,192,256]{2,1,0:T(8,128)(2,1)S(1)} %collective-permute-done.16.refs_0_), channel_id=1, source_target_pairs={{0,96},{1,97},{2,98},{3,99},{4,100},{5,101},{6,102},{7,103},{8,104... | collective-permute-start | bytes 589832 | tf_op jit(solution)/shard_map/ppermute | solution.py:46
  84.7 1.3 stitch.10.near
  86.0 5.9 %collective-permute-start.15 = (bf16[8,192,256]{2,1,0:T(8,128)(2,1)S(1)}, bf16[8,192,256]{2,1,0:T(8,128)(2,1)S(1)}, u32[]{:S(2)}, u32[]{:S(2)}) collective-permute-start(bf16[8,192,256]{2,1,0:T(8,128)(2,1)S(1)} %stitch.10.near), channel_id=1, source_target_pairs={{0,8},{1,9},{2,10},{3,11},{4,12},{5,13},{6,14},{7,15},{8,0},{9,1},... | collective-permute-start | bytes 2359304 | tf_op jit(solution)/shard_map/ppermute | solution.py:46
  93.3 1.3 stitch.11.far
  94.6 3.7 %collective-permute-start.20 = (bf16[8,192,256]{2,1,0:T(8,128)(2,1)S(1)}, bf16[8,192,256]{2,1,0:T(8,128)(2,1)S(1)}, u32[]{:S(2)}, u32[]{:S(2)}) collective-permute-start(bf16[8,192,256]{2,1,0:T(8,128)(2,1)S(1)} %stitch.11.far), channel_id=1, source_target_pairs={{0,8},{1,9},{2,10},{3,11},{4,12},{5,13},{6,14},{7,15},{8,0},{9,1},... | collective-permute-start | bytes 2359304 | tf_op jit(solution)/shard_map/ppermute | solution.py:46
  98.3 8.1 %attend.3 = (f32[4,8,768]{2,1,0:T(8,128)S(1)}, f32[4,128,768]{2,1,0:T(8,128)S(1)}) custom-call(s32[32]{0:T(128)S(1)} %concatenate.28.meta, bf16[8,192,256]{2,1,0:T(8,128)(2,1)S(1)} %stitch.10.near, bf16[8,192,256]{2,1,0:T(8,128)(2,1)S(1)} %stitch.11.far, bf16[384,1024]{1,0:T(8,128)(2,1)S(1)} %last_q.1.queries), custom_call_target="tpu_custom_call" | custom-call | flops 3019898880 | bytes 4194304 | tf_op jit(solution)/shard_map/attend/pallas_call | solution.py:462
  106.4 4.7 %attend.4 = (bf16[192,512]{1,0:T(8,128)(2,1)S(1)}, bf16[208,512]{1,0:T(8,128)(2,1)S(1)}) custom-call(s32[32]{0:T(128)S(1)} %concatenate.29.meta, bf16[8,192,256]{2,1,0:T(8,128)(2,1)S(1)} %collective-permute-done.15.near, bf16[8,192,256]{2,1,0:T(8,128)(2,1)S(1)} %collective-permute-done.20.far, bf16[384,1024]{1,0:T(8,128)(2,1)S(1)} %last_q.1.queries, ...), custom_call_target="tpu_custom_call" | custom-call | flops 1509949440 | bytes 4194304 | tf_op jit(solution)/shard_map/attend/pallas_call | solution.py:462
  111.1 1.5 %collective-permute-start.21 = (bf16[208,512]{1,0:T(8,128)(2,1)S(1)}, bf16[208,512]{1,0:T(8,128)(2,1)S(1)}, u32[]{:S(2)}, u32[]{:S(2)}) collective-permute-start(bf16[208,512]{1,0:T(8,128)(2,1)S(1)} %get-tuple-element.53), channel_id=1, source_target_pairs={{0,120},{1,121},{2,122},{3,123},{4,124},{5,125},{6,126},{7,127},{8... | collective-permute-start | bytes 638984 | tf_op jit(solution)/shard_map/ppermute | solution.py:46
  112.6 4.7 %attend.5 = (bf16[192,512]{1,0:T(8,128)(2,1)S(1)}, bf16[192,512]{1,0:T(8,128)(2,1)S(1)}) custom-call(s32[32]{0:T(128)S(1)} %concatenate.29.meta, bf16[8,192,256]{2,1,0:T(8,128)(2,1)S(1)} %collective-permute-done.15.near, bf16[8,192,256]{2,1,0:T(8,128)(2,1)S(1)} %collective-permute-done.20.far, bf16[384,1024]{1,0:T(8,128)(2,1)S(1)} %last_q.1.queries, ...), custom_call_target="tpu_custom_call" | custom-call | flops 1509949440 | bytes 4194304 | tf_op jit(solution)/shard_map/attend/pallas_call | solution.py:462
  117.3 4.2 %collective-permute-start.22 = (bf16[192,512]{1,0:T(8,128)(2,1)S(1)}, bf16[192,512]{1,0:T(8,128)(2,1)S(1)}, u32[]{:S(2)}, u32[]{:S(2)}) collective-permute-start(bf16[192,512]{1,0:T(8,128)(2,1)S(1)} %get-tuple-element.56), channel_id=1, source_target_pairs={{0,120},{1,121},{2,122},{3,123},{4,124},{5,125},{6,126},{7,127},{8... | collective-permute-start | bytes 589832 | tf_op jit(solution)/shard_map/ppermute | solution.py:46
  122.0 6.2 %collective-permute-done.22 = bf16[192,512]{1,0:T(8,128)(2,1)S(1)} collective-permute-done((bf16[192,512]{1,0:T(8,128)(2,1)S(1)}, bf16[192,512]{1,0:T(8,128)(2,1)S(1)}, u32[]{:S(2)}, u32[]{:S(2)}) %collective-permute-start.22) | collective-permute-done | bytes 196640 | tf_op jit(solution)/shard_map/ppermute | solution.py:46
  (90 shorter events, 13.1 us)
Async XLA Ops:
  1.1 13.3 %copy-start.1 = (bf16[192,1024]{1,0:T(8,128)(2,1)}, bf16[192,1024]{1,0:T(8,128)(2,1)S(1)}, u32[]{:S(2)}) copy-start(bf16[192,1024]{1,0:T(8,128)(2,1)S(1)} %get-tuple-element.39.refs_0_) | copy-start | bytes 1179652
  1.1 16.5 %collective-permute-start.2 = (bf16[192,1024]{1,0:T(8,128)(2,1)S(1)}, bf16[192,1024]{1,0:T(8,128)(2,1)S(1)}, u32[]{:S(2)}, u32[]{:S(2)}) collective-permute-start(bf16[192,1024]{1,0:T(8,128)(2,1)S(1)} %get-tuple-element.39.refs_0_), channel_id=1, source_target_pairs={{0,4},{1,5},{2,6},{3,7},{4,0},{5,1},{6,2},{7,3},{8,12},{9,13},{10,... | collective-permute-start | bytes 1179656 | tf_op jit(solution)/shard_map/ppermute | solution.py:46
  3.3 14.3 %collective-permute-start.1 = (bf16[192,1024]{1,0:T(8,128)(2,1)S(1)}, bf16[192,1024]{1,0:T(8,128)(2,1)S(1)}, u32[]{:S(2)}, u32[]{:S(2)}) collective-permute-start(bf16[192,1024]{1,0:T(8,128)(2,1)S(1)} %get-tuple-element.39.refs_0_), channel_id=1, source_target_pairs={{0,3},{1,0},{2,1},{3,2},{4,7},{5,4},{6,5},{7,6},{8,11},{9,8},{10,9... | collective-permute-start | bytes 1179656 | tf_op jit(solution)/shard_map/ppermute | solution.py:46
  7.0 10.6 %collective-permute-start = (bf16[192,1024]{1,0:T(8,128)(2,1)S(1)}, bf16[192,1024]{1,0:T(8,128)(2,1)S(1)}, u32[]{:S(2)}, u32[]{:S(2)}) collective-permute-start(bf16[192,1024]{1,0:T(8,128)(2,1)S(1)} %get-tuple-element.39.refs_0_), channel_id=1, source_target_pairs={{0,1},{1,2},{2,3},{3,0},{4,5},{5,6},{6,7},{7,4},{8,9},{9,10},{10,1... | collective-permute-start | bytes 1179656 | tf_op jit(solution)/shard_map/ppermute | solution.py:46
  7.0 15.1 %collective-permute-start.5 = (bf16[192,1024]{1,0:T(8,128)(2,1)S(1)}, bf16[192,1024]{1,0:T(8,128)(2,1)S(1)}, u32[]{:S(2)}, u32[]{:S(2)}) collective-permute-start(bf16[192,1024]{1,0:T(8,128)(2,1)S(1)} %get-tuple-element.36), channel_id=1, source_target_pairs={{0,124},{1,125},{2,126},{3,127},{4,120},{5,121},{6,122},{7,123},{8... | collective-permute-start | bytes 1179656 | tf_op jit(solution)/shard_map/ppermute | solution.py:46
  20.5 11.7 %collective-permute-start.3 = (bf16[192,1024]{1,0:T(8,128)(2,1)S(1)}, bf16[192,1024]{1,0:T(8,128)(2,1)S(1)}, u32[]{:S(2)}, u32[]{:S(2)}) collective-permute-start(bf16[192,1024]{1,0:T(8,128)(2,1)S(1)} %get-tuple-element.34), channel_id=1, source_target_pairs={{0,1},{1,2},{2,3},{3,0},{4,5},{5,6},{6,7},{7,4},{8,9},{9,10},{10,1... | collective-permute-start | bytes 1179656 | tf_op jit(solution)/shard_map/ppermute | solution.py:46
  22.2 10.0 %copy-start.12 = (bf16[192,1024]{1,0:T(8,128)(2,1)}, bf16[192,1024]{1,0:T(8,128)(2,1)S(1)}, u32[]{:S(2)}) copy-start(bf16[192,1024]{1,0:T(8,128)(2,1)S(1)} %collective-permute-done.5.refs_4_.refs_3_) | copy-start | bytes 1179652
  22.2 10.0 %collective-permute-start.6 = (bf16[192,1024]{1,0:T(8,128)(2,1)S(1)}, bf16[192,1024]{1,0:T(8,128)(2,1)S(1)}, u32[]{:S(2)}, u32[]{:S(2)}) collective-permute-start(bf16[192,1024]{1,0:T(8,128)(2,1)S(1)} %collective-permute-done.5.refs_4_.refs_3_), channel_id=1, source_target_pairs={{0,4},{1,5},{2,6},{3,7},{4,0},{5,1},{6,2},{7,3},{8,12},{9,13},{10,... | collective-permute-start | bytes 1179656 | tf_op jit(solution)/shard_map/ppermute | solution.py:46
  22.2 10.3 %collective-permute-start.4 = (bf16[192,1024]{1,0:T(8,128)(2,1)S(1)}, bf16[192,1024]{1,0:T(8,128)(2,1)S(1)}, u32[]{:S(2)}, u32[]{:S(2)}) collective-permute-start(bf16[192,1024]{1,0:T(8,128)(2,1)S(1)} %get-tuple-element.35), channel_id=1, source_target_pairs={{0,3},{1,0},{2,1},{3,2},{4,7},{5,4},{6,5},{7,6},{8,11},{9,8},{10,9... | collective-permute-start | bytes 1179656 | tf_op jit(solution)/shard_map/ppermute | solution.py:46
  32.2 0.9 copy-start.6
  35.3 19.2 %collective-permute-start.8 = (bf16[384,1024]{1,0:T(8,128)(2,1)S(1)}, bf16[384,1024]{1,0:T(8,128)(2,1)}, u32[]{:S(2)}, u32[]{:S(2)}) collective-permute-start(bf16[384,1024]{1,0:T(8,128)(2,1)S(1)} %get-tuple-element.38), channel_id=1, source_target_pairs={{0,1},{1,2},{2,3},{3,0},{4,5},{5,6},{6,7},{7,4},{8,9},{9,10},{10,1... | collective-permute-start | bytes 2359304 | tf_op jit(solution)/shard_map/ppermute | solution.py:46
  35.4 19.1 %collective-permute-start.9 = (bf16[384,1024]{1,0:T(8,128)(2,1)S(1)}, bf16[384,1024]{1,0:T(8,128)(2,1)}, u32[]{:S(2)}, u32[]{:S(2)}) collective-permute-start(bf16[384,1024]{1,0:T(8,128)(2,1)S(1)} %get-tuple-element.38), channel_id=1, source_target_pairs={{0,3},{1,0},{2,1},{3,2},{4,7},{5,4},{6,5},{7,6},{8,11},{9,8},{10,9... | collective-permute-start | bytes 2359304 | tf_op jit(solution)/shard_map/ppermute | solution.py:46
  38.5 20.0 %collective-permute-start.7 = (bf16[384,1024]{1,0:T(8,128)(2,1)S(1)}, bf16[384,1024]{1,0:T(8,128)(2,1)S(1)}, u32[]{:S(2)}, u32[]{:S(2)}) collective-permute-start(bf16[384,1024]{1,0:T(8,128)(2,1)S(1)} %get-tuple-element.37), channel_id=1, source_target_pairs={{0,4},{1,5},{2,6},{3,7},{4,0},{5,1},{6,2},{7,3},{8,12},{9,13},{10,... | collective-permute-start | bytes 2359304 | tf_op jit(solution)/shard_map/ppermute | solution.py:46
  55.8 11.9 %collective-permute-start.11 = (bf16[192,1024]{1,0:T(8,128)(2,1)S(1)}, bf16[192,1024]{1,0:T(8,128)(2,1)S(1)}, u32[]{:S(2)}, u32[]{:S(2)}) collective-permute-start(bf16[192,1024]{1,0:T(8,128)(2,1)S(1)} %get-tuple-element.42), channel_id=1, source_target_pairs={{0,3},{1,0},{2,1},{3,2},{4,7},{5,4},{6,5},{7,6},{8,11},{9,8},{10,9... | collective-permute-start | bytes 1179656 | tf_op jit(solution)/shard_map/ppermute | solution.py:46
  58.4 9.3 %collective-permute-start.10 = (bf16[192,1024]{1,0:T(8,128)(2,1)S(1)}, bf16[192,1024]{1,0:T(8,128)(2,1)S(1)}, u32[]{:S(2)}, u32[]{:S(2)}) collective-permute-start(bf16[192,1024]{1,0:T(8,128)(2,1)S(1)} %get-tuple-element.41), channel_id=1, source_target_pairs={{0,1},{1,2},{2,3},{3,0},{4,5},{5,6},{6,7},{7,4},{8,9},{9,10},{10,1... | collective-permute-start | bytes 1179656 | tf_op jit(solution)/shard_map/ppermute | solution.py:46
  58.4 10.1 %copy-start.3 = (f32[128]{0:T(128)S(1)}, f32[128]{0:T(128)}, u32[]{:S(2)}) copy-start(f32[128]{0:T(128)} %param.12) | copy-start | bytes 1540
  58.4 10.1 %copy-start.4 = (f32[128]{0:T(128)S(1)}, f32[128]{0:T(128)}, u32[]{:S(2)}) copy-start(f32[128]{0:T(128)} %param.13) | copy-start | bytes 1540
  58.4 0.9 copy-start.5
  68.6 6.0 %copy-start.2 = (f32[1024]{0:T(1024)S(1)}, f32[1024]{0:T(1024)}, u32[]{:S(2)}) copy-start(f32[1024]{0:T(1024)} %param.11) | copy-start | bytes 12292
  71.7 7.7 %copy-start = (bf16[2,192,256]{2,1,0:T(8,128)(2,1)}, bf16[2,192,256]{2,1,0:T(8,128)(2,1)S(1)}, u32[]{:S(2)}) copy-start(bf16[2,192,256]{2,1,0:T(8,128)(2,1)S(1)} %last_kv.1.refs_0_) | copy-start | bytes 589828
  71.7 7.7 %collective-permute-start.16 = (bf16[2,192,256]{2,1,0:T(8,128)(2,1)S(1)}, bf16[2,192,256]{2,1,0:T(8,128)(2,1)S(1)}, u32[]{:S(2)}, u32[]{:S(2)}) collective-permute-start(bf16[2,192,256]{2,1,0:T(8,128)(2,1)S(1)} %last_kv.1.refs_0_), channel_id=1, source_target_pairs={{0,16},{1,17},{2,18},{3,19},{4,20},{5,21},{6,22},{7,23},{8,24},{9,... | collective-permute-start | bytes 589832 | tf_op jit(solution)/shard_map/ppermute | solution.py:46
  71.8 11.5 %collective-permute-start.14 = (bf16[2,192,256]{2,1,0:T(8,128)(2,1)S(1)}, bf16[2,192,256]{2,1,0:T(8,128)(2,1)S(1)}, u32[]{:S(2)}, u32[]{:S(2)}) collective-permute-start(bf16[2,192,256]{2,1,0:T(8,128)(2,1)S(1)} %last_kv.1.refs_0_), channel_id=1, source_target_pairs={{0,64},{1,65},{2,66},{3,67},{4,68},{5,69},{6,70},{7,71},{8,72},{9,... | collective-permute-start | bytes 589832 | tf_op jit(solution)/shard_map/ppermute | solution.py:46
  73.1 10.2 %collective-permute-start.13 = (bf16[2,192,256]{2,1,0:T(8,128)(2,1)S(1)}, bf16[2,192,256]{2,1,0:T(8,128)(2,1)S(1)}, u32[]{:S(2)}, u32[]{:S(2)}) collective-permute-start(bf16[2,192,256]{2,1,0:T(8,128)(2,1)S(1)} %last_kv.1.refs_0_), channel_id=1, source_target_pairs={{0,96},{1,97},{2,98},{3,99},{4,100},{5,101},{6,102},{7,103},{8,104... | collective-permute-start | bytes 589832 | tf_op jit(solution)/shard_map/ppermute | solution.py:46
  74.0 9.3 %collective-permute-start.12 = (bf16[2,192,256]{2,1,0:T(8,128)(2,1)S(1)}, bf16[2,192,256]{2,1,0:T(8,128)(2,1)S(1)}, u32[]{:S(2)}, u32[]{:S(2)}) collective-permute-start(bf16[2,192,256]{2,1,0:T(8,128)(2,1)S(1)} %last_kv.1.refs_0_), channel_id=1, source_target_pairs={{0,32},{1,33},{2,34},{3,35},{4,36},{5,37},{6,38},{7,39},{8,40},{9,... | collective-permute-start | bytes 589832 | tf_op jit(solution)/shard_map/ppermute | solution.py:46
  79.4 12.6 %copy-start.15 = (bf16[2,192,256]{2,1,0:T(8,128)(2,1)}, bf16[2,192,256]{2,1,0:T(8,128)(2,1)S(1)}, u32[]{:S(2)}) copy-start(bf16[2,192,256]{2,1,0:T(8,128)(2,1)S(1)} %collective-permute-done.16.refs_0_) | copy-start | bytes 589828
  79.4 12.5 %collective-permute-start.19 = (bf16[2,192,256]{2,1,0:T(8,128)(2,1)S(1)}, bf16[2,192,256]{2,1,0:T(8,128)(2,1)S(1)}, u32[]{:S(2)}, u32[]{:S(2)}) collective-permute-start(bf16[2,192,256]{2,1,0:T(8,128)(2,1)S(1)} %collective-permute-done.16.refs_0_), channel_id=1, source_target_pairs={{0,64},{1,65},{2,66},{3,67},{4,68},{5,69},{6,70},{7,71},{8,72},{9,... | collective-permute-start | bytes 589832 | tf_op jit(solution)/shard_map/ppermute | solution.py:46
  81.2 10.7 %collective-permute-start.18 = (bf16[2,192,256]{2,1,0:T(8,128)(2,1)S(1)}, bf16[2,192,256]{2,1,0:T(8,128)(2,1)S(1)}, u32[]{:S(2)}, u32[]{:S(2)}) collective-permute-start(bf16[2,192,256]{2,1,0:T(8,128)(2,1)S(1)} %collective-permute-done.16.refs_0_), channel_id=1, source_target_pairs={{0,96},{1,97},{2,98},{3,99},{4,100},{5,101},{6,102},{7,103},{8,104... | collective-permute-start | bytes 589832 | tf_op jit(solution)/shard_map/ppermute | solution.py:46
  83.3 8.6 %collective-permute-start.17 = (bf16[2,192,256]{2,1,0:T(8,128)(2,1)S(1)}, bf16[2,192,256]{2,1,0:T(8,128)(2,1)S(1)}, u32[]{:S(2)}, u32[]{:S(2)}) collective-permute-start(bf16[2,192,256]{2,1,0:T(8,128)(2,1)S(1)} %collective-permute-done.16.refs_0_), channel_id=1, source_target_pairs={{0,32},{1,33},{2,34},{3,35},{4,36},{5,37},{6,38},{7,39},{8,40},{9,... | collective-permute-start | bytes 589832 | tf_op jit(solution)/shard_map/ppermute | solution.py:46
  86.0 20.4 %collective-permute-start.15 = (bf16[8,192,256]{2,1,0:T(8,128)(2,1)S(1)}, bf16[8,192,256]{2,1,0:T(8,128)(2,1)S(1)}, u32[]{:S(2)}, u32[]{:S(2)}) collective-permute-start(bf16[8,192,256]{2,1,0:T(8,128)(2,1)S(1)} %stitch.10.near), channel_id=1, source_target_pairs={{0,8},{1,9},{2,10},{3,11},{4,12},{5,13},{6,14},{7,15},{8,0},{9,1},... | collective-permute-start | bytes 2359304 | tf_op jit(solution)/shard_map/ppermute | solution.py:46
  94.6 11.8 %collective-permute-start.20 = (bf16[8,192,256]{2,1,0:T(8,128)(2,1)S(1)}, bf16[8,192,256]{2,1,0:T(8,128)(2,1)S(1)}, u32[]{:S(2)}, u32[]{:S(2)}) collective-permute-start(bf16[8,192,256]{2,1,0:T(8,128)(2,1)S(1)} %stitch.11.far), channel_id=1, source_target_pairs={{0,8},{1,9},{2,10},{3,11},{4,12},{5,13},{6,14},{7,15},{8,0},{9,1},... | collective-permute-start | bytes 2359304 | tf_op jit(solution)/shard_map/ppermute | solution.py:46
  111.1 10.8 %collective-permute-start.21 = (bf16[208,512]{1,0:T(8,128)(2,1)S(1)}, bf16[208,512]{1,0:T(8,128)(2,1)S(1)}, u32[]{:S(2)}, u32[]{:S(2)}) collective-permute-start(bf16[208,512]{1,0:T(8,128)(2,1)S(1)} %get-tuple-element.53), channel_id=1, source_target_pairs={{0,120},{1,121},{2,122},{3,123},{4,124},{5,125},{6,126},{7,127},{8... | collective-permute-start | bytes 638984 | tf_op jit(solution)/shard_map/ppermute | solution.py:46
  117.3 10.8 %collective-permute-start.22 = (bf16[192,512]{1,0:T(8,128)(2,1)S(1)}, bf16[192,512]{1,0:T(8,128)(2,1)S(1)}, u32[]{:S(2)}, u32[]{:S(2)}) collective-permute-start(bf16[192,512]{1,0:T(8,128)(2,1)S(1)} %get-tuple-element.56), channel_id=1, source_target_pairs={{0,120},{1,121},{2,122},{3,123},{4,124},{5,125},{6,126},{7,127},{8... | collective-permute-start | bytes 589832 | tf_op jit(solution)/shard_map/ppermute | solution.py:46
  (13 other events, 9.7 us)

commit v5 on v4

--- a/solution.py
+++ b/solution.py
@@ -316,7 +316,7 @@
     )(slices, *map(_in_hbm, arrays), w_q, acc, q_bias, cosine, sine)
 
 
-def _stitch(shapes, moves, *operands):
+def _stitch(shapes, moves, *operands, pinned=True):
     def body(*refs):
         sem = refs[-1]
         copies = []
@@ -341,12 +341,12 @@
         scratch_shapes=[pltpu.SemaphoreType.DMA((len(moves),))],
         compiler_params=pltpu.CompilerParams(vmem_limit_bytes=4 * 1024 * 1024),
         name="stitch",
-    )(*map(_in_hbm, operands))
+    )(*(map(_in_hbm, operands) if pinned else operands))
 
 
 def _stack_tiles(arrays):
     moves = [(i, 0, 2, 0, 2 * i) for i in range(4)]
-    return _stitch([(8, HALF, 2 * HEAD)], moves, *arrays)[0]
+    return _stitch([(8, HALF, 2 * HEAD)], moves, *arrays, pinned=False)[0]
 
 
 def _attend_body(first, final, part, meta, near, far, queries, *refs):

time: 129 us -> 128 us (level)
  local copies, waits for them, and re-layouts: 8.07 us -> 5.32 us
    unnamed x44 -> x28, local copies, waits for them, and re-layouts: 7.53 us -> 4.78 us
  transfers between devices with their start and end apart: 23 -> 23, of which waited for: 7 -> 8; matrix products, arithmetic and copies ran while one was open for 2% -> 2% of each run, Pallas kernels for 28% -> 28%
where the time goes in v5:
time: 128 us
  Pallas kernels  46.1 us (36%)
  starting transfers between devices  44.4 us (35%)
  waiting for transfers between devices  28.8 us (22%)
  local copies, waits for them, and re-layouts  5.32 us (4%)
  other arithmetic  2.62 us (2%)
    ppermute x23, starting transfers between devices, _send(): return lax.ppermute(value, AXES, pairs)  44.4 us
    ppermute x23, waiting for transfers between devices, _send(): return lax.ppermute(value, AXES, pairs)  28.8 us
    pallas_call x3, Pallas kernels, _attend(): pl.pallas_call(functools.partial(_attend_body, not states, final, part),...  17.5 us
    pallas_call x2, Pallas kernels, _project(): pl.pallas_call(functools.partial(_proj_body, len(arrays), pieces, acc is...  13.6 us
    pallas_call x6, Pallas kernels, _stitch(): pl.pallas_call(body, out_shape=[jax.ShapeDtypeStruct(shape, jnp.bfloat16)...  7.23 us
    unnamed x28, local copies, waits for them, and re-layouts  4.78 us
    pallas_call x1, Pallas kernels, _last_q(): pl.pallas_call(functools.partial(_last_q_body, len(arrays), pieces), out_...  4.71 us
    pallas_call x1, Pallas kernels, _last_kv(): pl.pallas_call(functools.partial(_last_kv_body, len(arrays), pieces), out...  3.08 us
  transfers between devices with their start and end apart: 23, of which 8 were waited for; matrix products, arithmetic and copies ran while one was open for 2% of the time, Pallas kernels for 28%

profile of v5, /device:TPU:1, one launch (start us, length us, event | category | flops | bytes accessed | tf_op | source)
XLA Modules:
  0.0 127.5 jit_solution(5479497505566238113)
XLA Ops:
  0.0 1.1 stitch.6
  1.1 2.1 %collective-permute-start.2 = (bf16[192,1024]{1,0:T(8,128)(2,1)S(1)}, bf16[192,1024]{1,0:T(8,128)(2,1)S(1)}, u32[]{:S(2)}, u32[]{:S(2)}) collective-permute-start(bf16[192,1024]{1,0:T(8,128)(2,1)S(1)} %get-tuple-element.39.refs_0_), channel_id=1, source_target_pairs={{0,4},{1,5},{2,6},{3,7},{4,0},{5,1},{6,2},{7,3},{8,12},{9,13},{10,... | collective-permute-start | bytes 1179656 | tf_op jit(solution)/shard_map/ppermute | solution.py:46
  3.3 3.8 %collective-permute-start.1 = (bf16[192,1024]{1,0:T(8,128)(2,1)S(1)}, bf16[192,1024]{1,0:T(8,128)(2,1)S(1)}, u32[]{:S(2)}, u32[]{:S(2)}) collective-permute-start(bf16[192,1024]{1,0:T(8,128)(2,1)S(1)} %get-tuple-element.39.refs_0_), channel_id=1, source_target_pairs={{0,3},{1,0},{2,1},{3,2},{4,7},{5,4},{6,5},{7,6},{8,11},{9,8},{10,9... | collective-permute-start | bytes 1179656 | tf_op jit(solution)/shard_map/ppermute | solution.py:46
  7.0 5.4 %collective-permute-start.5 = (bf16[192,1024]{1,0:T(8,128)(2,1)S(1)}, bf16[192,1024]{1,0:T(8,128)(2,1)S(1)}, u32[]{:S(2)}, u32[]{:S(2)}) collective-permute-start(bf16[192,1024]{1,0:T(8,128)(2,1)S(1)} %get-tuple-element.36), channel_id=1, source_target_pairs={{0,124},{1,125},{2,126},{3,127},{4,120},{5,121},{6,122},{7,123},{8... | collective-permute-start | bytes 1179656 | tf_op jit(solution)/shard_map/ppermute | solution.py:46
  14.4 3.2 %collective-permute-done.refs_0_ = bf16[192,1024]{1,0:T(8,128)(2,1)S(1)} collective-permute-done((bf16[192,1024]{1,0:T(8,128)(2,1)S(1)}, bf16[192,1024]{1,0:T(8,128)(2,1)S(1)}, u32[]{:S(2)}, u32[]{:S(2)}) %collective-permute-start) | collective-permute-done | bytes 393248 | tf_op jit(solution)/shard_map/ppermute | solution.py:46
  19.2 1.3 stitch.7
  20.6 1.6 %collective-permute-done.5.refs_4_.refs_3_ = bf16[192,1024]{1,0:T(8,128)(2,1)S(1)} collective-permute-done((bf16[192,1024]{1,0:T(8,128)(2,1)S(1)}, bf16[192,1024]{1,0:T(8,128)(2,1)S(1)}, u32[]{:S(2)}, u32[]{:S(2)}) %collective-permute-start.5) | collective-permute-done | bytes 393248 | tf_op jit(solution)/shard_map/ppermute | solution.py:46
  22.2 3.0 %collective-permute-start.4 = (bf16[192,1024]{1,0:T(8,128)(2,1)S(1)}, bf16[192,1024]{1,0:T(8,128)(2,1)S(1)}, u32[]{:S(2)}, u32[]{:S(2)}) collective-permute-start(bf16[192,1024]{1,0:T(8,128)(2,1)S(1)} %get-tuple-element.35), channel_id=1, source_target_pairs={{0,3},{1,0},{2,1},{3,2},{4,7},{5,4},{6,5},{7,6},{8,11},{9,8},{10,9... | collective-permute-start | bytes 1179656 | tf_op jit(solution)/shard_map/ppermute | solution.py:46
  25.1 7.0 %collective-permute-done.6.refs_5_.refs_1_ = bf16[192,1024]{1,0:T(8,128)(2,1)S(1)} collective-permute-done((bf16[192,1024]{1,0:T(8,128)(2,1)S(1)}, bf16[192,1024]{1,0:T(8,128)(2,1)S(1)}, u32[]{:S(2)}, u32[]{:S(2)}) %collective-permute-start.6) | collective-permute-done | bytes 393248 | tf_op jit(solution)/shard_map/ppermute | solution.py:46
  33.8 1.5 %stitch.8 = (bf16[384,1024]{1,0:T(8,128)(2,1)S(1)}, bf16[384,1024]{1,0:T(8,128)(2,1)S(1)}) custom-call(bf16[192,1024]{1,0:T(8,128)(2,1)} %copy-done.8, bf16[192,1024]{1,0:T(8,128)(2,1)} %copy-done.7, bf16[192,1024]{1,0:T(8,128)(2,1)} %copy-done.5, bf16[192,1024]{1,0:T(8,128)(2,1)} %copy-done.6, bf16[192,1024]{1,0:T(8,128)(2,1)} %copy-done.11, ...), custom_call_target="tpu_custom_call" | custom-call | tf_op jit(solution)/shard_map/stitch/pallas_call | solution.py:336
  35.4 3.1 %collective-permute-start.9 = (bf16[384,1024]{1,0:T(8,128)(2,1)S(1)}, bf16[384,1024]{1,0:T(8,128)(2,1)}, u32[]{:S(2)}, u32[]{:S(2)}) collective-permute-start(bf16[384,1024]{1,0:T(8,128)(2,1)S(1)} %get-tuple-element.38), channel_id=1, source_target_pairs={{0,3},{1,0},{2,1},{3,2},{4,7},{5,4},{6,5},{7,6},{8,11},{9,8},{10,9... | collective-permute-start | bytes 2359304 | tf_op jit(solution)/shard_map/ppermute | solution.py:46
  38.5 1.5 %collective-permute-start.7 = (bf16[384,1024]{1,0:T(8,128)(2,1)S(1)}, bf16[384,1024]{1,0:T(8,128)(2,1)S(1)}, u32[]{:S(2)}, u32[]{:S(2)}) collective-permute-start(bf16[384,1024]{1,0:T(8,128)(2,1)S(1)} %get-tuple-element.37), channel_id=1, source_target_pairs={{0,4},{1,5},{2,6},{3,7},{4,0},{5,1},{6,2},{7,3},{8,12},{9,13},{10,... | collective-permute-start | bytes 2359304 | tf_op jit(solution)/shard_map/ppermute | solution.py:46
  40.1 5.2 %project.2.refs_10_ = f32[384,1280]{1,0:T(8,128)S(1)} custom-call(s32[2]{0:T(128)S(1)} %pad_add_fusion.1.slices, bf16[192,1024]{1,0:T(8,128)(2,1)} %copy-done, bf16[192,1024]{1,0:T(8,128)(2,1)} %copy-done.12, bf16[192,1024]{1,0:T(8,128)(2,1)} %copy-done.13, bf16[192,1024]{1,0:T(8,128)(2,1)} %copy-done.11, bf16[8192,1024]{1,0:T(8,128)(2,1)} %refs_5_.5, ...), custom_call_target="tpu_custom_call" | custom-call | flops 2013265920 | bytes 5242880 | tf_op jit(solution)/shard_map/project/pallas_call | solution.py:184
  45.4 9.2 %collective-permute-done.8.refs_0_.refs_5_ = bf16[384,1024]{1,0:T(8,128)(2,1)} collective-permute-done((bf16[384,1024]{1,0:T(8,128)(2,1)S(1)}, bf16[384,1024]{1,0:T(8,128)(2,1)}, u32[]{:S(2)}, u32[]{:S(2)}) %collective-permute-start.8) | collective-permute-done | bytes 786464 | tf_op jit(solution)/shard_map/ppermute | solution.py:46
  54.6 1.3 stitch.9
  55.8 2.5 %collective-permute-start.11 = (bf16[192,1024]{1,0:T(8,128)(2,1)S(1)}, bf16[192,1024]{1,0:T(8,128)(2,1)S(1)}, u32[]{:S(2)}, u32[]{:S(2)}) collective-permute-start(bf16[192,1024]{1,0:T(8,128)(2,1)S(1)} %get-tuple-element.42), channel_id=1, source_target_pairs={{0,3},{1,0},{2,1},{3,2},{4,7},{5,4},{6,5},{7,6},{8,11},{9,8},{10,9... | collective-permute-start | bytes 1179656 | tf_op jit(solution)/shard_map/ppermute | solution.py:46
  59.3 8.3 %project.3.refs_7_.refs_6_ = f32[384,1280]{1,0:T(8,128)S(1)} custom-call(s32[4]{0:T(128)S(1)} %pad_add_fusion.2.slices, bf16[192,1024]{1,0:T(8,128)(2,1)} %copy-done.8, bf16[192,1024]{1,0:T(8,128)(2,1)} %copy-done.7, bf16[192,1024]{1,0:T(8,128)(2,1)} %copy-done.5, bf16[192,1024]{1,0:T(8,128)(2,1)} %copy-done.6, bf16[384,1024]{1,0:T(8,128)(2,1)} %copy-done.4, ...), custom_call_target="tpu_custom_call" | custom-call | flops 4026531840 | bytes 10485760 | tf_op jit(solution)/shard_map/project/pallas_call | solution.py:184
  68.6 3.1 %last_kv.1.refs_0_ = bf16[2,192,256]{2,1,0:T(8,128)(2,1)S(1)} custom-call(s32[2]{0:T(128)S(1)} %pad_add_fusion.slices, bf16[384,1024]{1,0:T(8,128)(2,1)} %copy-done.4, bf16[192,1024]{1,0:T(8,128)(2,1)} %copy-done.5, bf16[192,1024]{1,0:T(8,128)(2,1)} %copy-done.6, bf16[192,1024]{1,0:T(8,128)(2,1)} %copy-done.10, bf16[192,1024]{1,0:T(8,128)(2,1)} %copy-done.9, ...), custom_call_target="tpu_custom_call" | custom-call | flops 402653184 | bytes 1048576 | tf_op jit(solution)/shard_map/last_kv/pallas_call | solution.py:240
  71.8 1.3 %collective-permute-start.14 = (bf16[2,192,256]{2,1,0:T(8,128)(2,1)S(1)}, bf16[2,192,256]{2,1,0:T(8,128)(2,1)S(1)}, u32[]{:S(2)}, u32[]{:S(2)}) collective-permute-start(bf16[2,192,256]{2,1,0:T(8,128)(2,1)S(1)} %last_kv.1.refs_0_), channel_id=1, source_target_pairs={{0,64},{1,65},{2,66},{3,67},{4,68},{5,69},{6,70},{7,71},{8,72},{9,... | collective-permute-start | bytes 589832 | tf_op jit(solution)/shard_map/ppermute | solution.py:46
  74.6 4.7 %last_q.1.queries = bf16[384,1024]{1,0:T(8,128)(2,1)S(1)} custom-call(s32[2]{0:T(128)S(1)} %pad_add_fusion.slices, bf16[384,1024]{1,0:T(8,128)(2,1)} %copy-done.4, bf16[192,1024]{1,0:T(8,128)(2,1)} %copy-done.5, bf16[192,1024]{1,0:T(8,128)(2,1)} %copy-done.6, bf16[192,1024]{1,0:T(8,128)(2,1)} %copy-done.10, bf16[192,1024]{1,0:T(8,128)(2,1)} %copy-done.9, ...), custom_call_target="tpu_custom_call" | custom-call | flops 1610612736 | bytes 4194304 | tf_op jit(solution)/shard_map/last_q/pallas_call | solution.py:296
  79.3 1.9 %collective-permute-start.19 = (bf16[2,192,256]{2,1,0:T(8,128)(2,1)S(1)}, bf16[2,192,256]{2,1,0:T(8,128)(2,1)S(1)}, u32[]{:S(2)}, u32[]{:S(2)}) collective-permute-start(bf16[2,192,256]{2,1,0:T(8,128)(2,1)S(1)} %collective-permute-done.16.refs_0_), channel_id=1, source_target_pairs={{0,64},{1,65},{2,66},{3,67},{4,68},{5,69},{6,70},{7,71},{8,72},{9,... | collective-permute-start | bytes 589832 | tf_op jit(solution)/shard_map/ppermute | solution.py:46
  81.2 2.1 %collective-permute-start.18 = (bf16[2,192,256]{2,1,0:T(8,128)(2,1)S(1)}, bf16[2,192,256]{2,1,0:T(8,128)(2,1)S(1)}, u32[]{:S(2)}, u32[]{:S(2)}) collective-permute-start(bf16[2,192,256]{2,1,0:T(8,128)(2,1)S(1)} %collective-permute-done.16.refs_0_), channel_id=1, source_target_pairs={{0,96},{1,97},{2,98},{3,99},{4,100},{5,101},{6,102},{7,103},{8,104... | collective-permute-start | bytes 589832 | tf_op jit(solution)/shard_map/ppermute | solution.py:46
  83.3 1.1 stitch.10.near
  84.3 5.9 %collective-permute-start.15 = (bf16[8,192,256]{2,1,0:T(8,128)(2,1)S(1)}, bf16[8,192,256]{2,1,0:T(8,128)(2,1)S(1)}, u32[]{:S(2)}, u32[]{:S(2)}) collective-permute-start(bf16[8,192,256]{2,1,0:T(8,128)(2,1)S(1)} %stitch.10.near), channel_id=1, source_target_pairs={{0,8},{1,9},{2,10},{3,11},{4,12},{5,13},{6,14},{7,15},{8,0},{9,1},... | collective-permute-start | bytes 2359304 | tf_op jit(solution)/shard_map/ppermute | solution.py:46
  90.3 1.6 %collective-permute-done.17.refs_1_ = bf16[2,192,256]{2,1,0:T(8,128)(2,1)S(1)} collective-permute-done((bf16[2,192,256]{2,1,0:T(8,128)(2,1)S(1)}, bf16[2,192,256]{2,1,0:T(8,128)(2,1)S(1)}, u32[]{:S(2)}, u32[]{:S(2)}) %collective-permute-start.17) | collective-permute-done | bytes 196640 | tf_op jit(solution)/shard_map/ppermute | solution.py:46
  91.9 1.0 stitch.11.far
  92.9 4.4 %collective-permute-start.20 = (bf16[8,192,256]{2,1,0:T(8,128)(2,1)S(1)}, bf16[8,192,256]{2,1,0:T(8,128)(2,1)S(1)}, u32[]{:S(2)}, u32[]{:S(2)}) collective-permute-start(bf16[8,192,256]{2,1,0:T(8,128)(2,1)S(1)} %stitch.11.far), channel_id=1, source_target_pairs={{0,8},{1,9},{2,10},{3,11},{4,12},{5,13},{6,14},{7,15},{8,0},{9,1},... | collective-permute-start | bytes 2359304 | tf_op jit(solution)/shard_map/ppermute | solution.py:46
  97.3 8.1 %attend.3 = (f32[4,8,768]{2,1,0:T(8,128)S(1)}, f32[4,128,768]{2,1,0:T(8,128)S(1)}) custom-call(s32[32]{0:T(128)S(1)} %concatenate.28.meta, bf16[8,192,256]{2,1,0:T(8,128)(2,1)S(1)} %stitch.10.near, bf16[8,192,256]{2,1,0:T(8,128)(2,1)S(1)} %stitch.11.far, bf16[384,1024]{1,0:T(8,128)(2,1)S(1)} %last_q.1.queries), custom_call_target="tpu_custom_call" | custom-call | flops 3019898880 | bytes 4194304 | tf_op jit(solution)/shard_map/attend/pallas_call | solution.py:462
  105.5 4.7 %attend.4 = (bf16[192,512]{1,0:T(8,128)(2,1)S(1)}, bf16[208,512]{1,0:T(8,128)(2,1)S(1)}) custom-call(s32[32]{0:T(128)S(1)} %concatenate.29.meta, bf16[8,192,256]{2,1,0:T(8,128)(2,1)S(1)} %collective-permute-done.15.near, bf16[8,192,256]{2,1,0:T(8,128)(2,1)S(1)} %collective-permute-done.20.far, bf16[384,1024]{1,0:T(8,128)(2,1)S(1)} %last_q.1.queries, ...), custom_call_target="tpu_custom_call" | custom-call | flops 1509949440 | bytes 4194304 | tf_op jit(solution)/shard_map/attend/pallas_call | solution.py:462
  111.1 4.7 %attend.5 = (bf16[192,512]{1,0:T(8,128)(2,1)S(1)}, bf16[192,512]{1,0:T(8,128)(2,1)S(1)}) custom-call(s32[32]{0:T(128)S(1)} %concatenate.29.meta, bf16[8,192,256]{2,1,0:T(8,128)(2,1)S(1)} %collective-permute-done.15.near, bf16[8,192,256]{2,1,0:T(8,128)(2,1)S(1)} %collective-permute-done.20.far, bf16[384,1024]{1,0:T(8,128)(2,1)S(1)} %last_q.1.queries, ...), custom_call_target="tpu_custom_call" | custom-call | flops 1509949440 | bytes 4194304 | tf_op jit(solution)/shard_map/attend/pallas_call | solution.py:462
  115.7 4.9 %collective-permute-start.22 = (bf16[192,512]{1,0:T(8,128)(2,1)S(1)}, bf16[192,512]{1,0:T(8,128)(2,1)S(1)}, u32[]{:S(2)}, u32[]{:S(2)}) collective-permute-start(bf16[192,512]{1,0:T(8,128)(2,1)S(1)} %get-tuple-element.56), channel_id=1, source_target_pairs={{0,120},{1,121},{2,122},{3,123},{4,124},{5,125},{6,126},{7,127},{8... | collective-permute-start | bytes 589832 | tf_op jit(solution)/shard_map/ppermute | solution.py:46
  121.0 5.5 %collective-permute-done.22 = bf16[192,512]{1,0:T(8,128)(2,1)S(1)} collective-permute-done((bf16[192,512]{1,0:T(8,128)(2,1)S(1)}, bf16[192,512]{1,0:T(8,128)(2,1)S(1)}, u32[]{:S(2)}, u32[]{:S(2)}) %collective-permute-start.22) | collective-permute-done | bytes 196640 | tf_op jit(solution)/shard_map/ppermute | solution.py:46
  (74 shorter events, 11.2 us)
Async XLA Ops:
  1.1 13.3 %copy-start = (bf16[192,1024]{1,0:T(8,128)(2,1)}, bf16[192,1024]{1,0:T(8,128)(2,1)S(1)}, u32[]{:S(2)}) copy-start(bf16[192,1024]{1,0:T(8,128)(2,1)S(1)} %get-tuple-element.39.refs_0_) | copy-start | bytes 1179652
  1.1 16.5 %collective-permute-start.2 = (bf16[192,1024]{1,0:T(8,128)(2,1)S(1)}, bf16[192,1024]{1,0:T(8,128)(2,1)S(1)}, u32[]{:S(2)}, u32[]{:S(2)}) collective-permute-start(bf16[192,1024]{1,0:T(8,128)(2,1)S(1)} %get-tuple-element.39.refs_0_), channel_id=1, source_target_pairs={{0,4},{1,5},{2,6},{3,7},{4,0},{5,1},{6,2},{7,3},{8,12},{9,13},{10,... | collective-permute-start | bytes 1179656 | tf_op jit(solution)/shard_map/ppermute | solution.py:46
  3.3 14.3 %collective-permute-start.1 = (bf16[192,1024]{1,0:T(8,128)(2,1)S(1)}, bf16[192,1024]{1,0:T(8,128)(2,1)S(1)}, u32[]{:S(2)}, u32[]{:S(2)}) collective-permute-start(bf16[192,1024]{1,0:T(8,128)(2,1)S(1)} %get-tuple-element.39.refs_0_), channel_id=1, source_target_pairs={{0,3},{1,0},{2,1},{3,2},{4,7},{5,4},{6,5},{7,6},{8,11},{9,8},{10,9... | collective-permute-start | bytes 1179656 | tf_op jit(solution)/shard_map/ppermute | solution.py:46
  7.0 10.6 %collective-permute-start = (bf16[192,1024]{1,0:T(8,128)(2,1)S(1)}, bf16[192,1024]{1,0:T(8,128)(2,1)S(1)}, u32[]{:S(2)}, u32[]{:S(2)}) collective-permute-start(bf16[192,1024]{1,0:T(8,128)(2,1)S(1)} %get-tuple-element.39.refs_0_), channel_id=1, source_target_pairs={{0,1},{1,2},{2,3},{3,0},{4,5},{5,6},{6,7},{7,4},{8,9},{9,10},{10,1... | collective-permute-start | bytes 1179656 | tf_op jit(solution)/shard_map/ppermute | solution.py:46
  7.0 15.1 %collective-permute-start.5 = (bf16[192,1024]{1,0:T(8,128)(2,1)S(1)}, bf16[192,1024]{1,0:T(8,128)(2,1)S(1)}, u32[]{:S(2)}, u32[]{:S(2)}) collective-permute-start(bf16[192,1024]{1,0:T(8,128)(2,1)S(1)} %get-tuple-element.36), channel_id=1, source_target_pairs={{0,124},{1,125},{2,126},{3,127},{4,120},{5,121},{6,122},{7,123},{8... | collective-permute-start | bytes 1179656 | tf_op jit(solution)/shard_map/ppermute | solution.py:46
  17.6 0.9 copy-start.13
  20.5 11.6 %collective-permute-start.3 = (bf16[192,1024]{1,0:T(8,128)(2,1)S(1)}, bf16[192,1024]{1,0:T(8,128)(2,1)S(1)}, u32[]{:S(2)}, u32[]{:S(2)}) collective-permute-start(bf16[192,1024]{1,0:T(8,128)(2,1)S(1)} %get-tuple-element.34), channel_id=1, source_target_pairs={{0,1},{1,2},{2,3},{3,0},{4,5},{5,6},{6,7},{7,4},{8,9},{9,10},{10,1... | collective-permute-start | bytes 1179656 | tf_op jit(solution)/shard_map/ppermute | solution.py:46
  22.2 10.0 %copy-start.11 = (bf16[192,1024]{1,0:T(8,128)(2,1)}, bf16[192,1024]{1,0:T(8,128)(2,1)S(1)}, u32[]{:S(2)}) copy-start(bf16[192,1024]{1,0:T(8,128)(2,1)S(1)} %collective-permute-done.5.refs_4_.refs_3_) | copy-start | bytes 1179652
  22.2 10.0 %collective-permute-start.6 = (bf16[192,1024]{1,0:T(8,128)(2,1)S(1)}, bf16[192,1024]{1,0:T(8,128)(2,1)S(1)}, u32[]{:S(2)}, u32[]{:S(2)}) collective-permute-start(bf16[192,1024]{1,0:T(8,128)(2,1)S(1)} %collective-permute-done.5.refs_4_.refs_3_), channel_id=1, source_target_pairs={{0,4},{1,5},{2,6},{3,7},{4,0},{5,1},{6,2},{7,3},{8,12},{9,13},{10,... | collective-permute-start | bytes 1179656 | tf_op jit(solution)/shard_map/ppermute | solution.py:46
  22.2 10.2 %collective-permute-start.4 = (bf16[192,1024]{1,0:T(8,128)(2,1)S(1)}, bf16[192,1024]{1,0:T(8,128)(2,1)S(1)}, u32[]{:S(2)}, u32[]{:S(2)}) collective-permute-start(bf16[192,1024]{1,0:T(8,128)(2,1)S(1)} %get-tuple-element.35), channel_id=1, source_target_pairs={{0,3},{1,0},{2,1},{3,2},{4,7},{5,4},{6,5},{7,6},{8,11},{9,8},{10,9... | collective-permute-start | bytes 1179656 | tf_op jit(solution)/shard_map/ppermute | solution.py:46
  32.1 0.9 copy-start.5
  35.3 19.2 %collective-permute-start.8 = (bf16[384,1024]{1,0:T(8,128)(2,1)S(1)}, bf16[384,1024]{1,0:T(8,128)(2,1)}, u32[]{:S(2)}, u32[]{:S(2)}) collective-permute-start(bf16[384,1024]{1,0:T(8,128)(2,1)S(1)} %get-tuple-element.38), channel_id=1, source_target_pairs={{0,1},{1,2},{2,3},{3,0},{4,5},{5,6},{6,7},{7,4},{8,9},{9,10},{10,1... | collective-permute-start | bytes 2359304 | tf_op jit(solution)/shard_map/ppermute | solution.py:46
  35.4 19.2 %collective-permute-start.9 = (bf16[384,1024]{1,0:T(8,128)(2,1)S(1)}, bf16[384,1024]{1,0:T(8,128)(2,1)}, u32[]{:S(2)}, u32[]{:S(2)}) collective-permute-start(bf16[384,1024]{1,0:T(8,128)(2,1)S(1)} %get-tuple-element.38), channel_id=1, source_target_pairs={{0,3},{1,0},{2,1},{3,2},{4,7},{5,4},{6,5},{7,6},{8,11},{9,8},{10,9... | collective-permute-start | bytes 2359304 | tf_op jit(solution)/shard_map/ppermute | solution.py:46
  38.5 20.0 %collective-permute-start.7 = (bf16[384,1024]{1,0:T(8,128)(2,1)S(1)}, bf16[384,1024]{1,0:T(8,128)(2,1)S(1)}, u32[]{:S(2)}, u32[]{:S(2)}) collective-permute-start(bf16[384,1024]{1,0:T(8,128)(2,1)S(1)} %get-tuple-element.37), channel_id=1, source_target_pairs={{0,4},{1,5},{2,6},{3,7},{4,0},{5,1},{6,2},{7,3},{8,12},{9,13},{10,... | collective-permute-start | bytes 2359304 | tf_op jit(solution)/shard_map/ppermute | solution.py:46
  55.8 11.9 %collective-permute-start.11 = (bf16[192,1024]{1,0:T(8,128)(2,1)S(1)}, bf16[192,1024]{1,0:T(8,128)(2,1)S(1)}, u32[]{:S(2)}, u32[]{:S(2)}) collective-permute-start(bf16[192,1024]{1,0:T(8,128)(2,1)S(1)} %get-tuple-element.42), channel_id=1, source_target_pairs={{0,3},{1,0},{2,1},{3,2},{4,7},{5,4},{6,5},{7,6},{8,11},{9,8},{10,9... | collective-permute-start | bytes 1179656 | tf_op jit(solution)/shard_map/ppermute | solution.py:46
  58.4 9.3 %collective-permute-start.10 = (bf16[192,1024]{1,0:T(8,128)(2,1)S(1)}, bf16[192,1024]{1,0:T(8,128)(2,1)S(1)}, u32[]{:S(2)}, u32[]{:S(2)}) collective-permute-start(bf16[192,1024]{1,0:T(8,128)(2,1)S(1)} %get-tuple-element.41), channel_id=1, source_target_pairs={{0,1},{1,2},{2,3},{3,0},{4,5},{5,6},{6,7},{7,4},{8,9},{9,10},{10,1... | collective-permute-start | bytes 1179656 | tf_op jit(solution)/shard_map/ppermute | solution.py:46
  58.4 10.2 %copy-start.2 = (f32[128]{0:T(128)S(1)}, f32[128]{0:T(128)}, u32[]{:S(2)}) copy-start(f32[128]{0:T(128)} %param.12) | copy-start | bytes 1540
  58.4 10.2 %copy-start.3 = (f32[128]{0:T(128)S(1)}, f32[128]{0:T(128)}, u32[]{:S(2)}) copy-start(f32[128]{0:T(128)} %param.13) | copy-start | bytes 1540
  58.5 0.9 copy-start.4
  67.7 0.9 copy-start.10
  68.6 6.0 %copy-start.1 = (f32[1024]{0:T(1024)S(1)}, f32[1024]{0:T(1024)}, u32[]{:S(2)}) copy-start(f32[1024]{0:T(1024)} %param.11) | copy-start | bytes 12292
  71.7 7.6 %collective-permute-start.16 = (bf16[2,192,256]{2,1,0:T(8,128)(2,1)S(1)}, bf16[2,192,256]{2,1,0:T(8,128)(2,1)S(1)}, u32[]{:S(2)}, u32[]{:S(2)}) collective-permute-start(bf16[2,192,256]{2,1,0:T(8,128)(2,1)S(1)} %last_kv.1.refs_0_), channel_id=1, source_target_pairs={{0,16},{1,17},{2,18},{3,19},{4,20},{5,21},{6,22},{7,23},{8,24},{9,... | collective-permute-start | bytes 589832 | tf_op jit(solution)/shard_map/ppermute | solution.py:46
  71.8 11.5 %collective-permute-start.14 = (bf16[2,192,256]{2,1,0:T(8,128)(2,1)S(1)}, bf16[2,192,256]{2,1,0:T(8,128)(2,1)S(1)}, u32[]{:S(2)}, u32[]{:S(2)}) collective-permute-start(bf16[2,192,256]{2,1,0:T(8,128)(2,1)S(1)} %last_kv.1.refs_0_), channel_id=1, source_target_pairs={{0,64},{1,65},{2,66},{3,67},{4,68},{5,69},{6,70},{7,71},{8,72},{9,... | collective-permute-start | bytes 589832 | tf_op jit(solution)/shard_map/ppermute | solution.py:46
  73.1 10.2 %collective-permute-start.13 = (bf16[2,192,256]{2,1,0:T(8,128)(2,1)S(1)}, bf16[2,192,256]{2,1,0:T(8,128)(2,1)S(1)}, u32[]{:S(2)}, u32[]{:S(2)}) collective-permute-start(bf16[2,192,256]{2,1,0:T(8,128)(2,1)S(1)} %last_kv.1.refs_0_), channel_id=1, source_target_pairs={{0,96},{1,97},{2,98},{3,99},{4,100},{5,101},{6,102},{7,103},{8,104... | collective-permute-start | bytes 589832 | tf_op jit(solution)/shard_map/ppermute | solution.py:46
  74.0 9.3 %collective-permute-start.12 = (bf16[2,192,256]{2,1,0:T(8,128)(2,1)S(1)}, bf16[2,192,256]{2,1,0:T(8,128)(2,1)S(1)}, u32[]{:S(2)}, u32[]{:S(2)}) collective-permute-start(bf16[2,192,256]{2,1,0:T(8,128)(2,1)S(1)} %last_kv.1.refs_0_), channel_id=1, source_target_pairs={{0,32},{1,33},{2,34},{3,35},{4,36},{5,37},{6,38},{7,39},{8,40},{9,... | collective-permute-start | bytes 589832 | tf_op jit(solution)/shard_map/ppermute | solution.py:46
  79.3 11.0 %collective-permute-start.19 = (bf16[2,192,256]{2,1,0:T(8,128)(2,1)S(1)}, bf16[2,192,256]{2,1,0:T(8,128)(2,1)S(1)}, u32[]{:S(2)}, u32[]{:S(2)}) collective-permute-start(bf16[2,192,256]{2,1,0:T(8,128)(2,1)S(1)} %collective-permute-done.16.refs_0_), channel_id=1, source_target_pairs={{0,64},{1,65},{2,66},{3,67},{4,68},{5,69},{6,70},{7,71},{8,72},{9,... | collective-permute-start | bytes 589832 | tf_op jit(solution)/shard_map/ppermute | solution.py:46
  81.2 9.1 %collective-permute-start.18 = (bf16[2,192,256]{2,1,0:T(8,128)(2,1)S(1)}, bf16[2,192,256]{2,1,0:T(8,128)(2,1)S(1)}, u32[]{:S(2)}, u32[]{:S(2)}) collective-permute-start(bf16[2,192,256]{2,1,0:T(8,128)(2,1)S(1)} %collective-permute-done.16.refs_0_), channel_id=1, source_target_pairs={{0,96},{1,97},{2,98},{3,99},{4,100},{5,101},{6,102},{7,103},{8,104... | collective-permute-start | bytes 589832 | tf_op jit(solution)/shard_map/ppermute | solution.py:46
  83.3 8.6 %collective-permute-start.17 = (bf16[2,192,256]{2,1,0:T(8,128)(2,1)S(1)}, bf16[2,192,256]{2,1,0:T(8,128)(2,1)S(1)}, u32[]{:S(2)}, u32[]{:S(2)}) collective-permute-start(bf16[2,192,256]{2,1,0:T(8,128)(2,1)S(1)} %collective-permute-done.16.refs_0_), channel_id=1, source_target_pairs={{0,32},{1,33},{2,34},{3,35},{4,36},{5,37},{6,38},{7,39},{8,40},{9,... | collective-permute-start | bytes 589832 | tf_op jit(solution)/shard_map/ppermute | solution.py:46
  84.3 21.1 %collective-permute-start.15 = (bf16[8,192,256]{2,1,0:T(8,128)(2,1)S(1)}, bf16[8,192,256]{2,1,0:T(8,128)(2,1)S(1)}, u32[]{:S(2)}, u32[]{:S(2)}) collective-permute-start(bf16[8,192,256]{2,1,0:T(8,128)(2,1)S(1)} %stitch.10.near), channel_id=1, source_target_pairs={{0,8},{1,9},{2,10},{3,11},{4,12},{5,13},{6,14},{7,15},{8,0},{9,1},... | collective-permute-start | bytes 2359304 | tf_op jit(solution)/shard_map/ppermute | solution.py:46
  92.9 12.6 %collective-permute-start.20 = (bf16[8,192,256]{2,1,0:T(8,128)(2,1)S(1)}, bf16[8,192,256]{2,1,0:T(8,128)(2,1)S(1)}, u32[]{:S(2)}, u32[]{:S(2)}) collective-permute-start(bf16[8,192,256]{2,1,0:T(8,128)(2,1)S(1)} %stitch.11.far), channel_id=1, source_target_pairs={{0,8},{1,9},{2,10},{3,11},{4,12},{5,13},{6,14},{7,15},{8,0},{9,1},... | collective-permute-start | bytes 2359304 | tf_op jit(solution)/shard_map/ppermute | solution.py:46
  110.2 10.8 %collective-permute-start.21 = (bf16[208,512]{1,0:T(8,128)(2,1)S(1)}, bf16[208,512]{1,0:T(8,128)(2,1)S(1)}, u32[]{:S(2)}, u32[]{:S(2)}) collective-permute-start(bf16[208,512]{1,0:T(8,128)(2,1)S(1)} %get-tuple-element.53), channel_id=1, source_target_pairs={{0,120},{1,121},{2,122},{3,123},{4,124},{5,125},{6,126},{7,127},{8... | collective-permute-start | bytes 638984 | tf_op jit(solution)/shard_map/ppermute | solution.py:46
  115.7 10.8 %collective-permute-start.22 = (bf16[192,512]{1,0:T(8,128)(2,1)S(1)}, bf16[192,512]{1,0:T(8,128)(2,1)S(1)}, u32[]{:S(2)}, u32[]{:S(2)}) collective-permute-start(bf16[192,512]{1,0:T(8,128)(2,1)S(1)} %get-tuple-element.56), channel_id=1, source_target_pairs={{0,120},{1,121},{2,122},{3,123},{4,124},{5,125},{6,126},{7,127},{8... | collective-permute-start | bytes 589832 | tf_op jit(solution)/shard_map/ppermute | solution.py:46
  (5 other events, 3.8 us)

commit v6 on v5

--- a/solution.py
+++ b/solution.py
@@ -565,6 +565,7 @@
         up,
         down,
         side,
+        pinned=False,
     )
     from_down, from_up = _send(to_up, z_up), _send(to_down, z_down)
     late_side = _send(late, x_near)

time: 128 us -> 129 us (level)
  waiting for transfers between devices: 28.8 us -> 32 us
    ppermute x23, waiting for transfers between devices: 28.8 us -> 32 us  [_send(): return lax.ppermute(value, AXES, pairs)]
    unnamed x28 -> x30, local copies, waits for them, and re-layouts: 4.78 us -> 3.55 us
where the time goes in v6:
time: 129 us
  Pallas kernels  45.9 us (36%)
  starting transfers between devices  43.7 us (34%)
  waiting for transfers between devices  32 us (25%)
  local copies, waits for them, and re-layouts  4.09 us (3%)
  other arithmetic  2.62 us (2%)
    ppermute x23, starting transfers between devices, _send(): return lax.ppermute(value, AXES, pairs)  43.7 us
    ppermute x23, waiting for transfers between devices, _send(): return lax.ppermute(value, AXES, pairs)  32 us
    pallas_call x3, Pallas kernels, _attend(): pl.pallas_call(functools.partial(_attend_body, not states, final, part),...  17.5 us
    pallas_call x2, Pallas kernels, _project(): pl.pallas_call(functools.partial(_proj_body, len(arrays), pieces, acc is...  13.6 us
    pallas_call x6, Pallas kernels, _stitch(): pl.pallas_call(body, out_shape=[jax.ShapeDtypeStruct(shape, jnp.bfloat16)...  7.04 us
    pallas_call x1, Pallas kernels, _last_q(): pl.pallas_call(functools.partial(_last_q_body, len(arrays), pieces), out_...  4.71 us
    unnamed x30, local copies, waits for them, and re-layouts  3.55 us
    pallas_call x1, Pallas kernels, _last_kv(): pl.pallas_call(functools.partial(_last_kv_body, len(arrays), pieces), out...  3.08 us
  transfers between devices with their start and end apart: 23, of which 8 were waited for; matrix products, arithmetic and copies ran while one was open for 2% of the time, Pallas kernels for 28%

profile of v6, /device:TPU:1, one launch (start us, length us, event | category | flops | bytes accessed | tf_op | source)
XLA Modules:
  0.0 128.6 jit_solution(3710143604003759320)
XLA Ops:
  0.0 1.1 stitch.6
  1.1 2.1 %collective-permute-start.2 = (bf16[192,1024]{1,0:T(8,128)(2,1)S(1)}, bf16[192,1024]{1,0:T(8,128)(2,1)S(1)}, u32[]{:S(2)}, u32[]{:S(2)}) collective-permute-start(bf16[192,1024]{1,0:T(8,128)(2,1)S(1)} %get-tuple-element.39.refs_0_), channel_id=1, source_target_pairs={{0,4},{1,5},{2,6},{3,7},{4,0},{5,1},{6,2},{7,3},{8,12},{9,13},{10,... | collective-permute-start | bytes 1179656 | tf_op jit(solution)/shard_map/ppermute | solution.py:46
  3.3 3.8 %collective-permute-start.1 = (bf16[192,1024]{1,0:T(8,128)(2,1)S(1)}, bf16[192,1024]{1,0:T(8,128)(2,1)S(1)}, u32[]{:S(2)}, u32[]{:S(2)}) collective-permute-start(bf16[192,1024]{1,0:T(8,128)(2,1)S(1)} %get-tuple-element.39.refs_0_), channel_id=1, source_target_pairs={{0,3},{1,0},{2,1},{3,2},{4,7},{5,4},{6,5},{7,6},{8,11},{9,8},{10,9... | collective-permute-start | bytes 1179656 | tf_op jit(solution)/shard_map/ppermute | solution.py:46
  7.0 5.4 %collective-permute-start.5 = (bf16[192,1024]{1,0:T(8,128)(2,1)S(1)}, bf16[192,1024]{1,0:T(8,128)(2,1)S(1)}, u32[]{:S(2)}, u32[]{:S(2)}) collective-permute-start(bf16[192,1024]{1,0:T(8,128)(2,1)S(1)} %get-tuple-element.36), channel_id=1, source_target_pairs={{0,124},{1,125},{2,126},{3,127},{4,120},{5,121},{6,122},{7,123},{8... | collective-permute-start | bytes 1179656 | tf_op jit(solution)/shard_map/ppermute | solution.py:46
  14.4 3.2 %collective-permute-done.refs_0_ = bf16[192,1024]{1,0:T(8,128)(2,1)S(1)} collective-permute-done((bf16[192,1024]{1,0:T(8,128)(2,1)S(1)}, bf16[192,1024]{1,0:T(8,128)(2,1)S(1)}, u32[]{:S(2)}, u32[]{:S(2)}) %collective-permute-start) | collective-permute-done | bytes 393248 | tf_op jit(solution)/shard_map/ppermute | solution.py:46
  17.6 1.1 stitch.7
  18.8 3.4 %collective-permute-done.5.refs_4_.refs_3_ = bf16[192,1024]{1,0:T(8,128)(2,1)S(1)} collective-permute-done((bf16[192,1024]{1,0:T(8,128)(2,1)S(1)}, bf16[192,1024]{1,0:T(8,128)(2,1)S(1)}, u32[]{:S(2)}, u32[]{:S(2)}) %collective-permute-start.5) | collective-permute-done | bytes 393248 | tf_op jit(solution)/shard_map/ppermute | solution.py:46
  22.2 3.0 %collective-permute-start.4 = (bf16[192,1024]{1,0:T(8,128)(2,1)S(1)}, bf16[192,1024]{1,0:T(8,128)(2,1)S(1)}, u32[]{:S(2)}, u32[]{:S(2)}) collective-permute-start(bf16[192,1024]{1,0:T(8,128)(2,1)S(1)} %get-tuple-element.35), channel_id=1, source_target_pairs={{0,3},{1,0},{2,1},{3,2},{4,7},{5,4},{6,5},{7,6},{8,11},{9,8},{10,9... | collective-permute-start | bytes 1179656 | tf_op jit(solution)/shard_map/ppermute | solution.py:46
  25.1 7.1 %collective-permute-done.6.refs_5_.refs_1_ = bf16[192,1024]{1,0:T(8,128)(2,1)S(1)} collective-permute-done((bf16[192,1024]{1,0:T(8,128)(2,1)S(1)}, bf16[192,1024]{1,0:T(8,128)(2,1)S(1)}, u32[]{:S(2)}, u32[]{:S(2)}) %collective-permute-start.6) | collective-permute-done | bytes 393248 | tf_op jit(solution)/shard_map/ppermute | solution.py:46
  33.8 1.5 %stitch.8 = (bf16[384,1024]{1,0:T(8,128)(2,1)S(1)}, bf16[384,1024]{1,0:T(8,128)(2,1)S(1)}) custom-call(bf16[192,1024]{1,0:T(8,128)(2,1)} %copy-done.1, bf16[192,1024]{1,0:T(8,128)(2,1)} %copy-done, bf16[192,1024]{1,0:T(8,128)(2,1)} %copy-done.8, bf16[192,1024]{1,0:T(8,128)(2,1)} %copy-done.9, bf16[192,1024]{1,0:T(8,128)(2,1)} %copy-done.13, ...), custom_call_target="tpu_custom_call" | custom-call | tf_op jit(solution)/shard_map/stitch/pallas_call | solution.py:336
  35.5 3.4 %collective-permute-start.9 = (bf16[384,1024]{1,0:T(8,128)(2,1)S(1)}, bf16[384,1024]{1,0:T(8,128)(2,1)}, u32[]{:S(2)}, u32[]{:S(2)}) collective-permute-start(bf16[384,1024]{1,0:T(8,128)(2,1)S(1)} %get-tuple-element.38), channel_id=1, source_target_pairs={{0,3},{1,0},{2,1},{3,2},{4,7},{5,4},{6,5},{7,6},{8,11},{9,8},{10,9... | collective-permute-start | bytes 2359304 | tf_op jit(solution)/shard_map/ppermute | solution.py:46
  38.8 1.1 collective-permute-start.7
  40.1 5.2 %project.2.refs_10_ = f32[384,1280]{1,0:T(8,128)S(1)} custom-call(s32[2]{0:T(128)S(1)} %pad_add_fusion.1.slices, bf16[192,1024]{1,0:T(8,128)(2,1)} %copy-done.3, bf16[192,1024]{1,0:T(8,128)(2,1)} %copy-done.14, bf16[192,1024]{1,0:T(8,128)(2,1)} %copy-done.2, bf16[192,1024]{1,0:T(8,128)(2,1)} %copy-done.13, bf16[8192,1024]{1,0:T(8,128)(2,1)} %refs_5_.5, ...), custom_call_target="tpu_custom_call" | custom-call | flops 2013265920 | bytes 5242880 | tf_op jit(solution)/shard_map/project/pallas_call | solution.py:184
  45.4 9.7 %collective-permute-done.8.refs_0_.refs_5_ = bf16[384,1024]{1,0:T(8,128)(2,1)S(1)} collective-permute-done((bf16[384,1024]{1,0:T(8,128)(2,1)S(1)}, bf16[384,1024]{1,0:T(8,128)(2,1)S(1)}, u32[]{:S(2)}, u32[]{:S(2)}) %collective-permute-start.8) | collective-permute-done | bytes 786464 | tf_op jit(solution)/shard_map/ppermute | solution.py:46
  56.0 1.3 stitch.9
  57.3 1.7 %collective-permute-start.11 = (bf16[192,1024]{1,0:T(8,128)(2,1)S(1)}, bf16[192,1024]{1,0:T(8,128)(2,1)S(1)}, u32[]{:S(2)}, u32[]{:S(2)}) collective-permute-start(bf16[192,1024]{1,0:T(8,128)(2,1)S(1)} %get-tuple-element.42), channel_id=1, source_target_pairs={{0,3},{1,0},{2,1},{3,2},{4,7},{5,4},{6,5},{7,6},{8,11},{9,8},{10,9... | collective-permute-start | bytes 1179656 | tf_op jit(solution)/shard_map/ppermute | solution.py:46
  60.0 8.3 %project.3.refs_7_.refs_6_ = f32[384,1280]{1,0:T(8,128)S(1)} custom-call(s32[4]{0:T(128)S(1)} %pad_add_fusion.2.slices, bf16[192,1024]{1,0:T(8,128)(2,1)} %copy-done.1, bf16[192,1024]{1,0:T(8,128)(2,1)} %copy-done, bf16[192,1024]{1,0:T(8,128)(2,1)} %copy-done.8, bf16[192,1024]{1,0:T(8,128)(2,1)} %copy-done.9, bf16[384,1024]{1,0:T(8,128)(2,1)} %copy-done.7, ...), custom_call_target="tpu_custom_call" | custom-call | flops 4026531840 | bytes 10485760 | tf_op jit(solution)/shard_map/project/pallas_call | solution.py:184
  69.2 3.1 %last_kv.1.refs_0_ = bf16[2,192,256]{2,1,0:T(8,128)(2,1)S(1)} custom-call(s32[2]{0:T(128)S(1)} %pad_add_fusion.slices, bf16[384,1024]{1,0:T(8,128)(2,1)} %copy-done.7, bf16[192,1024]{1,0:T(8,128)(2,1)} %copy-done.8, bf16[192,1024]{1,0:T(8,128)(2,1)} %copy-done.9, bf16[192,1024]{1,0:T(8,128)(2,1)} %copy-done.12, bf16[192,1024]{1,0:T(8,128)(2,1)} %copy-done.11, ...), custom_call_target="tpu_custom_call" | custom-call | flops 402653184 | bytes 1048576 | tf_op jit(solution)/shard_map/last_kv/pallas_call | solution.py:240
  72.4 1.7 %collective-permute-start.14 = (bf16[2,192,256]{2,1,0:T(8,128)(2,1)S(1)}, bf16[2,192,256]{2,1,0:T(8,128)(2,1)S(1)}, u32[]{:S(2)}, u32[]{:S(2)}) collective-permute-start(bf16[2,192,256]{2,1,0:T(8,128)(2,1)S(1)} %last_kv.1.refs_0_), channel_id=1, source_target_pairs={{0,64},{1,65},{2,66},{3,67},{4,68},{5,69},{6,70},{7,71},{8,72},{9,... | collective-permute-start | bytes 589832 | tf_op jit(solution)/shard_map/ppermute | solution.py:46
  75.7 4.7 %last_q.1.queries = bf16[384,1024]{1,0:T(8,128)(2,1)S(1)} custom-call(s32[2]{0:T(128)S(1)} %pad_add_fusion.slices, bf16[384,1024]{1,0:T(8,128)(2,1)} %copy-done.7, bf16[192,1024]{1,0:T(8,128)(2,1)} %copy-done.8, bf16[192,1024]{1,0:T(8,128)(2,1)} %copy-done.9, bf16[192,1024]{1,0:T(8,128)(2,1)} %copy-done.12, bf16[192,1024]{1,0:T(8,128)(2,1)} %copy-done.11, ...), custom_call_target="tpu_custom_call" | custom-call | flops 1610612736 | bytes 4194304 | tf_op jit(solution)/shard_map/last_q/pallas_call | solution.py:296
  80.4 1.9 %collective-permute-start.19 = (bf16[2,192,256]{2,1,0:T(8,128)(2,1)S(1)}, bf16[2,192,256]{2,1,0:T(8,128)(2,1)S(1)}, u32[]{:S(2)}, u32[]{:S(2)}) collective-permute-start(bf16[2,192,256]{2,1,0:T(8,128)(2,1)S(1)} %collective-permute-done.16.refs_0_), channel_id=1, source_target_pairs={{0,64},{1,65},{2,66},{3,67},{4,68},{5,69},{6,70},{7,71},{8,72},{9,... | collective-permute-start | bytes 589832 | tf_op jit(solution)/shard_map/ppermute | solution.py:46
  82.3 2.1 %collective-permute-start.18 = (bf16[2,192,256]{2,1,0:T(8,128)(2,1)S(1)}, bf16[2,192,256]{2,1,0:T(8,128)(2,1)S(1)}, u32[]{:S(2)}, u32[]{:S(2)}) collective-permute-start(bf16[2,192,256]{2,1,0:T(8,128)(2,1)S(1)} %collective-permute-done.16.refs_0_), channel_id=1, source_target_pairs={{0,96},{1,97},{2,98},{3,99},{4,100},{5,101},{6,102},{7,103},{8,104... | collective-permute-start | bytes 589832 | tf_op jit(solution)/shard_map/ppermute | solution.py:46
  84.4 1.1 stitch.10.near
  85.5 5.4 %collective-permute-start.15 = (bf16[8,192,256]{2,1,0:T(8,128)(2,1)S(1)}, bf16[8,192,256]{2,1,0:T(8,128)(2,1)S(1)}, u32[]{:S(2)}, u32[]{:S(2)}) collective-permute-start(bf16[8,192,256]{2,1,0:T(8,128)(2,1)S(1)} %stitch.10.near), channel_id=1, source_target_pairs={{0,8},{1,9},{2,10},{3,11},{4,12},{5,13},{6,14},{7,15},{8,0},{9,1},... | collective-permute-start | bytes 2359304 | tf_op jit(solution)/shard_map/ppermute | solution.py:46
  90.8 1.4 %collective-permute-done.17.refs_1_ = bf16[2,192,256]{2,1,0:T(8,128)(2,1)S(1)} collective-permute-done((bf16[2,192,256]{2,1,0:T(8,128)(2,1)S(1)}, bf16[2,192,256]{2,1,0:T(8,128)(2,1)S(1)}, u32[]{:S(2)}, u32[]{:S(2)}) %collective-permute-start.17) | collective-permute-done | bytes 196640 | tf_op jit(solution)/shard_map/ppermute | solution.py:46
  93.3 4.6 %collective-permute-start.20 = (bf16[8,192,256]{2,1,0:T(8,128)(2,1)S(1)}, bf16[8,192,256]{2,1,0:T(8,128)(2,1)S(1)}, u32[]{:S(2)}, u32[]{:S(2)}) collective-permute-start(bf16[8,192,256]{2,1,0:T(8,128)(2,1)S(1)} %stitch.11.far), channel_id=1, source_target_pairs={{0,8},{1,9},{2,10},{3,11},{4,12},{5,13},{6,14},{7,15},{8,0},{9,1},... | collective-permute-start | bytes 2359304 | tf_op jit(solution)/shard_map/ppermute | solution.py:46
  97.9 8.1 %attend.3 = (f32[4,8,768]{2,1,0:T(8,128)S(1)}, f32[4,128,768]{2,1,0:T(8,128)S(1)}) custom-call(s32[32]{0:T(128)S(1)} %concatenate.28.meta, bf16[8,192,256]{2,1,0:T(8,128)(2,1)S(1)} %stitch.10.near, bf16[8,192,256]{2,1,0:T(8,128)(2,1)S(1)} %stitch.11.far, bf16[384,1024]{1,0:T(8,128)(2,1)S(1)} %last_q.1.queries), custom_call_target="tpu_custom_call" | custom-call | flops 3019898880 | bytes 4194304 | tf_op jit(solution)/shard_map/attend/pallas_call | solution.py:462
  106.0 4.7 %attend.4 = (bf16[192,512]{1,0:T(8,128)(2,1)S(1)}, bf16[208,512]{1,0:T(8,128)(2,1)S(1)}) custom-call(s32[32]{0:T(128)S(1)} %concatenate.29.meta, bf16[8,192,256]{2,1,0:T(8,128)(2,1)S(1)} %collective-permute-done.15.near, bf16[8,192,256]{2,1,0:T(8,128)(2,1)S(1)} %collective-permute-done.20.far, bf16[384,1024]{1,0:T(8,128)(2,1)S(1)} %last_q.1.queries, ...), custom_call_target="tpu_custom_call" | custom-call | flops 1509949440 | bytes 4194304 | tf_op jit(solution)/shard_map/attend/pallas_call | solution.py:462
  110.7 1.4 %collective-permute-start.21 = (bf16[208,512]{1,0:T(8,128)(2,1)S(1)}, bf16[208,512]{1,0:T(8,128)(2,1)S(1)}, u32[]{:S(2)}, u32[]{:S(2)}) collective-permute-start(bf16[208,512]{1,0:T(8,128)(2,1)S(1)} %get-tuple-element.53), channel_id=1, source_target_pairs={{0,120},{1,121},{2,122},{3,123},{4,124},{5,125},{6,126},{7,127},{8... | collective-permute-start | bytes 638984 | tf_op jit(solution)/shard_map/ppermute | solution.py:46
  112.2 4.7 %attend.5 = (bf16[192,512]{1,0:T(8,128)(2,1)S(1)}, bf16[192,512]{1,0:T(8,128)(2,1)S(1)}) custom-call(s32[32]{0:T(128)S(1)} %concatenate.29.meta, bf16[8,192,256]{2,1,0:T(8,128)(2,1)S(1)} %collective-permute-done.15.near, bf16[8,192,256]{2,1,0:T(8,128)(2,1)S(1)} %collective-permute-done.20.far, bf16[384,1024]{1,0:T(8,128)(2,1)S(1)} %last_q.1.queries, ...), custom_call_target="tpu_custom_call" | custom-call | flops 1509949440 | bytes 4194304 | tf_op jit(solution)/shard_map/attend/pallas_call | solution.py:462
  116.8 4.3 %collective-permute-start.22 = (bf16[192,512]{1,0:T(8,128)(2,1)S(1)}, bf16[192,512]{1,0:T(8,128)(2,1)S(1)}, u32[]{:S(2)}, u32[]{:S(2)}) collective-permute-start(bf16[192,512]{1,0:T(8,128)(2,1)S(1)} %get-tuple-element.56), channel_id=1, source_target_pairs={{0,120},{1,121},{2,122},{3,123},{4,124},{5,125},{6,126},{7,127},{8... | collective-permute-start | bytes 589832 | tf_op jit(solution)/shard_map/ppermute | solution.py:46
  121.6 6.1 %collective-permute-done.22 = bf16[192,512]{1,0:T(8,128)(2,1)S(1)} collective-permute-done((bf16[192,512]{1,0:T(8,128)(2,1)S(1)}, bf16[192,512]{1,0:T(8,128)(2,1)S(1)}, u32[]{:S(2)}, u32[]{:S(2)}) %collective-permute-start.22) | collective-permute-done | bytes 196640 | tf_op jit(solution)/shard_map/ppermute | solution.py:46
  (76 shorter events, 10.7 us)
Async XLA Ops:
  1.1 13.3 %copy-start.3 = (bf16[192,1024]{1,0:T(8,128)(2,1)}, bf16[192,1024]{1,0:T(8,128)(2,1)S(1)}, u32[]{:S(2)}) copy-start(bf16[192,1024]{1,0:T(8,128)(2,1)S(1)} %get-tuple-element.39.refs_0_) | copy-start | bytes 1179652
  1.1 16.5 %collective-permute-start.2 = (bf16[192,1024]{1,0:T(8,128)(2,1)S(1)}, bf16[192,1024]{1,0:T(8,128)(2,1)S(1)}, u32[]{:S(2)}, u32[]{:S(2)}) collective-permute-start(bf16[192,1024]{1,0:T(8,128)(2,1)S(1)} %get-tuple-element.39.refs_0_), channel_id=1, source_target_pairs={{0,4},{1,5},{2,6},{3,7},{4,0},{5,1},{6,2},{7,3},{8,12},{9,13},{10,... | collective-permute-start | bytes 1179656 | tf_op jit(solution)/shard_map/ppermute | solution.py:46
  3.3 14.3 %collective-permute-start.1 = (bf16[192,1024]{1,0:T(8,128)(2,1)S(1)}, bf16[192,1024]{1,0:T(8,128)(2,1)S(1)}, u32[]{:S(2)}, u32[]{:S(2)}) collective-permute-start(bf16[192,1024]{1,0:T(8,128)(2,1)S(1)} %get-tuple-element.39.refs_0_), channel_id=1, source_target_pairs={{0,3},{1,0},{2,1},{3,2},{4,7},{5,4},{6,5},{7,6},{8,11},{9,8},{10,9... | collective-permute-start | bytes 1179656 | tf_op jit(solution)/shard_map/ppermute | solution.py:46
  7.0 10.6 %collective-permute-start = (bf16[192,1024]{1,0:T(8,128)(2,1)S(1)}, bf16[192,1024]{1,0:T(8,128)(2,1)S(1)}, u32[]{:S(2)}, u32[]{:S(2)}) collective-permute-start(bf16[192,1024]{1,0:T(8,128)(2,1)S(1)} %get-tuple-element.39.refs_0_), channel_id=1, source_target_pairs={{0,1},{1,2},{2,3},{3,0},{4,5},{5,6},{6,7},{7,4},{8,9},{9,10},{10,1... | collective-permute-start | bytes 1179656 | tf_op jit(solution)/shard_map/ppermute | solution.py:46
  7.0 15.1 %collective-permute-start.5 = (bf16[192,1024]{1,0:T(8,128)(2,1)S(1)}, bf16[192,1024]{1,0:T(8,128)(2,1)S(1)}, u32[]{:S(2)}, u32[]{:S(2)}) collective-permute-start(bf16[192,1024]{1,0:T(8,128)(2,1)S(1)} %get-tuple-element.36), channel_id=1, source_target_pairs={{0,124},{1,125},{2,126},{3,127},{4,120},{5,121},{6,122},{7,123},{8... | collective-permute-start | bytes 1179656 | tf_op jit(solution)/shard_map/ppermute | solution.py:46
  17.6 15.4 %copy-start.1 = (bf16[192,1024]{1,0:T(8,128)(2,1)}, bf16[192,1024]{1,0:T(8,128)(2,1)S(1)}, u32[]{:S(2)}) copy-start(bf16[192,1024]{1,0:T(8,128)(2,1)S(1)} %collective-permute-done.refs_0_) | copy-start | bytes 1179652
  17.6 17.8 %copy-start.2 = (bf16[192,1024]{1,0:T(8,128)(2,1)}, bf16[192,1024]{1,0:T(8,128)(2,1)S(1)}, u32[]{:S(2)}) copy-start(bf16[192,1024]{1,0:T(8,128)(2,1)S(1)} %collective-permute-done.2.refs_2_) | copy-start | bytes 1179652
  17.6 15.3 %copy-start = (bf16[192,1024]{1,0:T(8,128)(2,1)}, bf16[192,1024]{1,0:T(8,128)(2,1)S(1)}, u32[]{:S(2)}) copy-start(bf16[192,1024]{1,0:T(8,128)(2,1)S(1)} %collective-permute-done.1.refs_1_) | copy-start | bytes 1179652
  18.7 13.5 %collective-permute-start.3 = (bf16[192,1024]{1,0:T(8,128)(2,1)S(1)}, bf16[192,1024]{1,0:T(8,128)(2,1)S(1)}, u32[]{:S(2)}, u32[]{:S(2)}) collective-permute-start(bf16[192,1024]{1,0:T(8,128)(2,1)S(1)} %get-tuple-element.34), channel_id=1, source_target_pairs={{0,1},{1,2},{2,3},{3,0},{4,5},{5,6},{6,7},{7,4},{8,9},{9,10},{10,1... | collective-permute-start | bytes 1179656 | tf_op jit(solution)/shard_map/ppermute | solution.py:46
  22.2 10.1 %copy-start.13 = (bf16[192,1024]{1,0:T(8,128)(2,1)}, bf16[192,1024]{1,0:T(8,128)(2,1)S(1)}, u32[]{:S(2)}) copy-start(bf16[192,1024]{1,0:T(8,128)(2,1)S(1)} %collective-permute-done.5.refs_4_.refs_3_) | copy-start | bytes 1179652
  22.2 10.0 %collective-permute-start.6 = (bf16[192,1024]{1,0:T(8,128)(2,1)S(1)}, bf16[192,1024]{1,0:T(8,128)(2,1)S(1)}, u32[]{:S(2)}, u32[]{:S(2)}) collective-permute-start(bf16[192,1024]{1,0:T(8,128)(2,1)S(1)} %collective-permute-done.5.refs_4_.refs_3_), channel_id=1, source_target_pairs={{0,4},{1,5},{2,6},{3,7},{4,0},{5,1},{6,2},{7,3},{8,12},{9,13},{10,... | collective-permute-start | bytes 1179656 | tf_op jit(solution)/shard_map/ppermute | solution.py:46
  22.2 10.8 %collective-permute-start.4 = (bf16[192,1024]{1,0:T(8,128)(2,1)S(1)}, bf16[192,1024]{1,0:T(8,128)(2,1)S(1)}, u32[]{:S(2)}, u32[]{:S(2)}) collective-permute-start(bf16[192,1024]{1,0:T(8,128)(2,1)S(1)} %get-tuple-element.35), channel_id=1, source_target_pairs={{0,3},{1,0},{2,1},{3,2},{4,7},{5,4},{6,5},{7,6},{8,11},{9,8},{10,9... | collective-permute-start | bytes 1179656 | tf_op jit(solution)/shard_map/ppermute | solution.py:46
  35.4 19.7 %collective-permute-start.8 = (bf16[384,1024]{1,0:T(8,128)(2,1)S(1)}, bf16[384,1024]{1,0:T(8,128)(2,1)S(1)}, u32[]{:S(2)}, u32[]{:S(2)}) collective-permute-start(bf16[384,1024]{1,0:T(8,128)(2,1)S(1)} %get-tuple-element.38), channel_id=1, source_target_pairs={{0,1},{1,2},{2,3},{3,0},{4,5},{5,6},{6,7},{7,4},{8,9},{9,10},{10,1... | collective-permute-start | bytes 2359304 | tf_op jit(solution)/shard_map/ppermute | solution.py:46
  35.5 20.6 %collective-permute-start.9 = (bf16[384,1024]{1,0:T(8,128)(2,1)S(1)}, bf16[384,1024]{1,0:T(8,128)(2,1)}, u32[]{:S(2)}, u32[]{:S(2)}) collective-permute-start(bf16[384,1024]{1,0:T(8,128)(2,1)S(1)} %get-tuple-element.38), channel_id=1, source_target_pairs={{0,3},{1,0},{2,1},{3,2},{4,7},{5,4},{6,5},{7,6},{8,11},{9,8},{10,9... | collective-permute-start | bytes 2359304 | tf_op jit(solution)/shard_map/ppermute | solution.py:46
  38.8 20.3 %collective-permute-start.7 = (bf16[384,1024]{1,0:T(8,128)(2,1)S(1)}, bf16[384,1024]{1,0:T(8,128)(2,1)S(1)}, u32[]{:S(2)}, u32[]{:S(2)}) collective-permute-start(bf16[384,1024]{1,0:T(8,128)(2,1)S(1)} %get-tuple-element.37), channel_id=1, source_target_pairs={{0,4},{1,5},{2,6},{3,7},{4,0},{5,1},{6,2},{7,3},{8,12},{9,13},{10,... | collective-permute-start | bytes 2359304 | tf_op jit(solution)/shard_map/ppermute | solution.py:46
  55.1 0.9 copy-start.10
  57.3 11.1 %collective-permute-start.11 = (bf16[192,1024]{1,0:T(8,128)(2,1)S(1)}, bf16[192,1024]{1,0:T(8,128)(2,1)S(1)}, u32[]{:S(2)}, u32[]{:S(2)}) collective-permute-start(bf16[192,1024]{1,0:T(8,128)(2,1)S(1)} %get-tuple-element.42), channel_id=1, source_target_pairs={{0,3},{1,0},{2,1},{3,2},{4,7},{5,4},{6,5},{7,6},{8,11},{9,8},{10,9... | collective-permute-start | bytes 1179656 | tf_op jit(solution)/shard_map/ppermute | solution.py:46
  59.0 9.3 %collective-permute-start.10 = (bf16[192,1024]{1,0:T(8,128)(2,1)S(1)}, bf16[192,1024]{1,0:T(8,128)(2,1)S(1)}, u32[]{:S(2)}, u32[]{:S(2)}) collective-permute-start(bf16[192,1024]{1,0:T(8,128)(2,1)S(1)} %get-tuple-element.41), channel_id=1, source_target_pairs={{0,1},{1,2},{2,3},{3,0},{4,5},{5,6},{6,7},{7,4},{8,9},{9,10},{10,1... | collective-permute-start | bytes 1179656 | tf_op jit(solution)/shard_map/ppermute | solution.py:46
  59.1 10.1 %copy-start.5 = (f32[128]{0:T(128)S(1)}, f32[128]{0:T(128)}, u32[]{:S(2)}) copy-start(f32[128]{0:T(128)} %param.12) | copy-start | bytes 1540
  59.1 10.1 %copy-start.6 = (f32[128]{0:T(128)S(1)}, f32[128]{0:T(128)}, u32[]{:S(2)}) copy-start(f32[128]{0:T(128)} %param.13) | copy-start | bytes 1540
  69.2 6.5 %copy-start.4 = (f32[1024]{0:T(1024)S(1)}, f32[1024]{0:T(1024)}, u32[]{:S(2)}) copy-start(f32[1024]{0:T(1024)} %param.11) | copy-start | bytes 12292
  72.3 8.1 %collective-permute-start.16 = (bf16[2,192,256]{2,1,0:T(8,128)(2,1)S(1)}, bf16[2,192,256]{2,1,0:T(8,128)(2,1)S(1)}, u32[]{:S(2)}, u32[]{:S(2)}) collective-permute-start(bf16[2,192,256]{2,1,0:T(8,128)(2,1)S(1)} %last_kv.1.refs_0_), channel_id=1, source_target_pairs={{0,16},{1,17},{2,18},{3,19},{4,20},{5,21},{6,22},{7,23},{8,24},{9,... | collective-permute-start | bytes 589832 | tf_op jit(solution)/shard_map/ppermute | solution.py:46
  72.4 12.0 %collective-permute-start.14 = (bf16[2,192,256]{2,1,0:T(8,128)(2,1)S(1)}, bf16[2,192,256]{2,1,0:T(8,128)(2,1)S(1)}, u32[]{:S(2)}, u32[]{:S(2)}) collective-permute-start(bf16[2,192,256]{2,1,0:T(8,128)(2,1)S(1)} %last_kv.1.refs_0_), channel_id=1, source_target_pairs={{0,64},{1,65},{2,66},{3,67},{4,68},{5,69},{6,70},{7,71},{8,72},{9,... | collective-permute-start | bytes 589832 | tf_op jit(solution)/shard_map/ppermute | solution.py:46
  74.1 10.3 %collective-permute-start.13 = (bf16[2,192,256]{2,1,0:T(8,128)(2,1)S(1)}, bf16[2,192,256]{2,1,0:T(8,128)(2,1)S(1)}, u32[]{:S(2)}, u32[]{:S(2)}) collective-permute-start(bf16[2,192,256]{2,1,0:T(8,128)(2,1)S(1)} %last_kv.1.refs_0_), channel_id=1, source_target_pairs={{0,96},{1,97},{2,98},{3,99},{4,100},{5,101},{6,102},{7,103},{8,104... | collective-permute-start | bytes 589832 | tf_op jit(solution)/shard_map/ppermute | solution.py:46
  75.1 9.3 %collective-permute-start.12 = (bf16[2,192,256]{2,1,0:T(8,128)(2,1)S(1)}, bf16[2,192,256]{2,1,0:T(8,128)(2,1)S(1)}, u32[]{:S(2)}, u32[]{:S(2)}) collective-permute-start(bf16[2,192,256]{2,1,0:T(8,128)(2,1)S(1)} %last_kv.1.refs_0_), channel_id=1, source_target_pairs={{0,32},{1,33},{2,34},{3,35},{4,36},{5,37},{6,38},{7,39},{8,40},{9,... | collective-permute-start | bytes 589832 | tf_op jit(solution)/shard_map/ppermute | solution.py:46
  80.4 10.4 %collective-permute-start.19 = (bf16[2,192,256]{2,1,0:T(8,128)(2,1)S(1)}, bf16[2,192,256]{2,1,0:T(8,128)(2,1)S(1)}, u32[]{:S(2)}, u32[]{:S(2)}) collective-permute-start(bf16[2,192,256]{2,1,0:T(8,128)(2,1)S(1)} %collective-permute-done.16.refs_0_), channel_id=1, source_target_pairs={{0,64},{1,65},{2,66},{3,67},{4,68},{5,69},{6,70},{7,71},{8,72},{9,... | collective-permute-start | bytes 589832 | tf_op jit(solution)/shard_map/ppermute | solution.py:46
  82.3 8.5 %collective-permute-start.18 = (bf16[2,192,256]{2,1,0:T(8,128)(2,1)S(1)}, bf16[2,192,256]{2,1,0:T(8,128)(2,1)S(1)}, u32[]{:S(2)}, u32[]{:S(2)}) collective-permute-start(bf16[2,192,256]{2,1,0:T(8,128)(2,1)S(1)} %collective-permute-done.16.refs_0_), channel_id=1, source_target_pairs={{0,96},{1,97},{2,98},{3,99},{4,100},{5,101},{6,102},{7,103},{8,104... | collective-permute-start | bytes 589832 | tf_op jit(solution)/shard_map/ppermute | solution.py:46
  84.4 7.8 %collective-permute-start.17 = (bf16[2,192,256]{2,1,0:T(8,128)(2,1)S(1)}, bf16[2,192,256]{2,1,0:T(8,128)(2,1)S(1)}, u32[]{:S(2)}, u32[]{:S(2)}) collective-permute-start(bf16[2,192,256]{2,1,0:T(8,128)(2,1)S(1)} %collective-permute-done.16.refs_0_), channel_id=1, source_target_pairs={{0,32},{1,33},{2,34},{3,35},{4,36},{5,37},{6,38},{7,39},{8,40},{9,... | collective-permute-start | bytes 589832 | tf_op jit(solution)/shard_map/ppermute | solution.py:46
  85.5 20.5 %collective-permute-start.15 = (bf16[8,192,256]{2,1,0:T(8,128)(2,1)S(1)}, bf16[8,192,256]{2,1,0:T(8,128)(2,1)S(1)}, u32[]{:S(2)}, u32[]{:S(2)}) collective-permute-start(bf16[8,192,256]{2,1,0:T(8,128)(2,1)S(1)} %stitch.10.near), channel_id=1, source_target_pairs={{0,8},{1,9},{2,10},{3,11},{4,12},{5,13},{6,14},{7,15},{8,0},{9,1},... | collective-permute-start | bytes 2359304 | tf_op jit(solution)/shard_map/ppermute | solution.py:46
  93.3 12.8 %collective-permute-start.20 = (bf16[8,192,256]{2,1,0:T(8,128)(2,1)S(1)}, bf16[8,192,256]{2,1,0:T(8,128)(2,1)S(1)}, u32[]{:S(2)}, u32[]{:S(2)}) collective-permute-start(bf16[8,192,256]{2,1,0:T(8,128)(2,1)S(1)} %stitch.11.far), channel_id=1, source_target_pairs={{0,8},{1,9},{2,10},{3,11},{4,12},{5,13},{6,14},{7,15},{8,0},{9,1},... | collective-permute-start | bytes 2359304 | tf_op jit(solution)/shard_map/ppermute | solution.py:46
  110.7 10.8 %collective-permute-start.21 = (bf16[208,512]{1,0:T(8,128)(2,1)S(1)}, bf16[208,512]{1,0:T(8,128)(2,1)S(1)}, u32[]{:S(2)}, u32[]{:S(2)}) collective-permute-start(bf16[208,512]{1,0:T(8,128)(2,1)S(1)} %get-tuple-element.53), channel_id=1, source_target_pairs={{0,120},{1,121},{2,122},{3,123},{4,124},{5,125},{6,126},{7,127},{8... | collective-permute-start | bytes 638984 | tf_op jit(solution)/shard_map/ppermute | solution.py:46
  116.8 10.8 %collective-permute-start.22 = (bf16[192,512]{1,0:T(8,128)(2,1)S(1)}, bf16[192,512]{1,0:T(8,128)(2,1)S(1)}, u32[]{:S(2)}, u32[]{:S(2)}) collective-permute-start(bf16[192,512]{1,0:T(8,128)(2,1)S(1)} %get-tuple-element.56), channel_id=1, source_target_pairs={{0,120},{1,121},{2,122},{3,123},{4,124},{5,125},{6,126},{7,127},{8... | collective-permute-start | bytes 589832 | tf_op jit(solution)/shard_map/ppermute | solution.py:46
  (6 other events, 4.9 us)
